TPU v7x, 32 devices: a whole 2x2x4 slice. The times are simulated.
32 devices in a mesh: space: 16 (over z, y, x), load: 2 (over core).
Axes of the slice: x: 2, y: 2, z: 4, core: 2. Of those that a mesh axis runs over, the one named last changes fastest.
Arguments:
- forward_disp: float32 [2, 3, 32, 128, 128], P('load', None, 'space'), may hold values from -6 to 6
- adjoint_rhs: float32 [2, 3, 32, 128, 128], P('load', None, 'space'), may hold values from -72 to 72
- modulus_factor: float32 [32, 128, 128], P('space'), may hold values from 0.5 to 2
- zone_base: float32 [8], replicated, may hold values from 0.3 to 3
- zone_ids: int32 [32, 128, 128], P('space'), may hold values from 0 to 7
- fixed_mask: int32 [32, 128, 128], P('space'), may hold values 0 or 1
Outputs:
- adjoint_disp: float32 [2, 3, 32, 128, 128], P('load', None, 'space')
- modulus_grad: float32 [32, 128, 128], P('space', 'load')
All inputs are finite; a program needn't handle non-finite values. No bound on the sum of `fixed_mask` on one device may be relied on, other than what follows from the above.
Results may differ from a plain program's by a relative error of at most 0.00016.
Values sent between devices are 32-bit elements; how exact they have to be, the bound alone decides.
No kernel may reach another device: no remote copies, remote signals or barrier semaphores. Data moves between devices by JAX's collectives and lax.ppermute only.
A program may use at most 64 MiB of HBM per device.

v0:
```python
import jax
import jax.numpy as jnp
import numpy as np
from jax import lax
from jax.sharding import PartitionSpec as P

ITERS = 2


def from_behind(shard, axis, by):
    devices = lax.axis_size(axis)
    pairs = [(i, i + by) for i in range(devices) if 0 <= i + by < devices]
    return lax.ppermute(shard, axis, pairs)


def unit_stiffness():
    poisson = 0.3
    lame_first = poisson / ((1.0 + poisson) * (1.0 - 2.0 * poisson))
    shear_mod = 0.5 / (1.0 + poisson)
    elastic = np.zeros((6, 6))
    elastic[:3, :3] = lame_first
    for index in range(3):
        elastic[index, index] += 2.0 * shear_mod
        elastic[index + 3, index + 3] = shear_mod
    points = [0.5 - 0.5 / np.sqrt(3.0), 0.5 + 0.5 / np.sqrt(3.0)]
    stiffness = np.zeros((24, 24))
    for point_z in points:
        for point_y in points:
            for point_x in points:
                gradient = np.zeros((3, 8))
                for corner in range(8):
                    off_z, off_y, off_x = (corner // 4, corner // 2 % 2, corner % 2)
                    shape_x = point_x if off_x else 1.0 - point_x
                    shape_y = point_y if off_y else 1.0 - point_y
                    shape_z = point_z if off_z else 1.0 - point_z
                    sign_x = 1.0 if off_x else -1.0
                    sign_y = 1.0 if off_y else -1.0
                    sign_z = 1.0 if off_z else -1.0
                    gradient[0, corner] = sign_x * shape_y * shape_z
                    gradient[1, corner] = shape_x * sign_y * shape_z
                    gradient[2, corner] = shape_x * shape_y * sign_z
                strain_map = np.zeros((6, 24))
                for corner in range(8):
                    strain_map[0, corner] = gradient[0, corner]
                    strain_map[1, 8 + corner] = gradient[1, corner]
                    strain_map[2, 16 + corner] = gradient[2, corner]
                    strain_map[3, corner] = gradient[1, corner]
                    strain_map[3, 8 + corner] = gradient[0, corner]
                    strain_map[4, 8 + corner] = gradient[2, corner]
                    strain_map[4, 16 + corner] = gradient[1, corner]
                    strain_map[5, 16 + corner] = gradient[0, corner]
                    strain_map[5, corner] = gradient[2, corner]
                stiffness += strain_map.T @ elastic @ strain_map / 8.0
    return stiffness


def corner_offsets(corner):
    return (corner // 4, corner // 2 % 2, corner % 2)


def element_vectors(extended):
    lead = extended.ndim - 4
    padded = jnp.pad(extended, [(0, 0)] * (lead + 2) + [(0, 1), (0, 1)])
    layers = extended.shape[-3] - 1
    height = extended.shape[-2]
    width = extended.shape[-1]
    pieces = []
    for corner in range(8):
        off_z, off_y, off_x = corner_offsets(corner)
        pieces.append(
            padded[..., off_z : off_z + layers, off_y : off_y + height, off_x : off_x + width]
        )
    stacked = jnp.stack(pieces, axis=-4)
    return stacked.reshape(stacked.shape[:lead] + (24, layers, height, width))


def stiff_product(vectors, stiffness):
    return jnp.einsum("ab,...bzyx->...azyx", stiffness, vectors, precision=lax.Precision.HIGHEST)


def assemble(forces):
    lead = forces.ndim - 4
    layers, height, width = forces.shape[-3:]
    split = forces.reshape(forces.shape[:lead] + (3, 8, layers, height, width))
    total = None
    for corner in range(8):
        off_z, off_y, off_x = corner_offsets(corner)
        placed = jnp.pad(
            split[..., corner, :, :, :],
            [(0, 0)] * (lead + 1) + [(off_z, 1 - off_z), (off_y, 1 - off_y), (off_x, 1 - off_x)],
        )
        total = placed if total is None else total + placed
    return total[..., :height, :width]


def node_diagonal(padded, layers, height, width):
    total = None
    for corner in range(8):
        off_z, off_y, off_x = corner_offsets(corner)
        piece = padded[
            1 - off_z : 1 - off_z + layers,
            1 - off_y : 1 - off_y + height,
            1 - off_x : 1 - off_x + width,
        ]
        total = piece if total is None else total + piece
    return total


def inner(left, right):
    return jnp.sum(left * right, axis=(1, 2, 3, 4))


def expand(scalar):
    return scalar[:, None, None, None, None]


def shards(forward_disp, adjoint_rhs, modulus_factor, zone_base, zone_ids, fixed_mask):
    stiffness = jnp.asarray(unit_stiffness(), jnp.float32)
    labels = jnp.arange(zone_base.shape[0], dtype=jnp.int32)
    zone_scale = jnp.sum(
        jnp.where(
            zone_ids[None] == labels[:, None, None, None], zone_base[:, None, None, None], 0.0
        ),
        axis=0,
    )
    modulus = modulus_factor * zone_scale
    free = (1 - fixed_mask).astype(jnp.float32)
    layers, height, width = modulus.shape
    lower = from_behind(modulus[-1:], "space", 1)
    below_mod = jnp.concatenate([lower, modulus], axis=0)
    padded = jnp.pad(below_mod, ((0, 0), (1, 0), (1, 0)))
    diagonal = node_diagonal(padded, layers, height, width) * stiffness[0, 0]
    inverse = free / diagonal
    residual = free * adjoint_rhs
    solution = jnp.zeros_like(residual)
    precond = inverse * residual
    direction = precond
    along = precond
    step_size = None
    norm_prev = None
    for iteration in range(ITERS):
        upper = from_behind(precond[:, :, :1], "space", -1)
        extended = jnp.concatenate([precond, upper], axis=2)
        nodal = assemble(stiff_product(element_vectors(extended), stiffness) * modulus)
        spill = from_behind(nodal[:, :, layers:], "space", 1)
        own = jnp.concatenate([nodal[:, :, :1] + spill, nodal[:, :, 1:layers]], axis=2)
        image = free * own
        norm_now, curvature = lax.psum((inner(residual, precond), inner(image, precond)), "space")
        if iteration == 0:
            step_size = norm_now / curvature
            direction = precond
            along = image
        else:
            ratio = norm_now / norm_prev
            step_size = norm_now / (curvature - ratio * norm_now / step_size)
            direction = precond + expand(ratio) * direction
            along = image + expand(ratio) * along
        solution = solution + expand(step_size) * direction
        if iteration + 1 < ITERS:
            residual = residual - expand(step_size) * along
            precond = inverse * residual
        norm_prev = norm_now
    lowest = jnp.concatenate([forward_disp[:, :, :1], solution[:, :, :1]], axis=2)
    arrived = from_behind(lowest, "space", -1)
    forward_vec = element_vectors(jnp.concatenate([forward_disp, arrived[:, :, :1]], axis=2))
    solution_vec = element_vectors(jnp.concatenate([solution, arrived[:, :, 1:2]], axis=2))
    term = jnp.sum(solution_vec * stiff_product(forward_vec, stiffness), axis=(0, 1)) * zone_scale
    gradient_share = lax.psum_scatter(term, "load", scatter_dimension=1, tiled=True)
    return (solution, gradient_share)


def solution(mesh):
    placed = (
        P("load", None, "space", None, None),
        P("load", None, "space", None, None),
        P("space", None, None),
        P(),
        P("space", None, None),
        P("space", None, None),
    )
    return jax.shard_map(
        shards,
        mesh=mesh,
        in_specs=placed,
        out_specs=(P("load", None, "space", None, None), P("space", "load", None)),
        check_vma=False,
    )
```

profile of v0, /device:TPU:0, one launch (start us, length us, event | category | flops | bytes accessed | tf_op | source)
XLA Modules:
  0.0 184.4 jit_solution(373645483599434225)
XLA Ops:
  7.2 1.1 select_reduce_fusion
  8.3 0.9 mul.150
  9.3 4.8 %collective-permute-start = (f32[1,128,128]{2,1,0:T(8,128)S(1)}, f32[1,128,128]{2,1,0:T(8,128)S(1)}, u32[]{:S(2)}, u32[]{:S(2)}) collective-permute-start(f32[1,128,128]{2,1,0:T(8,128)S(1)} %slice.283), channel_id=1, source_target_pairs={{0,2},{2,4},{4,6},{6,8},{8,10},{10,12},{12,14},{14,16},{16,18},{18... | collective-permute-start | bytes 196616 | tf_op jit(solution)/shard_map/ppermute | solution.py:13
  14.1 0.9 subtract_convert_fusion
  15.0 1.0 collective-permute-done
  16.0 1.1 fusion.86
  17.1 1.1 bitcast_dynamic-update-slice_fusion.3
  18.2 1.3 collective-permute-start.1
  19.5 6.7 %collective-permute-done.1 = f32[1,3,1,128,128]{4,3,2,1,0:T(8,128)S(1)} collective-permute-done((f32[1,3,1,128,128]{4,3,2,1,0:T(8,128)S(1)}, f32[1,3,1,128,128]{4,3,2,1,0:T(8,128)S(1)}, u32[]{:S(2)}, u32[]{:S(2)}) %collective-permute-start.1) | collective-permute-done | bytes 196640 | tf_op jit(solution)/shard_map/ppermute | solution.py:13
  26.3 0.2 fusion.31
  26.5 0.2 fusion.35
  26.7 0.2 fusion.37
  26.9 0.2 fusion.41
  27.2 4.6 %fusion.6 = f32[1,3,8,2,128,128]{5,2,1,4,3,0:T(8,128)S(1)} fusion(f32[24,24,1,1]{1,0,3,2:T(8,128)S(1)} %copy-done.3, f32[1,3,8,2,128,128]{5,4,3,1,2,0:T(8,128)S(1)} %fusion.41, f32[2,128,128]{2,1,0:T(8,128)S(1)} %mul.150), kind=kOutput, calls=%fused_computation.9 | convolution fusion | flops 227278848 | bytes 6424832 | tf_op jit(solution)/shard_map/ab,...bzyx->...azyx/dot_general | solution.py:78
  31.7 2.1 %fusion.91 = (f32[1,3,1,2,128,128]{5,2,1,4,3,0:T(1,128)S(1)}, f32[1,3,1,2,128,128]{5,2,1,4,3,0:T(1,128)S(1)}, f32[1,3,1,2,128,128]{5,2,1,4,3,0:T(1,128)S(1)}, f3...) fusion(f32[1,3,8,2,128,128]{5,2,1,4,3,0:T(8,128)S(1)} %fusion.6), kind=kLoop, calls=%fused_computation.170 | loop fusion | bytes 6291456 | tf_op jit(solution)/shard_map/slice | solution.py:89
  34.2 0.9 pad_add_fusion.1
  35.1 4.7 %collective-permute-start.2 = (f32[1,3,1,128,128]{4,3,2,1,0:T(8,128)S(1)}, f32[1,3,1,128,128]{4,3,2,1,0:T(8,128)S(1)}, u32[]{:S(2)}, u32[]{:S(2)}) collective-permute-start(f32[1,3,1,128,128]{4,3,2,1,0:T(8,128)S(1)} %slice.298), channel_id=1, source_target_pairs={{0,2},{2,4},{4,6},{6,8},{8,10},{10,12},{12,14},{14,16},{16,18},{18... | collective-permute-start | bytes 589832 | tf_op jit(solution)/shard_map/ppermute | solution.py:13
  39.8 3.2 %collective-permute-done.2 = f32[1,3,1,128,128]{4,3,2,1,0:T(8,128)S(1)} collective-permute-done((f32[1,3,1,128,128]{4,3,2,1,0:T(8,128)S(1)}, f32[1,3,1,128,128]{4,3,2,1,0:T(8,128)S(1)}, u32[]{:S(2)}, u32[]{:S(2)}) %collective-permute-start.2) | collective-permute-done | bytes 196640 | tf_op jit(solution)/shard_map/ppermute | solution.py:13
  43.1 0.7 multiply_reduce_fusion.1
  43.8 42.2 %all-reduce.22 = (f32[1]{0:T(128)}, f32[1]{0:T(128)}) all-reduce(f32[1]{0:T(128)} %bitcast, f32[1]{0:T(128)} %bitcast.24), channel_id=1, replica_groups=mesh['space'=16,'load'=2] {'space'}, use_global_device_ids=true, to_apply=%region_2.3 | all-reduce | flops 2 | bytes 16 | tf_op jit(solution)/shard_map/psum | solution.py:148
  87.3 0.1 bitcast_dynamic-update-slice_fusion.2
  87.4 1.5 collective-permute-start.3
  88.9 6.1 %collective-permute-done.3 = f32[1,3,1,128,128]{4,3,2,1,0:T(8,128)S(1)} collective-permute-done((f32[1,3,1,128,128]{4,3,2,1,0:T(8,128)S(1)}, f32[1,3,1,128,128]{4,3,2,1,0:T(8,128)S(1)}, u32[]{:S(2)}, u32[]{:S(2)}) %collective-permute-start.3) | collective-permute-done | bytes 196640 | tf_op jit(solution)/shard_map/ppermute | solution.py:13
  95.0 0.2 fusion.43
  95.3 0.2 fusion.47
  95.5 0.2 fusion.49
  95.7 0.2 fusion.53
  95.8 4.6 %fusion.3 = f32[1,3,8,2,128,128]{5,2,1,4,3,0:T(8,128)S(1)} fusion(f32[24,24,1,1]{1,0,3,2:T(8,128)S(1)} %copy-done.3, f32[1,3,8,2,128,128]{5,4,3,1,2,0:T(8,128)S(1)} %fusion.53, f32[2,128,128]{2,1,0:T(8,128)S(1)} %mul.150), kind=kOutput, calls=%fused_computation.5 | convolution fusion | flops 227278848 | bytes 6424832 | tf_op jit(solution)/shard_map/ab,...bzyx->...azyx/dot_general | solution.py:78
  100.4 2.1 %fusion.90 = (f32[1,3,1,2,128,128]{5,2,1,4,3,0:T(1,128)S(1)}, f32[1,3,1,2,128,128]{5,2,1,4,3,0:T(1,128)S(1)}, f32[1,3,1,2,128,128]{5,2,1,4,3,0:T(1,128)S(1)}, f3...) fusion(f32[1,3,8,2,128,128]{5,2,1,4,3,0:T(8,128)S(1)} %fusion.3), kind=kLoop, calls=%fused_computation.169 | loop fusion | bytes 6291456 | tf_op jit(solution)/shard_map/slice | solution.py:89
  102.8 0.9 pad_add_fusion
  103.8 2.5 %collective-permute-start.4 = (f32[1,3,1,128,128]{4,3,2,1,0:T(8,128)S(1)}, f32[1,3,1,128,128]{4,3,2,1,0:T(8,128)S(1)}, u32[]{:S(2)}, u32[]{:S(2)}) collective-permute-start(f32[1,3,1,128,128]{4,3,2,1,0:T(8,128)S(1)} %slice.312), channel_id=1, source_target_pairs={{0,2},{2,4},{4,6},{6,8},{8,10},{10,12},{12,14},{14,16},{16,18},{18... | collective-permute-start | bytes 589832 | tf_op jit(solution)/shard_map/ppermute | solution.py:13
  106.3 3.2 %collective-permute-done.4 = f32[1,3,1,128,128]{4,3,2,1,0:T(8,128)S(1)} collective-permute-done((f32[1,3,1,128,128]{4,3,2,1,0:T(8,128)S(1)}, f32[1,3,1,128,128]{4,3,2,1,0:T(8,128)S(1)}, u32[]{:S(2)}, u32[]{:S(2)}) %collective-permute-start.4) | collective-permute-done | bytes 196640 | tf_op jit(solution)/shard_map/ppermute | solution.py:13
  109.6 0.8 fusion.79
  110.5 39.7 %all-reduce.21 = (f32[1]{0:T(128)}, f32[1]{0:T(128)}) all-reduce(f32[1]{0:T(128)} %bitcast.26, f32[1]{0:T(128)} %bitcast.49), channel_id=1, replica_groups=mesh['space'=16,'load'=2] {'space'}, use_global_device_ids=true, to_apply=%region_6.7 | all-reduce | flops 2 | bytes 16 | tf_op jit(solution)/shard_map/psum | solution.py:148
  154.6 0.1 bitcast_dynamic-update-slice_fusion.1
  154.7 1.5 collective-permute-start.5
  156.3 8.1 %collective-permute-done.5 = f32[1,3,2,128,128]{4,3,2,1,0:T(8,128)S(1)} collective-permute-done((f32[1,3,2,128,128]{4,3,2,1,0:T(8,128)S(1)}, f32[1,3,2,128,128]{4,3,2,1,0:T(8,128)S(1)}, u32[]{:S(2)}, u32[]{:S(2)}) %collective-permute-start.5) | collective-permute-done | bytes 393248 | tf_op jit(solution)/shard_map/ppermute | solution.py:13
  164.5 0.2 fusion.55
  164.7 0.2 fusion.59
  164.9 0.2 fusion.61
  165.1 0.2 fusion.65
  165.4 0.2 fusion.67
  165.6 0.2 fusion.71
  165.8 0.2 fusion.73
  166.0 0.2 fusion.77
  166.2 6.7 %fusion = f32[2,128,128]{2,1,0:T(8,128)S(1)} fusion(f32[1,3,8,2,128,128]{5,4,3,1,2,0:T(8,128)S(1)} %fusion.65, f32[24,24,1,1]{1,0,3,2:T(8,128)S(1)} %copy-done.3, f32[1,3,8,2,128,128]{5,4,3,1,2,0:T(8,128)S(1)} %fusion.77), kind=kOutput, calls=%fused_computation.1 | convolution fusion | flops 228032512 | bytes 6424832 | tf_op jit(solution)/shard_map/ab,...bzyx->...azyx/dot_general | solution.py:78
  172.9 0.7 mul.179
  173.6 4.0 %reduce-scatter.2.cloned.1.call-done = f32[2,64,128]{2,1,0:T(8,128)} async-done(((f32[2,128,128]{2,1,0:T(8,128)}), f32[2,64,128]{2,1,0:T(8,128)}) %reduce-scatter.2.cloned.1.call-update) | async-done | bytes 65552 | tf_op jit(solution)/shard_map/reduce_scatter | solution.py:168
  (52 shorter events, 1.4 us)
Async XLA Ops:
  7.2 170.4 %reduce-scatter.2.cloned.1.call-start = ((), (), s32[]{:S(2)}) async-start(), calls=%async_computation.1 | async-start | bytes 196608 | tf_op jit(solution)/shard_map/reduce_scatter | solution.py:168
  9.3 6.7 %collective-permute-start = (f32[1,128,128]{2,1,0:T(8,128)S(1)}, f32[1,128,128]{2,1,0:T(8,128)S(1)}, u32[]{:S(2)}, u32[]{:S(2)}) collective-permute-start(f32[1,128,128]{2,1,0:T(8,128)S(1)} %slice.283), channel_id=1, source_target_pairs={{0,2},{2,4},{4,6},{6,8},{8,10},{10,12},{12,14},{14,16},{16,18},{18... | collective-permute-start | bytes 196616 | tf_op jit(solution)/shard_map/ppermute | solution.py:13
  18.2 8.0 %collective-permute-start.1 = (f32[1,3,1,128,128]{4,3,2,1,0:T(8,128)S(1)}, f32[1,3,1,128,128]{4,3,2,1,0:T(8,128)S(1)}, u32[]{:S(2)}, u32[]{:S(2)}) collective-permute-start(f32[1,3,1,128,128]{4,3,2,1,0:T(8,128)S(1)} %slice.286), channel_id=1, source_target_pairs={{2,0},{4,2},{6,4},{8,6},{10,8},{12,10},{14,12},{16,14},{18,16},{20... | collective-permute-start | bytes 589832 | tf_op jit(solution)/shard_map/ppermute | solution.py:13
  26.4 0.7 copy-start.3
  34.2 8.9 %copy-start = (f32[1,3,2,128,128]{4,3,2,1,0:T(8,128)S(1)}, f32[1,3,2,128,128]{4,3,2,1,0:T(8,128)}, u32[]{:S(2)}) copy-start(f32[1,3,2,128,128]{4,3,2,1,0:T(8,128)} %param.8) | copy-start | bytes 1179652
  35.1 7.9 %collective-permute-start.2 = (f32[1,3,1,128,128]{4,3,2,1,0:T(8,128)S(1)}, f32[1,3,1,128,128]{4,3,2,1,0:T(8,128)S(1)}, u32[]{:S(2)}, u32[]{:S(2)}) collective-permute-start(f32[1,3,1,128,128]{4,3,2,1,0:T(8,128)S(1)} %slice.298), channel_id=1, source_target_pairs={{0,2},{2,4},{4,6},{6,8},{8,10},{10,12},{12,14},{14,16},{16,18},{18... | collective-permute-start | bytes 589832 | tf_op jit(solution)/shard_map/ppermute | solution.py:13
  87.4 7.6 %collective-permute-start.3 = (f32[1,3,1,128,128]{4,3,2,1,0:T(8,128)S(1)}, f32[1,3,1,128,128]{4,3,2,1,0:T(8,128)S(1)}, u32[]{:S(2)}, u32[]{:S(2)}) collective-permute-start(f32[1,3,1,128,128]{4,3,2,1,0:T(8,128)S(1)} %slice.300), channel_id=1, source_target_pairs={{2,0},{4,2},{6,4},{8,6},{10,8},{12,10},{14,12},{16,14},{18,16},{20... | collective-permute-start | bytes 589832 | tf_op jit(solution)/shard_map/ppermute | solution.py:13
  103.7 51.0 %slice-start = ((f32[1,3,2,128,128]{4,3,2,1,0:T(8,128)}), f32[1,3,1,128,128]{4,3,2,1,0:T(8,128)S(1)}, s32[]{:S(2)}) async-start(f32[1,3,2,128,128]{4,3,2,1,0:T(8,128)} %param.7), calls=%async_computation.2 | async-start | bytes 393216 | tf_op jit(solution)/shard_map/slice | solution.py:163
  103.8 52.5 %copy-start.1 = (f32[1,3,2,128,128]{4,3,2,1,0:T(8,128)S(1)}, f32[1,3,2,128,128]{4,3,2,1,0:T(8,128)}, u32[]{:S(2)}) copy-start(f32[1,3,2,128,128]{4,3,2,1,0:T(8,128)} %param.7) | copy-start | bytes 1179652
  103.8 5.8 %collective-permute-start.4 = (f32[1,3,1,128,128]{4,3,2,1,0:T(8,128)S(1)}, f32[1,3,1,128,128]{4,3,2,1,0:T(8,128)S(1)}, u32[]{:S(2)}, u32[]{:S(2)}) collective-permute-start(f32[1,3,1,128,128]{4,3,2,1,0:T(8,128)S(1)} %slice.312), channel_id=1, source_target_pairs={{0,2},{2,4},{4,6},{6,8},{8,10},{10,12},{12,14},{14,16},{16,18},{18... | collective-permute-start | bytes 589832 | tf_op jit(solution)/shard_map/ppermute | solution.py:13
  154.7 10.2 %copy-start.2 = (f32[1,3,2,128,128]{4,3,2,1,0:T(8,128)}, f32[1,3,2,128,128]{4,3,2,1,0:T(8,128)S(1)}, u32[]{:S(2)}) copy-start(f32[1,3,2,128,128]{4,3,2,1,0:T(8,128)S(1)} %get-tuple-element.11) | copy-start | bytes 1179652
  154.7 9.7 %collective-permute-start.5 = (f32[1,3,2,128,128]{4,3,2,1,0:T(8,128)S(1)}, f32[1,3,2,128,128]{4,3,2,1,0:T(8,128)S(1)}, u32[]{:S(2)}, u32[]{:S(2)}) collective-permute-start(f32[1,3,2,128,128]{4,3,2,1,0:T(8,128)S(1)} %pad_maximum_fusion.4), channel_id=1, source_target_pairs={{2,0},{4,2},{6,4},{8,6},{10,8},{12,10},{14,12},{16,14},{18,16},{20... | collective-permute-start | bytes 1179656 | tf_op jit(solution)/shard_map/ppermute | solution.py:13
Sparse Core Ops, SparseCore 0:
  173.7 3.7 reduce-scatter.1
where the time goes:
time: 185 us; the launch traced here: 184 us
  blocking collectives  81.9 us (44%)
  waiting for transfers between devices  32.2 us (17%)
  between operations  20.3 us (11%)
  starting transfers between devices  16.4 us (9%)
  matrix products  15.9 us (9%)
  other arithmetic  9.75 us (5%)
  local copies, waits for them, and re-layouts  7.95 us (4%)
    psum x2, blocking collectives, shards(): lax.psum((inner(residual, precond), inner(image, precond)), 'space')  81.9 us
    ppermute x6, waiting for transfers between devices, from_behind(): return lax.ppermute(shard, axis, pairs)  28.3 us
    ppermute x6, starting transfers between devices, from_behind(): return lax.ppermute(shard, axis, pairs)  16.4 us
    dot_general x3, matrix products, stiff_product(): jnp.einsum('ab,...bzyx->...azyx', stiffness, vectors, precision=lax.Preci...  15.9 us
    slice x2, local copies, waits for them, and re-layouts, assemble(): split[..., corner, :, :, :]  4.29 us
    reduce_scatter x1, waiting for transfers between devices, shards(): lax.psum_scatter(term, 'load', scatter_dimension=1, tiled=True)  3.96 us
  transfers between devices with their start and end apart: 7, of which 7 were waited for; matrix products, arithmetic and copies ran while one was open for 1% of the time, Pallas kernels for 0%

commit v1 on v0

v1 whole, which is shorter than its diff:
```python
import functools

import jax
import jax.numpy as jnp
from jax import lax
from jax.experimental import pallas as pl
from jax.experimental.pallas import tpu as pltpu
from jax.sharding import PartitionSpec as P

POISSON = 0.3
SHEAR = 0.5 / (1.0 + POISSON)
RATIO = 2.0 * POISSON / (1.0 - 2.0 * POISSON)
CLASS = [0.0] + [12.0 * SHEAR / 64.0 / 3.0**order for order in (1, 2, 3)]
CORNER = CLASS[1] * (RATIO + 4.0) + CLASS[2] * (2.0 * (RATIO + 3.0) + 2.0) + CLASS[3] * (RATIO + 4.0)
ROWS = 8


def permute(shard, axis, by, wrap=False):
    devices = lax.axis_size(axis)
    if wrap:
        pairs = [(i, (i + by) % devices) for i in range(devices)]
    else:
        pairs = [(i, i + by) for i in range(devices) if 0 <= i + by < devices]
    return lax.ppermute(shard, axis, pairs)


def next_lane(value):
    width = value.shape[-1]
    lane = lax.broadcasted_iota(jnp.int32, value.shape, value.ndim - 1)
    return jnp.where(lane == width - 1, 0.0, pltpu.roll(value, width - 1, value.ndim - 1))


def last_lane(value):
    lane = lax.broadcasted_iota(jnp.int32, value.shape, value.ndim - 1)
    return jnp.where(lane == 0, 0.0, pltpu.roll(value, 1, value.ndim - 1))


def store_pair(ref, at, rows, value):
    after = next_lane(value)
    ref[at + (0, rows)] = value + after
    ref[at + (1, rows)] = after - value


def plane_modes(ref, plane, start):
    out = []
    for comp in range(3):
        per = []
        for along in range(2):
            here = ref[plane, comp, along, pl.ds(start, ROWS), :]
            below = ref[plane, comp, along, pl.ds(start + 1, ROWS), :]
            per.append((here + below, below - here))
        out.append(per)
    return out


def layer_modes(low, high):
    out = []
    for comp in range(3):
        modes = {}
        for a in range(2):
            for b in range(2):
                if a or b:
                    modes[a, b, 0] = low[comp][a][b] + high[comp][a][b]
                modes[a, b, 1] = high[comp][a][b] - low[comp][a][b]
        out.append(modes)
    return out


PAIRS = (((0, (1, 1, 0)), (2, (0, 1, 1))), ((1, (1, 1, 0)), (2, (1, 0, 1))), ((0, (1, 0, 1)), (1, (0, 1, 1))))


def stiff(modes):
    u, v, w = modes
    out = [{}, {}, {}]
    trace = RATIO * (u[1, 0, 0] + v[0, 1, 0] + w[0, 0, 1])
    out[0][1, 0, 0] = trace + 2.0 * u[1, 0, 0]
    out[1][0, 1, 0] = trace + 2.0 * v[0, 1, 0]
    out[2][0, 0, 1] = trace + 2.0 * w[0, 0, 1]
    for (one, at), (two, by) in PAIRS:
        both = RATIO * (modes[one][at] + modes[two][by])
        out[one][at] = both + 3.0 * modes[one][at]
        out[two][by] = both + 3.0 * modes[two][by]
    out[0][0, 1, 0] = out[1][1, 0, 0] = u[0, 1, 0] + v[1, 0, 0]
    out[1][0, 0, 1] = out[2][0, 1, 0] = v[0, 0, 1] + w[0, 1, 0]
    out[2][1, 0, 0] = out[0][0, 0, 1] = w[1, 0, 0] + u[0, 0, 1]
    first = u[0, 1, 1] + v[1, 0, 1]
    second = v[1, 0, 1] + w[1, 1, 0]
    third = w[1, 1, 0] + u[0, 1, 1]
    out[0][0, 1, 1] = first + third
    out[1][1, 0, 1] = first + second
    out[2][1, 1, 0] = second + third
    for comp in range(3):
        out[comp][1, 1, 1] = (RATIO + 4.0) * modes[comp][1, 1, 1]
    return out


def paired(modes, forces):
    total = None
    for order in (1, 2, 3):
        part = None
        for comp in range(3):
            for key, force in forces[comp].items():
                if sum(key) == order:
                    term = modes[comp][key] * force
                    part = term if part is None else part + term
        part = CLASS[order] * part
        total = part if total is None else total + part
    return total


def pack_kernel(base_ref, rhs_ref, factor_ref, ids_ref, mask_ref, up_ref, down_ref, res_ref, mod_ref, scale_ref):
    layers, height, width = factor_ref.shape
    ids = ids_ref[...]
    scale = jnp.zeros(ids.shape, jnp.float32)
    for zone in range(base_ref.shape[0]):
        scale = jnp.where(ids == zone, base_ref[zone], scale)
    modulus = factor_ref[...] * scale
    scale_ref[...] = scale
    mod_ref[...] = modulus
    free = 1.0 - mask_ref[...].astype(jnp.float32)
    res = free[None] * rhs_ref[0]
    res_ref[...] = res
    row = lax.broadcasted_iota(jnp.int32, (height, width), 0)

    def inverse(lower, upper, free):
        total = lower + upper
        total = total + last_lane(total)
        total = total + jnp.where(row == 0, 0.0, pltpu.roll(total, 1, 0))
        return free / (CORNER * total)

    high = res[:, layers - 1] * inverse(modulus[layers - 2], modulus[layers - 1], free[layers - 1])
    up_ref[0:3] = high
    up_ref[3] = modulus[layers - 1]
    second = high if layers == 2 else res[:, 1] * inverse(modulus[0], modulus[1], free[1])
    down_ref[0:3] = res[:, 0]
    down_ref[3:6] = second
    down_ref[6] = modulus[0]
    down_ref[7] = free[0]


def image_kernel(
    mask_ref, up_ref, down_ref, res_ref, mod_ref, z_ref, v_ref, sums_ref, z_pair, v_pair, carry, edge, inv
):
    layers, height, width = mod_ref.shape
    blocks = height // ROWS

    def modulus(layer, rows):
        if layer < 0:
            return up_ref[3, rows, :]
        return mod_ref[layer, rows, :] if layer < layers else down_ref[6, rows, :]

    edge[:, 0:ROWS, :] = jnp.zeros((layers + 1, ROWS, width), jnp.float32)
    z_pair[:, :, :, height : height + ROWS, :] = jnp.zeros((layers + 3, 3, 2, ROWS, width), jnp.float32)
    v_pair[:, :, :, height : height + ROWS, :] = jnp.zeros((layers + 1, 3, 2, ROWS, width), jnp.float32)
    carry[:, :, :, 0:ROWS, :] = jnp.zeros((layers + 1, 3, 2, ROWS, width), jnp.float32)

    def start_block(block, norm):
        start = pl.multiple_of(block * ROWS, ROWS)
        rows = pl.ds(start, ROWS)
        for plane in range(layers + 1):
            total = modulus(plane - 1, rows) + modulus(plane, rows)
            total = total + last_lane(total)
            edge[plane, pl.ds(start + ROWS, ROWS), :] = total
            total = total + edge[plane, pl.ds(start + ROWS - 1, ROWS), :]
            free = down_ref[7, rows, :] if plane == layers else 1.0 - mask_ref[plane, rows, :].astype(jnp.float32)
            inverse = free / (CORNER * total)
            inv[plane, rows, :] = inverse
            for comp in range(3):
                res = res_ref[comp, plane, rows, :] if plane < layers else down_ref[comp, rows, :]
                z = inverse * res
                z_ref[comp, plane, rows, :] = z
                store_pair(z_pair, (plane + 1, comp), rows, z)
                if plane < layers:
                    norm = norm + res * z
        for comp in range(3):
            store_pair(z_pair, (0, comp), rows, up_ref[comp, rows, :])
            store_pair(z_pair, (layers + 2, comp), rows, down_ref[3 + comp, rows, :])
        return norm

    zero = jnp.zeros((ROWS, width), jnp.float32)
    norm = lax.fori_loop(0, blocks, start_block, zero)

    def image_block(block, sums):
        along, across = sums
        start = pl.multiple_of(block * ROWS, ROWS)
        rows = pl.ds(start, ROWS)
        low = plane_modes(z_pair, 0, start)
        held = None
        for layer in range(layers + 2):
            high = plane_modes(z_pair, layer + 1, start)
            forces = stiff(layer_modes(low, high))
            stiffness = modulus(layer - 1, rows)
            weight = [None] + [CLASS[order] * stiffness for order in (1, 2, 3)]
            lower, upper = {}, {}
            for comp in range(3):
                for a in range(2):
                    for b in range(2):
                        change = weight[a + b + 1] * forces[comp][a, b, 1]
                        if a or b:
                            level = weight[a + b] * forces[comp][a, b, 0]
                            lower[comp, a, b] = level - change
                            upper[comp, a, b] = level + change
                        else:
                            lower[comp, a, b] = -change
                            upper[comp, a, b] = change
            if layer > 0:
                plane = layer - 1
                inverse = inv[plane, rows, :]
                for comp in range(3):
                    sides = []
                    for a in range(2):
                        level = held[comp, a, 0] + lower[comp, a, 0]
                        change = held[comp, a, 1] + lower[comp, a, 1]
                        carry[plane, comp, a, pl.ds(start + 1, ROWS), :] = level + change
                        sides.append(level - change + carry[plane, comp, a, rows, :])
                    image = sides[0] - sides[1] + last_lane(sides[0] + sides[1])
                    v = inverse * image
                    v_ref[comp, plane, rows, :] = v
                    store_pair(v_pair, (plane, comp), rows, v)
                    if plane < layers:
                        along = along + image * z_ref[comp, plane, rows, :]
                        across = across + image * v
            held = upper
            low = high
        return along, across

    along, across = lax.fori_loop(0, blocks, image_block, (zero, zero))

    def energy_block(block, energy):
        start = pl.multiple_of(block * ROWS, ROWS)
        low = plane_modes(v_pair, 0, start)
        for layer in range(layers):
            high = plane_modes(v_pair, layer + 1, start)
            modes = layer_modes(low, high)
            energy = energy + mod_ref[layer, pl.ds(start, ROWS), :] * paired(modes, stiff(modes))
            low = high
        return energy

    energy = lax.fori_loop(0, blocks, energy_block, zero)
    lane = lax.broadcasted_iota(jnp.int32, sums_ref.shape, 1)
    out = jnp.zeros(sums_ref.shape, jnp.float32)
    for place, part in enumerate((norm, along, across, energy)):
        out = jnp.where(lane == place, jnp.sum(part), out)
    sums_ref[...] = out


def finish_kernel(load_ref, sums_ref, z_ref, v_ref, disp_ref, above_ref, scale_ref, x_ref, grad_ref, x_pair, u_pair):
    layers, height, width = scale_ref.shape
    blocks = height // ROWS
    loads = load_ref[1]
    device = lax.broadcasted_iota(jnp.int32, sums_ref.shape, 0)
    lane = lax.broadcasted_iota(jnp.int32, sums_ref.shape, 1)
    mine = jnp.where(lax.rem(device, loads) == load_ref[0], sums_ref[...], 0.0)
    norm, along, across, energy = [jnp.sum(jnp.where(lane == place, mine, 0.0)) for place in range(4)]
    tail = (ROWS, width)
    norm, along, across, energy = [jnp.full(tail, part) for part in (norm, along, across, energy)]
    first = norm / along
    later = first * first * across - norm
    second = later / (first * first * (energy - across * across / along))
    from_z = first + second * (first * across / along)
    from_v = second * first
    x_pair[:, :, :, height : height + ROWS, :] = jnp.zeros((layers + 1, 3, 2, ROWS, width), jnp.float32)
    u_pair[:, :, :, height : height + ROWS, :] = jnp.zeros((layers + 1, 3, 2, ROWS, width), jnp.float32)

    def combine_block(block, _):
        rows = pl.ds(pl.multiple_of(block * ROWS, ROWS), ROWS)
        for comp in range(3):
            for plane in range(layers + 1):
                x = from_z * z_ref[comp, plane, rows, :] - from_v * v_ref[comp, plane, rows, :]
                if plane < layers:
                    x_ref[0, comp, plane, rows, :] = x
                store_pair(x_pair, (plane, comp), rows, x)
                u = disp_ref[0, comp, plane, rows, :] if plane < layers else above_ref[comp, rows, :]
                store_pair(u_pair, (plane, comp), rows, u)
        return 0

    lax.fori_loop(0, blocks, combine_block, 0)

    def grad_block(block, _):
        start = pl.multiple_of(block * ROWS, ROWS)
        rows = pl.ds(start, ROWS)
        x_low = plane_modes(x_pair, 0, start)
        u_low = plane_modes(u_pair, 0, start)
        for layer in range(layers):
            x_high = plane_modes(x_pair, layer + 1, start)
            u_high = plane_modes(u_pair, layer + 1, start)
            term = paired(layer_modes(x_low, x_high), stiff(layer_modes(u_low, u_high)))
            grad_ref[layer, rows, :] = term * scale_ref[layer, rows, :]
            x_low, u_low = x_high, u_high
        return 0

    lax.fori_loop(0, blocks, grad_block, 0)


def f32(*shape):
    return jax.ShapeDtypeStruct(shape, jnp.float32)


def shards(forward_disp, adjoint_rhs, modulus_factor, zone_base, zone_ids, fixed_mask):
    layers, height, width = modulus_factor.shape
    loads = lax.axis_size("load")
    devices = lax.axis_size("space") * loads
    load = lax.axis_index("load")
    whole = pl.BlockSpec(memory_space=pltpu.VMEM)
    scalar = pl.BlockSpec(memory_space=pltpu.SMEM)
    params = pltpu.CompilerParams(vmem_limit_bytes=32 * 2**20)
    pad = height + ROWS

    up, down, res, modulus, scale = pl.pallas_call(
        pack_kernel,
        out_shape=(
            f32(4, height, width),
            f32(8, height, width),
            f32(3, layers, height, width),
            f32(layers, height, width),
            f32(layers, height, width),
        ),
        in_specs=[scalar] + [whole] * 4,
        out_specs=[whole] * 5,
        compiler_params=params,
        name="pack",
    )(zone_base, adjoint_rhs, modulus_factor, zone_ids, fixed_mask)
    from_below = permute(up, "space", 1)
    from_above = permute(down, "space", -1)
    above_disp = permute(forward_disp[0, :, 0], "space", -1)

    z, v, sums = pl.pallas_call(
        image_kernel,
        out_shape=(
            f32(3, layers + 1, height, width),
            f32(3, layers + 1, height, width),
            f32(devices, 128),
        ),
        in_specs=[whole] * 5,
        out_specs=[whole] * 3,
        scratch_shapes=[
            pltpu.VMEM((layers + 3, 3, 2, pad, width), jnp.float32),
            pltpu.VMEM((layers + 1, 3, 2, pad, width), jnp.float32),
            pltpu.VMEM((layers + 1, 3, 2, pad, width), jnp.float32),
            pltpu.VMEM((layers + 1, pad, width), jnp.float32),
            pltpu.VMEM((layers + 1, height, width), jnp.float32),
        ],
        compiler_params=params,
        name="image",
    )(fixed_mask, from_below, from_above, res, modulus)
    sums = lax.all_to_all(sums, ("space", "load"), 0, 0, tiled=True)

    solution, grad = pl.pallas_call(
        finish_kernel,
        out_shape=(f32(1, 3, layers, height, width), f32(layers, height, width)),
        in_specs=[scalar] + [whole] * 6,
        out_specs=[whole] * 2,
        scratch_shapes=[
            pltpu.VMEM((layers + 1, 3, 2, pad, width), jnp.float32),
            pltpu.VMEM((layers + 1, 3, 2, pad, width), jnp.float32),
        ],
        compiler_params=params,
        name="finish",
    )(jnp.stack([load, loads]).astype(jnp.int32), sums, z, v, forward_disp, above_disp, scale)
    share = height // loads
    total = lax.dynamic_slice_in_dim(grad, load * share, share, 1)
    for by in range(1, loads):
        other = lax.dynamic_slice_in_dim(grad, (load + by) % loads * share, share, 1)
        total = total + permute(other, "load", by, wrap=True)
    return (solution, total)


def solution(mesh):
    placed = (
        P("load", None, "space", None, None),
        P("load", None, "space", None, None),
        P("space", None, None),
        P(),
        P("space", None, None),
        P("space", None, None),
    )
    return jax.shard_map(
        shards,
        mesh=mesh,
        in_specs=placed,
        out_specs=(P("load", None, "space", None, None), P("space", "load", None)),
        check_vma=False,
    )
```

time: 185 us -> 59.5 us (0.32)
  blocking collectives: 81.9 us -> 0 us
  between operations: 20.3 us -> 0.73 us
  matrix products: 15.9 us -> 0 us
  Pallas kernels: 0 us -> 12.7 us
  other arithmetic: 9.75 us -> 0.71 us
  waiting for transfers between devices: 32.2 us -> 27.7 us
  local copies, waits for them, and re-layouts: 7.95 us -> 4.39 us
  starting transfers between devices: 16.4 us -> 13.1 us
    psum x2 -> x0, blocking collectives: 81.9 us -> none  [shards(): lax.psum((inner(residual, precond), inner(image, precond)), 'space')]
    dot_general x3 -> x0, matrix products: 15.9 us -> none  [stiff_product(): jnp.einsum('ab,...bzyx->...azyx', stiffness, vectors, precision=lax.Preci...]
    pallas_call x0 -> x3, Pallas kernels: none -> 12.7 us  [the longest x1 8.04 us: shards(): pl.pallas_call(image_kernel, out_shape=(f32(3, layers + 1, height, width)...]
    ppermute x6 -> x4, starting transfers between devices: 16.4 us -> 8.21 us  [permute(): return lax.ppermute(shard, axis, pairs)]
    ppermute x6 -> x4, waiting for transfers between devices: 28.3 us -> 20.7 us  [permute(): return lax.ppermute(shard, axis, pairs)]
    all_to_all x0 -> x1, waiting for transfers between devices: none -> 6.99 us  [shards(): sums = lax.all_to_all(sums, ('space', 'load'), 0, 0, tiled=True)]
    all_to_all x0 -> x1, starting transfers between devices: none -> 4.87 us  [shards(): sums = lax.all_to_all(sums, ('space', 'load'), 0, 0, tiled=True)]
    slice x11 -> x0, local copies, waits for them, and re-layouts: 4.4 us -> none  [the longest x2 4.29 us: assemble(): split[..., corner, :, :, :]]
  transfers between devices with their start and end apart: 7 -> 5, of which waited for: 7 -> 3; matrix products, arithmetic and copies ran while one was open for 1% -> 0% of each run, Pallas kernels for 0% -> 14%
where the time goes in v1:
time: 59.5 us; the launch traced here: 59.2 us
  waiting for transfers between devices  27.7 us (47%)
  starting transfers between devices  13.1 us (22%)
  Pallas kernels  12.7 us (21%)
  local copies, waits for them, and re-layouts  4.39 us (7%)
  between operations  0.73 us (1%)
  other arithmetic  0.71 us (1%)
    ppermute x4, waiting for transfers between devices, permute(): return lax.ppermute(shard, axis, pairs)  20.7 us
    ppermute x4, starting transfers between devices, permute(): return lax.ppermute(shard, axis, pairs)  8.21 us
    pallas_call x1, Pallas kernels, shards(): pl.pallas_call(image_kernel, out_shape=(f32(3, layers + 1, height, width)...  8.04 us
    all_to_all x1, waiting for transfers between devices, shards(): sums = lax.all_to_all(sums, ('space', 'load'), 0, 0, tiled=True)  6.99 us
    all_to_all x1, starting transfers between devices, shards(): sums = lax.all_to_all(sums, ('space', 'load'), 0, 0, tiled=True)  4.87 us
    unnamed x14, local copies, waits for them, and re-layouts  4.37 us
    pallas_call x1, Pallas kernels, shards(): pl.pallas_call(finish_kernel, out_shape=(f32(1, 3, layers, height, width)...  3.92 us
  transfers between devices with their start and end apart: 5, of which 3 were waited for; matrix products, arithmetic and copies ran while one was open for 0% of the time, Pallas kernels for 14%

profile of v1, /device:TPU:0, one launch (start us, length us, event | category | flops | bytes accessed | tf_op | source)
XLA Modules:
  0.0 59.2 jit_solution(7412360479676339529)
XLA Ops:
  0.6 0.0 copy-start.1
  0.6 0.9 %copy-done.1 = s32[2,128,128]{2,1,0:T(8,128)S(1)} copy-done((s32[2,128,128]{2,1,0:T(8,128)S(1)}, s32[2,128,128]{2,1,0:T(8,128)}, u32[]{:S(2)}) %copy-start.1) | copy-done | bytes 131096
  1.5 0.0 copy-start.3
  1.5 1.0 %copy-done.3 = f32[1,3,2,128,128]{4,3,2,1,0:T(8,128)S(1)} copy-done((f32[1,3,2,128,128]{4,3,2,1,0:T(8,128)S(1)}, f32[1,3,2,128,128]{4,3,2,1,0:T(8,128)}, u32[]{:S(2)}) %copy-start.3) | copy-done | bytes 393240
  2.5 0.0 copy-start.4
  2.5 0.9 %copy-done.4 = f32[2,128,128]{2,1,0:T(8,128)S(1)} copy-done((f32[2,128,128]{2,1,0:T(8,128)S(1)}, f32[2,128,128]{2,1,0:T(8,128)}, u32[]{:S(2)}) %copy-start.4) | copy-done | bytes 131096
  3.4 0.0 copy-start.5
  3.4 0.9 %copy-done.5 = s32[2,128,128]{2,1,0:T(8,128)S(1)} copy-done((s32[2,128,128]{2,1,0:T(8,128)S(1)}, s32[2,128,128]{2,1,0:T(8,128)}, u32[]{:S(2)}) %copy-start.5) | copy-done | bytes 131096
  4.3 0.0 copy-start.6
  4.3 0.7 %copy-done.6 = f32[8]{0:T(128)S(1)} copy-done((f32[8]{0:T(128)S(1)}, f32[8]{0:T(128)}, u32[]{:S(2)}) %copy-start.6) | copy-done | bytes 56
  5.0 0.0 copy-start
  5.0 0.7 %pack.1 = (f32[4,128,128]{2,1,0:T(8,128)S(1)}, f32[8,128,128]{2,1,0:T(8,128)S(1)}, f32[3,2,128,128]{3,2,1,0:T(8,128)S(1)}, f32[2,128,128]{2,1,0:T(8,128)S(1)}, f32[2,128,128]{2,1,0:T(8,128)S(1)}) custom-call(f32[8]{0:T(128)S(1)} %copy-done.6, f32[1,3,2,128,128]{4,3,2,1,0:T(8,128)S(1)} %copy-done.3, f32[2,128,128]{2,1,0:T(8,128)S(1)} %copy-done.4, ...), custom_call_target="tpu_custom_call" | custom-call | tf_op jit(solution)/shard_map/pack/pallas_call | solution.py:309
  5.7 1.3 %collective-permute-start.1 = (f32[8,128,128]{2,1,0:T(8,128)S(1)}, f32[8,128,128]{2,1,0:T(8,128)S(1)}, u32[]{:S(2)}, u32[]{:S(2)}) collective-permute-start(f32[8,128,128]{2,1,0:T(8,128)S(1)} %get-tuple-element.13), channel_id=1, source_target_pairs={{2,0},{4,2},{6,4},{8,6},{10,8},{12,10},{14,12},{16,14},{18,16},{20... | collective-permute-start | bytes 1572872 | tf_op jit(solution)/shard_map/ppermute | solution.py:24
  7.0 0.0 copy-start.2
  7.0 5.6 %collective-permute-start = (f32[4,128,128]{2,1,0:T(8,128)S(1)}, f32[4,128,128]{2,1,0:T(8,128)S(1)}, u32[]{:S(2)}, u32[]{:S(2)}) collective-permute-start(f32[4,128,128]{2,1,0:T(8,128)S(1)} %get-tuple-element.12), channel_id=1, source_target_pairs={{0,2},{2,4},{4,6},{6,8},{8,10},{10,12},{12,14},{14,16},{16,18},{18... | collective-permute-start | bytes 786440 | tf_op jit(solution)/shard_map/ppermute | solution.py:24
  12.7 0.0 copy-done
  12.7 1.3 %collective-permute-start.2 = (f32[3,128,128]{2,1,0:T(8,128)S(1)}, f32[3,128,128]{2,1,0:T(8,128)S(1)}, u32[]{:S(2)}, u32[]{:S(2)}) collective-permute-start(f32[3,128,128]{2,1,0:T(8,128)S(1)} %slice_bitcast_fusion), channel_id=1, source_target_pairs={{2,0},{4,2},{6,4},{8,6},{10,8},{12,10},{14,12},{16,14},{18,16},{20... | collective-permute-start | bytes 589832 | tf_op jit(solution)/shard_map/ppermute | solution.py:24
  14.0 19.4 %collective-permute-done.up_ref = f32[4,128,128]{2,1,0:T(8,128)S(1)} collective-permute-done((f32[4,128,128]{2,1,0:T(8,128)S(1)}, f32[4,128,128]{2,1,0:T(8,128)S(1)}, u32[]{:S(2)}, u32[]{:S(2)}) %collective-permute-start) | collective-permute-done | bytes 262176 | tf_op jit(solution)/shard_map/ppermute | solution.py:24
  33.4 0.0 collective-permute-done.1.down_ref
  33.4 0.0 copy-done.2
  33.4 8.0 %image.1 = (f32[3,3,128,128]{3,2,1,0:T(8,128)S(1)}, f32[3,3,128,128]{3,2,1,0:T(8,128)S(1)}, f32[32,128]{1,0:T(8,128)}) custom-call(s32[2,128,128]{2,1,0:T(8,128)S(1)} %copy-done.2, f32[4,128,128]{2,1,0:T(8,128)S(1)} %collective-permute-done.up_ref, f32[8,128,128]{2,1,0:T(8,128)S(1)} %collective-permute-done.1.down_ref, ...), custom_call_target="tpu_custom_call" | custom-call | tf_op jit(solution)/shard_map/image/pallas_call | solution.py:327
  41.5 4.9 %all-to-all-start = ((f32[32,1,128]{2,1,0:T(1,128)}), f32[32,1,128]{2,1,0:T(1,128)S(1)}, u32[]{:S(2)}, u32[]{:S(2)}) async-start(f32[32,1,128]{2,1,0:T(1,128)} %bitcast.2), calls=%async_computation | async-start | bytes 32768 | tf_op jit(solution)/shard_map/all_to_all | solution.py:346
  46.3 0.1 pad_add_fusion.load_ref
  46.4 0.0 collective-permute-done.2.above_ref
  46.4 7.0 %all-to-all-done = f32[32,1,128]{2,1,0:T(1,128)S(1)} async-done(((f32[32,1,128]{2,1,0:T(1,128)}), f32[32,1,128]{2,1,0:T(1,128)S(1)}, u32[]{:S(2)}, u32[]{:S(2)}) %all-to-all-start) | async-done | bytes 16416 | tf_op jit(solution)/shard_map/all_to_all | solution.py:346
  53.4 3.9 %finish.1 = (f32[1,3,2,128,128]{4,3,2,1,0:T(8,128)}, f32[2,128,128]{2,1,0:T(8,128)S(1)}) custom-call(s32[2]{0:T(128)S(1)} %pad_add_fusion.load_ref, f32[32,128]{1,0:T(8,128)S(1)} %bitcast.9, f32[3,3,128,128]{3,2,1,0:T(8,128)S(1)} %get-tuple-element.17.z_ref, f32[3,3,128,128]{3,2,1,0:T(8,128)S(1)} %get-tuple-element.18.v_ref, ...), custom_call_target="tpu_custom_call" | custom-call | tf_op jit(solution)/shard_map/finish/pallas_call | solution.py:348
  57.3 0.0 collective-permute-start.3
  57.3 1.2 %collective-permute-done.3 = f32[2,64,128]{2,1,0:T(8,128)S(1)} collective-permute-done((f32[2,64,128]{2,1,0:T(8,128)S(1)}, f32[2,64,128]{2,1,0:T(8,128)S(1)}, u32[]{:S(2)}, u32[]{:S(2)}) %collective-permute-start.3) | collective-permute-done | bytes 65568 | tf_op jit(solution)/shard_map/ppermute | solution.py:24
  58.6 0.6 %dynamic-slice_add_fusion = f32[2,64,128]{2,1,0:T(8,128)} fusion(f32[2,64,128]{2,1,0:T(8,128)S(1)} %collective-permute-done.3, f32[2,128,128]{2,1,0:T(8,128)S(1)} %get-tuple-element.21, s32[]{:T(128)S(6)} %select_n.13), kind=kLoop, calls=%fused_computation.1 | loop fusion | flops 16384 | bytes 196612 | tf_op jit(solution)/shard_map/add | solution.py:364
  (2 shorter events, 0.0 us)
Async XLA Ops:
  0.6 0.9 %copy-start.1 = (s32[2,128,128]{2,1,0:T(8,128)S(1)}, s32[2,128,128]{2,1,0:T(8,128)}, u32[]{:S(2)}) copy-start(s32[2,128,128]{2,1,0:T(8,128)} %mask_ref.3) | copy-start | bytes 393220
  1.5 1.0 %copy-start.3 = (f32[1,3,2,128,128]{4,3,2,1,0:T(8,128)S(1)}, f32[1,3,2,128,128]{4,3,2,1,0:T(8,128)}, u32[]{:S(2)}) copy-start(f32[1,3,2,128,128]{4,3,2,1,0:T(8,128)} %rhs_ref.1) | copy-start | bytes 1179652
  2.5 0.9 %copy-start.4 = (f32[2,128,128]{2,1,0:T(8,128)S(1)}, f32[2,128,128]{2,1,0:T(8,128)}, u32[]{:S(2)}) copy-start(f32[2,128,128]{2,1,0:T(8,128)} %factor_ref.1) | copy-start | bytes 393220
  3.4 0.9 %copy-start.5 = (s32[2,128,128]{2,1,0:T(8,128)S(1)}, s32[2,128,128]{2,1,0:T(8,128)}, u32[]{:S(2)}) copy-start(s32[2,128,128]{2,1,0:T(8,128)} %ids_ref.1) | copy-start | bytes 393220
  4.3 0.7 %copy-start.6 = (f32[8]{0:T(128)S(1)}, f32[8]{0:T(128)}, u32[]{:S(2)}) copy-start(f32[8]{0:T(128)} %base_ref.1) | copy-start | bytes 100
  5.0 7.7 %copy-start = (f32[1,3,2,128,128]{4,3,2,1,0:T(8,128)S(1)}, f32[1,3,2,128,128]{4,3,2,1,0:T(8,128)}, u32[]{:S(2)}) copy-start(f32[1,3,2,128,128]{4,3,2,1,0:T(8,128)} %disp_ref.1) | copy-start | bytes 1179652
  5.7 27.7 %collective-permute-start.1 = (f32[8,128,128]{2,1,0:T(8,128)S(1)}, f32[8,128,128]{2,1,0:T(8,128)S(1)}, u32[]{:S(2)}, u32[]{:S(2)}) collective-permute-start(f32[8,128,128]{2,1,0:T(8,128)S(1)} %get-tuple-element.13), channel_id=1, source_target_pairs={{2,0},{4,2},{6,4},{8,6},{10,8},{12,10},{14,12},{16,14},{18,16},{20... | collective-permute-start | bytes 1572872 | tf_op jit(solution)/shard_map/ppermute | solution.py:24
  7.0 26.4 %copy-start.2 = (s32[2,128,128]{2,1,0:T(8,128)S(1)}, s32[2,128,128]{2,1,0:T(8,128)}, u32[]{:S(2)}) copy-start(s32[2,128,128]{2,1,0:T(8,128)} %mask_ref.3) | copy-start | bytes 393220
  7.0 26.4 %collective-permute-start = (f32[4,128,128]{2,1,0:T(8,128)S(1)}, f32[4,128,128]{2,1,0:T(8,128)S(1)}, u32[]{:S(2)}, u32[]{:S(2)}) collective-permute-start(f32[4,128,128]{2,1,0:T(8,128)S(1)} %get-tuple-element.12), channel_id=1, source_target_pairs={{0,2},{2,4},{4,6},{6,8},{8,10},{10,12},{12,14},{14,16},{16,18},{18... | collective-permute-start | bytes 786440 | tf_op jit(solution)/shard_map/ppermute | solution.py:24
  12.7 33.7 %collective-permute-start.2 = (f32[3,128,128]{2,1,0:T(8,128)S(1)}, f32[3,128,128]{2,1,0:T(8,128)S(1)}, u32[]{:S(2)}, u32[]{:S(2)}) collective-permute-start(f32[3,128,128]{2,1,0:T(8,128)S(1)} %slice_bitcast_fusion), channel_id=1, source_target_pairs={{2,0},{4,2},{6,4},{8,6},{10,8},{12,10},{14,12},{16,14},{18,16},{20... | collective-permute-start | bytes 589832 | tf_op jit(solution)/shard_map/ppermute | solution.py:24
  41.5 12.0 %all-to-all-start = ((f32[32,1,128]{2,1,0:T(1,128)}), f32[32,1,128]{2,1,0:T(1,128)S(1)}, u32[]{:S(2)}, u32[]{:S(2)}) async-start(f32[32,1,128]{2,1,0:T(1,128)} %bitcast.2), calls=%async_computation | async-start | bytes 32768 | tf_op jit(solution)/shard_map/all_to_all | solution.py:346
  57.3 1.3 %collective-permute-start.3 = (f32[2,64,128]{2,1,0:T(8,128)S(1)}, f32[2,64,128]{2,1,0:T(8,128)S(1)}, u32[]{:S(2)}, u32[]{:S(2)}) collective-permute-start(f32[2,64,128]{2,1,0:T(8,128)S(1)} %constant_dynamic-slice_fusion), channel_id=1, source_target_pairs={{0,1},{1,0},{2,3},{3,2},{4,5},{5,4},{6,7},{7,6},{8,9},{9,8},{10,11... | collective-permute-start | bytes 196616 | tf_op jit(solution)/shard_map/ppermute | solution.py:24

commit v2 on v1

v2 whole, which is shorter than its diff:
```python
import functools

import jax
import jax.numpy as jnp
from jax import lax
from jax.experimental import pallas as pl
from jax.experimental.pallas import tpu as pltpu
from jax.sharding import PartitionSpec as P

POISSON = 0.3
SHEAR = 0.5 / (1.0 + POISSON)
RATIO = 2.0 * POISSON / (1.0 - 2.0 * POISSON)
CLASS = [0.0] + [12.0 * SHEAR / 64.0 / 3.0**order for order in (1, 2, 3)]
CORNER = CLASS[1] * (RATIO + 4.0) + CLASS[2] * (2.0 * (RATIO + 3.0) + 2.0) + CLASS[3] * (RATIO + 4.0)
ROWS = 64


def permute(shard, axis, by, wrap=False):
    devices = lax.axis_size(axis)
    if wrap:
        pairs = [(i, (i + by) % devices) for i in range(devices)]
    else:
        pairs = [(i, i + by) for i in range(devices) if 0 <= i + by < devices]
    return lax.ppermute(shard, axis, pairs)


def next_lane(value):
    width = value.shape[-1]
    lane = lax.broadcasted_iota(jnp.int32, value.shape, value.ndim - 1)
    return jnp.where(lane == width - 1, 0.0, pltpu.roll(value, width - 1, value.ndim - 1))


def last_lane(value):
    lane = lax.broadcasted_iota(jnp.int32, value.shape, value.ndim - 1)
    return jnp.where(lane == 0, 0.0, pltpu.roll(value, 1, value.ndim - 1))


def plane_modes(ref, plane, start):
    out = []
    for comp in range(3):
        here = ref[plane, comp, pl.ds(start, ROWS), :]
        below = ref[plane, comp, pl.ds(start + 1, ROWS), :]
        level, change = here + below, below - here
        level_next, change_next = next_lane(level), next_lane(change)
        out.append(((level + level_next, change + change_next), (level_next - level, change_next - change)))
    return out


def layer_modes(low, high):
    out = []
    for comp in range(3):
        modes = {}
        for a in range(2):
            for b in range(2):
                if a or b:
                    modes[a, b, 0] = low[comp][a][b] + high[comp][a][b]
                modes[a, b, 1] = high[comp][a][b] - low[comp][a][b]
        out.append(modes)
    return out


PAIRS = (((0, (1, 1, 0)), (2, (0, 1, 1))), ((1, (1, 1, 0)), (2, (1, 0, 1))), ((0, (1, 0, 1)), (1, (0, 1, 1))))


def stiff(modes):
    u, v, w = modes
    out = [{}, {}, {}]
    trace = RATIO * (u[1, 0, 0] + v[0, 1, 0] + w[0, 0, 1])
    out[0][1, 0, 0] = trace + 2.0 * u[1, 0, 0]
    out[1][0, 1, 0] = trace + 2.0 * v[0, 1, 0]
    out[2][0, 0, 1] = trace + 2.0 * w[0, 0, 1]
    for (one, at), (two, by) in PAIRS:
        both = RATIO * (modes[one][at] + modes[two][by])
        out[one][at] = both + 3.0 * modes[one][at]
        out[two][by] = both + 3.0 * modes[two][by]
    out[0][0, 1, 0] = out[1][1, 0, 0] = u[0, 1, 0] + v[1, 0, 0]
    out[1][0, 0, 1] = out[2][0, 1, 0] = v[0, 0, 1] + w[0, 1, 0]
    out[2][1, 0, 0] = out[0][0, 0, 1] = w[1, 0, 0] + u[0, 0, 1]
    first = u[0, 1, 1] + v[1, 0, 1]
    second = v[1, 0, 1] + w[1, 1, 0]
    third = w[1, 1, 0] + u[0, 1, 1]
    out[0][0, 1, 1] = first + third
    out[1][1, 0, 1] = first + second
    out[2][1, 1, 0] = second + third
    for comp in range(3):
        out[comp][1, 1, 1] = (RATIO + 4.0) * modes[comp][1, 1, 1]
    return out


def paired(modes, forces):
    total = None
    for order in (1, 2, 3):
        part = None
        for comp in range(3):
            for key, force in forces[comp].items():
                if sum(key) == order:
                    term = modes[comp][key] * force
                    part = term if part is None else part + term
        part = CLASS[order] * part
        total = part if total is None else total + part
    return total


def pack_kernel(
    base_hbm, rhs_hbm, factor_hbm, ids_hbm, mask_hbm,
    up_ref, down_ref, res_ref, mod_ref, scale_ref, free_ref,
    base_ref, rhs_ref, factor_ref, ids_ref, mask_ref, sems,
):
    layers, height, width = factor_ref.shape
    pairs = (
        (base_hbm, base_ref),
        (ids_hbm, ids_ref),
        (factor_hbm, factor_ref),
        (mask_hbm, mask_ref),
        (rhs_hbm.at[0], rhs_ref),
    )
    copies = [pltpu.make_async_copy(source, target, sems.at[place]) for place, (source, target) in enumerate(pairs)]
    for copy in copies:
        copy.start()
    for copy in copies[:3]:
        copy.wait()
    ids = ids_ref[...]
    scale = jnp.full(ids.shape, base_ref[0])
    for zone in range(1, base_ref.shape[0]):
        scale = jnp.where(ids == zone, base_ref[zone], scale)
    modulus = factor_ref[...] * scale
    scale_ref[...] = scale
    mod_ref[...] = modulus
    copies[3].wait()
    free = 1.0 - mask_ref[...].astype(jnp.float32)
    free_ref[...] = free
    row = lax.broadcasted_iota(jnp.int32, (height, width), 0)

    def inverse(lower, upper, free):
        total = lower + upper
        total = total + last_lane(total)
        total = total + jnp.where(row == 0, 0.0, pltpu.roll(total, 1, 0))
        return free / (CORNER * total)

    top = inverse(modulus[layers - 2], modulus[layers - 1], free[layers - 1])
    second = top if layers == 2 else inverse(modulus[0], modulus[1], free[1])
    up_ref[3] = modulus[layers - 1]
    down_ref[6] = modulus[0]
    down_ref[7] = free[0]
    copies[4].wait()
    res = free[None] * rhs_ref[...]
    res_ref[...] = res
    up_ref[0:3] = res[:, layers - 1] * top
    down_ref[0:3] = res[:, 0]
    down_ref[3:6] = res[:, 1] * second


def image_kernel(free_ref, up_ref, down_ref, res_ref, mod_ref, z_ref, v_ref, sums_ref, carry, edge, inv):
    layers, height, width = mod_ref.shape
    blocks = height // ROWS

    def modulus(layer, rows):
        if layer < 0:
            return up_ref[3, rows, :]
        return mod_ref[layer, rows, :] if layer < layers else down_ref[6, rows, :]

    edge[:, 0:8, :] = jnp.zeros((layers + 1, 8, width), jnp.float32)
    carry[:, :, 0:8, :] = jnp.zeros((layers + 1, 3, 8, width), jnp.float32)
    z_ref[:, :, height : height + 8, :] = jnp.zeros((layers + 3, 3, 8, width), jnp.float32)
    v_ref[:, :, height : height + 8, :] = jnp.zeros((layers + 1, 3, 8, width), jnp.float32)

    def start_block(block, norm):
        start = pl.multiple_of(block * ROWS, ROWS)
        rows = pl.ds(start, ROWS)
        for plane in range(layers + 1):
            total = modulus(plane - 1, rows) + modulus(plane, rows)
            total = total + last_lane(total)
            edge[plane, pl.ds(start + 8, ROWS), :] = total
            total = total + edge[plane, pl.ds(start + 7, ROWS), :]
            free = down_ref[7, rows, :] if plane == layers else free_ref[plane, rows, :]
            inverse = free / (CORNER * total)
            inv[plane, rows, :] = inverse
            for comp in range(3):
                res = res_ref[comp, plane, rows, :] if plane < layers else down_ref[comp, rows, :]
                z = inverse * res
                z_ref[plane + 1, comp, rows, :] = z
                if plane < layers:
                    norm = norm + res * z
        for comp in range(3):
            z_ref[0, comp, rows, :] = up_ref[comp, rows, :]
            z_ref[layers + 2, comp, rows, :] = down_ref[3 + comp, rows, :]
        return norm

    zero = jnp.zeros((ROWS, width), jnp.float32)
    norm = lax.fori_loop(0, blocks, start_block, zero)

    def image_block(block, sums):
        along, across = sums
        start = pl.multiple_of(block * ROWS, ROWS)
        rows = pl.ds(start, ROWS)
        low = plane_modes(z_ref, 0, start)
        held = None
        for layer in range(layers + 2):
            high = plane_modes(z_ref, layer + 1, start)
            forces = stiff(layer_modes(low, high))
            stiffness = modulus(layer - 1, rows)
            weight = [None] + [CLASS[order] * stiffness for order in (1, 2, 3)]
            lower, upper = {}, {}
            for comp in range(3):
                for a in range(2):
                    for b in range(2):
                        change = weight[a + b + 1] * forces[comp][a, b, 1]
                        if a or b:
                            level = weight[a + b] * forces[comp][a, b, 0]
                            lower[comp, a, b] = level - change
                            upper[comp, a, b] = level + change
                        else:
                            lower[comp, a, b] = -change
                            upper[comp, a, b] = change
            if layer > 0:
                plane = layer - 1
                inverse = inv[plane, rows, :]
                for comp in range(3):
                    sides = []
                    for b in range(2):
                        level = held[comp, 0, b] + lower[comp, 0, b]
                        change = held[comp, 1, b] + lower[comp, 1, b]
                        sides.append(level - change + last_lane(level + change))
                    carry[plane, comp, pl.ds(start + 8, ROWS), :] = sides[0] + sides[1]
                    image = sides[0] - sides[1] + carry[plane, comp, pl.ds(start + 7, ROWS), :]
                    v = inverse * image
                    v_ref[plane, comp, rows, :] = v
                    if plane < layers:
                        along = along + image * z_ref[plane + 1, comp, rows, :]
                        across = across + image * v
            held = upper
            low = high
        return along, across

    along, across = lax.fori_loop(0, blocks, image_block, (zero, zero))

    def energy_block(block, energy):
        start = pl.multiple_of(block * ROWS, ROWS)
        low = plane_modes(v_ref, 0, start)
        for layer in range(layers):
            high = plane_modes(v_ref, layer + 1, start)
            modes = layer_modes(low, high)
            energy = energy + mod_ref[layer, pl.ds(start, ROWS), :] * paired(modes, stiff(modes))
            low = high
        return energy

    energy = lax.fori_loop(0, blocks, energy_block, zero)
    lane = lax.broadcasted_iota(jnp.int32, sums_ref.shape, 1)
    out = jnp.zeros(sums_ref.shape, jnp.float32)
    for place, part in enumerate((norm, along, across, energy)):
        out = jnp.where(lane == place, jnp.sum(part), out)
    sums_ref[...] = out


def term_kernel(load_ref, z_ref, v_ref, disp_ref, above_ref, scale_ref, term_ref, u_pad):
    layers, height, width = scale_ref.shape
    loads, share = term_ref.shape[0], term_ref.shape[3]
    u_pad[:, :, height : height + 8, :] = jnp.zeros((layers + 1, 3, 8, width), jnp.float32)
    for comp in range(3):
        for plane in range(layers + 1):
            u_pad[plane, comp, 0:height, :] = disp_ref[0, comp, plane] if plane < layers else above_ref[comp]

    def term_block(block, _):
        start = pl.multiple_of(block * ROWS, ROWS)
        rows = pl.ds(start, ROWS)
        place = lax.rem(start // share - load_ref[0] + loads, loads)
        target = pl.ds(pl.multiple_of(lax.rem(start, share), ROWS), ROWS)
        z_low = plane_modes(z_ref, 1, start)
        v_low = plane_modes(v_ref, 0, start)
        u_low = plane_modes(u_pad, 0, start)
        for layer in range(layers):
            z_high = plane_modes(z_ref, layer + 2, start)
            v_high = plane_modes(v_ref, layer + 1, start)
            u_high = plane_modes(u_pad, layer + 1, start)
            forces = stiff(layer_modes(u_low, u_high))
            scale = scale_ref[layer, rows, :]
            term_ref[place, 0, layer, target, :] = scale * paired(layer_modes(z_low, z_high), forces)
            term_ref[place, 1, layer, target, :] = scale * paired(layer_modes(v_low, v_high), forces)
            z_low, v_low, u_low = z_high, v_high, u_high
        return 0

    lax.fori_loop(0, height // ROWS, term_block, 0)


def finish_kernel(load_ref, sums_ref, z_ref, v_ref, *refs):
    x_ref, grad_ref = refs[-2:]
    term_refs = refs[:-2]
    loads, layers, height = len(term_refs), x_ref.shape[2], x_ref.shape[3]
    load = load_ref[0]
    device = lax.broadcasted_iota(jnp.int32, sums_ref.shape, 0)
    lane = lax.broadcasted_iota(jnp.int32, sums_ref.shape, 1)

    def weights(load):
        mine = jnp.where(lax.rem(device, loads) == load, sums_ref[...], 0.0)
        mine = jnp.sum(mine, axis=0, keepdims=True)
        norm, along, across, energy = [
            jnp.sum(jnp.where(lane[:1] == place, mine, 0.0), axis=1, keepdims=True) for place in range(4)
        ]
        first = norm / along
        later = first * first * across - norm
        second = later / (first * first * (energy - across * across / along))
        return first + second * (first * across / along), second * first

    for place in range(loads):
        from_z, from_v = weights(lax.rem(load - place + loads, loads))
        part = from_z * term_refs[place][0] - from_v * term_refs[place][1]
        total = part if place == 0 else total + part
        if place == 0:
            for comp in range(3):
                for plane in range(layers):
                    x_ref[0, comp, plane] = from_z * z_ref[plane + 1, comp, 0:height] - from_v * v_ref[plane, comp, 0:height]
    grad_ref[...] = total


def f32(*shape):
    return jax.ShapeDtypeStruct(shape, jnp.float32)


def shards(forward_disp, adjoint_rhs, modulus_factor, zone_base, zone_ids, fixed_mask):
    layers, height, width = modulus_factor.shape
    loads = lax.axis_size("load")
    devices = lax.axis_size("space") * loads
    load = lax.axis_index("load")
    whole = pl.BlockSpec(memory_space=pltpu.VMEM)
    scalar = pl.BlockSpec(memory_space=pltpu.SMEM)
    params = pltpu.CompilerParams(vmem_limit_bytes=12 * 2**20)
    pad = height + 8
    share = height // loads
    position = load.astype(jnp.int32)[None]

    up, down, res, modulus, scale, free = pl.pallas_call(
        pack_kernel,
        out_shape=(
            f32(4, height, width),
            f32(8, height, width),
            f32(3, layers, height, width),
            f32(layers, height, width),
            f32(layers, height, width),
            f32(layers, height, width),
        ),
        in_specs=[pl.BlockSpec(memory_space=pltpu.HBM)] * 5,
        out_specs=[whole] * 6,
        scratch_shapes=[
            pltpu.SMEM(zone_base.shape, jnp.float32),
            pltpu.VMEM((3, layers, height, width), jnp.float32),
            pltpu.VMEM((layers, height, width), jnp.float32),
            pltpu.VMEM((layers, height, width), jnp.int32),
            pltpu.VMEM((layers, height, width), jnp.int32),
            pltpu.SemaphoreType.DMA((5,)),
        ],
        compiler_params=pltpu.CompilerParams(vmem_limit_bytes=12 * 2**20),
        name="pack",
    )(*[pltpu.with_memory_space_constraint(part, pltpu.HBM) for part in (zone_base, adjoint_rhs, modulus_factor, zone_ids, fixed_mask)])
    from_below = permute(up, "space", 1)
    from_above = permute(down, "space", -1)
    lowest = forward_disp[0, :, 0]
    from_above, lowest = lax.optimization_barrier((from_above, lowest))
    above_disp = permute(lowest, "space", -1)
    z, v, sums = pl.pallas_call(
        image_kernel,
        out_shape=(
            f32(layers + 3, 3, pad, width),
            f32(layers + 1, 3, pad, width),
            f32(devices, 128),
        ),
        in_specs=[whole] * 5,
        out_specs=[whole] * 3,
        scratch_shapes=[
            pltpu.VMEM((layers + 1, 3, pad, width), jnp.float32),
            pltpu.VMEM((layers + 1, pad, width), jnp.float32),
            pltpu.VMEM((layers + 1, height, width), jnp.float32),
        ],
        compiler_params=params,
        name="image",
    )(free, from_below, from_above, res, modulus)
    sums = lax.all_to_all(sums, ("space", "load"), 0, 0, tiled=True)

    terms = pl.pallas_call(
        term_kernel,
        out_shape=f32(loads, 2, layers, share, width),
        in_specs=[scalar] + [whole] * 5,
        out_specs=whole,
        scratch_shapes=[pltpu.VMEM((layers + 1, 3, pad, width), jnp.float32)],
        compiler_params=params,
        cost_estimate=pl.CostEstimate(flops=4 * 10**9, bytes_accessed=8 * 2**20, transcendentals=0),
        name="term",
    )(position, z, v, forward_disp, above_disp, scale)
    sums, terms = lax.optimization_barrier((sums, terms))
    terms = [terms[0]] + [permute(terms[by], "load", by, wrap=True) for by in range(1, loads)]

    return pl.pallas_call(
        finish_kernel,
        out_shape=(f32(1, 3, layers, height, width), f32(layers, share, width)),
        in_specs=[scalar] + [whole] * (3 + loads),
        out_specs=[whole] * 2,
        compiler_params=params,
        name="finish",
    )(position, sums, z, v, *terms)


def solution(mesh):
    placed = (
        P("load", None, "space", None, None),
        P("load", None, "space", None, None),
        P("space", None, None),
        P(),
        P("space", None, None),
        P("space", None, None),
    )
    return jax.shard_map(
        shards,
        mesh=mesh,
        in_specs=placed,
        out_specs=(P("load", None, "space", None, None), P("space", "load", None)),
        check_vma=False,
    )
```

time: 59.5 us -> 47.3 us (0.79)
  waiting for transfers between devices: 27.7 us -> 19.4 us
  Pallas kernels: 12.7 us -> 9.17 us
  starting transfers between devices: 13.1 us -> 16.1 us
  local copies, waits for them, and re-layouts: 4.39 us -> 1.61 us
  other arithmetic: 0.71 us -> 0 us
    ppermute x4, waiting for transfers between devices: 20.7 us -> 16.1 us  [permute(): return lax.ppermute(shard, axis, pairs)]
    all_to_all x1, waiting for transfers between devices: 6.99 us -> 3.27 us  [shards(): sums = lax.all_to_all(sums, ('space', 'load'), 0, 0, tiled=True)]
    unnamed x14 -> x6, local copies, waits for them, and re-layouts: 4.37 us -> 0.91 us
    all_to_all x1, starting transfers between devices: 4.87 us -> 8.02 us  [shards(): sums = lax.all_to_all(sums, ('space', 'load'), 0, 0, tiled=True)]
    pallas_call x1, Pallas kernels: 3.92 us -> 0.92 us  [shards(): pl.pallas_call(finish_kernel, out_shape=(f32(1, 3, layers, height, width)...]
    pallas_call x1 -> x2, Pallas kernels: 8.04 us -> 6.91 us  [the longest x1 4.02 us: shards(): pl.pallas_call(image_kernel, out_shape=(f32(layers + 3, 3, pad, width), f...]
    squeeze x1 -> x2, local copies, waits for them, and re-layouts: 0.01 us -> 0.71 us  [the longest x1 0.69 us: shards(): lowest = forward_disp[0, :, 0]]
    pallas_call x1, Pallas kernels: 0.7 us -> 1.35 us  [shards(): pl.pallas_call(pack_kernel, out_shape=(f32(4, height, width), f32(8, heig...]
  transfers between devices with their start and end apart: 5 -> 5, of which waited for: 3 -> 4; matrix products, arithmetic and copies ran while one was open for 0% -> 1% of each run, Pallas kernels for 14% -> 15%
where the time goes in v2:
time: 47.3 us; the launch traced here: 47.1 us
  waiting for transfers between devices  19.4 us (41%)
  starting transfers between devices  16.1 us (34%)
  Pallas kernels  9.17 us (19%)
  local copies, waits for them, and re-layouts  1.61 us (3%)
  between operations  0.74 us (2%)
    ppermute x4, waiting for transfers between devices, permute(): return lax.ppermute(shard, axis, pairs)  16.1 us
    ppermute x4, starting transfers between devices, permute(): return lax.ppermute(shard, axis, pairs)  8.13 us
    all_to_all x1, starting transfers between devices, shards(): sums = lax.all_to_all(sums, ('space', 'load'), 0, 0, tiled=True)  8.02 us
    pallas_call x1, Pallas kernels, shards(): pl.pallas_call(image_kernel, out_shape=(f32(layers + 3, 3, pad, width), f...  4.02 us
    all_to_all x1, waiting for transfers between devices, shards(): sums = lax.all_to_all(sums, ('space', 'load'), 0, 0, tiled=True)  3.27 us
    pallas_call x1, Pallas kernels, shards(): pl.pallas_call(term_kernel, out_shape=f32(loads, 2, layers, share, width)...  2.89 us
    pallas_call x1, Pallas kernels, shards(): pl.pallas_call(pack_kernel, out_shape=(f32(4, height, width), f32(8, heig...  1.35 us
  transfers between devices with their start and end apart: 5, of which 4 were waited for; matrix products, arithmetic and copies ran while one was open for 1% of the time, Pallas kernels for 15%

profile of v2, /device:TPU:0, one launch (start us, length us, event | category | flops | bytes accessed | tf_op | source)
XLA Modules:
  0.0 47.1 jit_solution(6340140223706052013)
XLA Ops:
  0.6 0.0 copy-start
  0.6 1.3 %pack.1 = (f32[4,128,128]{2,1,0:T(8,128)S(1)}, f32[8,128,128]{2,1,0:T(8,128)S(1)}, f32[3,2,128,128]{3,2,1,0:T(8,128)S(1)}, f32[2,128,128]{2,1,0:T(8,128)S(1)}, f...) custom-call(f32[8]{0:T(128)} %base_hbm.1, f32[1,3,2,128,128]{4,3,2,1,0:T(8,128)} %rhs_hbm.1, ...), custom_call_target="tpu_custom_call" | custom-call | tf_op jit(solution)/shard_map/pack/pallas_call | solution.py:331
  2.0 0.0 copy-start.1
  2.0 1.3 %collective-permute-start.1 = (f32[8,128,128]{2,1,0:T(8,128)S(1)}, f32[8,128,128]{2,1,0:T(8,128)S(1)}, u32[]{:S(2)}, u32[]{:S(2)}) collective-permute-start(f32[8,128,128]{2,1,0:T(8,128)S(1)} %get-tuple-element.17), channel_id=1, source_target_pairs={{2,0},{4,2},{6,4},{8,6},{10,8},{12,10},{14,12},{16,14},{18,16},{20... | collective-permute-start | bytes 1572872 | tf_op jit(solution)/shard_map/ppermute | solution.py:24
  3.3 5.5 %collective-permute-start = (f32[4,128,128]{2,1,0:T(8,128)S(1)}, f32[4,128,128]{2,1,0:T(8,128)S(1)}, u32[]{:S(2)}, u32[]{:S(2)}) collective-permute-start(f32[4,128,128]{2,1,0:T(8,128)S(1)} %get-tuple-element.16), channel_id=1, source_target_pairs={{0,2},{2,4},{4,6},{6,8},{8,10},{10,12},{12,14},{14,16},{16,18},{18... | collective-permute-start | bytes 786440 | tf_op jit(solution)/shard_map/ppermute | solution.py:24
  8.8 0.0 copy-done
  8.8 0.7 %slice_bitcast_fusion = f32[3,128,128]{2,1,0:T(8,128)} fusion(f32[1,3,2,128,128]{4,3,2,1,0:T(8,128)S(1)} %copy-done), kind=kLoop, calls=%fused_computation | loop fusion | bytes 393216 | tf_op jit(solution)/shard_map/squeeze | solution.py:356
  9.5 0.0 copy-done.1
  9.5 10.1 %collective-permute-done.1.down_ref = f32[8,128,128]{2,1,0:T(8,128)S(1)} collective-permute-done((f32[8,128,128]{2,1,0:T(8,128)S(1)}, f32[8,128,128]{2,1,0:T(8,128)S(1)}, u32[]{:S(2)}, u32[]{:S(2)}) %collective-permute-start.1) | collective-permute-done | bytes 524320 | tf_op jit(solution)/shard_map/ppermute | solution.py:24
  19.6 1.3 %collective-permute-start.2 = (f32[3,128,128]{2,1,0:T(8,128)}, f32[3,128,128]{2,1,0:T(8,128)}, u32[]{:S(2)}, u32[]{:S(2)}) collective-permute-start(f32[3,128,128]{2,1,0:T(8,128)} %slice_bitcast_fusion), channel_id=1, source_target_pairs={{2,0},{4,2},{6,4},{8,6},{10,8},{12,10},{14,12},{16,14},{18,16},{20... | collective-permute-start | bytes 589832 | tf_op jit(solution)/shard_map/ppermute | solution.py:24
  20.9 4.7 %collective-permute-done.up_ref = f32[4,128,128]{2,1,0:T(8,128)S(1)} collective-permute-done((f32[4,128,128]{2,1,0:T(8,128)S(1)}, f32[4,128,128]{2,1,0:T(8,128)S(1)}, u32[]{:S(2)}, u32[]{:S(2)}) %collective-permute-start) | collective-permute-done | bytes 262176 | tf_op jit(solution)/shard_map/ppermute | solution.py:24
  25.6 4.0 %image.1 = (f32[5,3,136,128]{3,2,1,0:T(8,128)S(1)}, f32[3,3,136,128]{3,2,1,0:T(8,128)S(1)}, f32[32,128]{1,0:T(8,128)}) custom-call(f32[2,128,128]{2,1,0:T(8,128)S(1)} %get-tuple-element.15.free_ref, f32[4,128,128]{2,1,0:T(8,128)S(1)} %collective-permute-done.up_ref, f32[8,128,128]{2,1,0:T(8,128)S(1)} %collective-permute-done.1.down_ref, ...), custom_call_target="tpu_custom_call" | custom-call | tf_op jit(solution)/shard_map/image/pallas_call | solution.py:359
  29.6 8.0 %all-to-all-start = ((f32[32,1,128]{2,1,0:T(1,128)}), f32[32,1,128]{2,1,0:T(1,128)S(1)}, u32[]{:S(2)}, u32[]{:S(2)}) async-start(f32[32,1,128]{2,1,0:T(1,128)} %bitcast.3), calls=%async_computation | async-start | bytes 32768 | tf_op jit(solution)/shard_map/all_to_all | solution.py:376
  37.6 0.0 collective-permute-done.2.above_ref
  37.6 0.0 copy-start.2
  37.6 0.9 %copy-done.2 = f32[2,128,128]{2,1,0:T(8,128)S(1)} copy-done((f32[2,128,128]{2,1,0:T(8,128)S(1)}, f32[2,128,128]{2,1,0:T(8,128)}, u32[]{:S(2)}) %copy-start.2) | copy-done | bytes 131096
  38.5 2.9 %term.1 = f32[2,2,2,64,128]{4,3,2,1,0:T(8,128)S(1)} custom-call(s32[1]{0:T(128)} %bitcast.load_ref, f32[5,3,136,128]{3,2,1,0:T(8,128)S(1)} %get-tuple-element.22.z_ref, f32[3,3,136,128]{3,2,1,0:T(8,128)S(1)} %get-tuple-element.23.v_ref, f32[1,3,2,128,128]{4,3,2,1,0:T(8,128)S(1)} %copy-done, f32[3,128,128]{2,1,0:T(8,128)} %collective-permute-done.2.above_ref, ...), custom_call_target="tpu_custom_call" | custom-call | flops 4000000000 | bytes 8388608 | tf_op jit(solution)/shard_map/term/pallas_call | solution.py:378
  41.4 3.3 %all-to-all-done = f32[32,1,128]{2,1,0:T(1,128)S(1)} async-done(((f32[32,1,128]{2,1,0:T(1,128)}), f32[32,1,128]{2,1,0:T(1,128)S(1)}, u32[]{:S(2)}, u32[]{:S(2)}) %all-to-all-start) | async-done | bytes 16416 | tf_op jit(solution)/shard_map/all_to_all | solution.py:376
  44.7 0.1 collective-permute-start.3
  44.8 1.3 %collective-permute-done.3.refs_1_ = f32[2,2,64,128]{3,2,1,0:T(8,128)S(1)} collective-permute-done((f32[2,2,64,128]{3,2,1,0:T(8,128)S(1)}, f32[2,2,64,128]{3,2,1,0:T(8,128)S(1)}, u32[]{:S(2)}, u32[]{:S(2)}) %collective-permute-start.3) | collective-permute-done | bytes 131104 | tf_op jit(solution)/shard_map/ppermute | solution.py:24
  46.1 0.9 %finish.1 = (f32[1,3,2,128,128]{4,3,2,1,0:T(8,128)}, f32[2,64,128]{2,1,0:T(8,128)}) custom-call(s32[1]{0:T(128)} %bitcast.load_ref, f32[32,128]{1,0:T(8,128)S(1)} %bitcast.13, f32[5,3,136,128]{3,2,1,0:T(8,128)S(1)} %get-tuple-element.22.z_ref, f32[3,3,136,128]{3,2,1,0:T(8,128)S(1)} %get-tuple-element.23.v_ref, ...), custom_call_target="tpu_custom_call" | custom-call | tf_op jit(solution)/shard_map/finish/pallas_call | solution.py:391
  (1 shorter events, 0.0 us)
Async XLA Ops:
  0.6 8.2 %copy-start = (f32[1,3,2,128,128]{4,3,2,1,0:T(8,128)S(1)}, f32[1,3,2,128,128]{4,3,2,1,0:T(8,128)}, u32[]{:S(2)}) copy-start(f32[1,3,2,128,128]{4,3,2,1,0:T(8,128)} %disp_ref.1) | copy-start | bytes 1179652
  2.0 7.5 %copy-start.1 = (f32[2,128,128]{2,1,0:T(8,128)}, f32[2,128,128]{2,1,0:T(8,128)S(1)}, u32[]{:S(2)}) copy-start(f32[2,128,128]{2,1,0:T(8,128)S(1)} %get-tuple-element.25.scale_ref) | copy-start | bytes 393220
  2.0 17.6 %collective-permute-start.1 = (f32[8,128,128]{2,1,0:T(8,128)S(1)}, f32[8,128,128]{2,1,0:T(8,128)S(1)}, u32[]{:S(2)}, u32[]{:S(2)}) collective-permute-start(f32[8,128,128]{2,1,0:T(8,128)S(1)} %get-tuple-element.17), channel_id=1, source_target_pairs={{2,0},{4,2},{6,4},{8,6},{10,8},{12,10},{14,12},{16,14},{18,16},{20... | collective-permute-start | bytes 1572872 | tf_op jit(solution)/shard_map/ppermute | solution.py:24
  3.3 22.3 %collective-permute-start = (f32[4,128,128]{2,1,0:T(8,128)S(1)}, f32[4,128,128]{2,1,0:T(8,128)S(1)}, u32[]{:S(2)}, u32[]{:S(2)}) collective-permute-start(f32[4,128,128]{2,1,0:T(8,128)S(1)} %get-tuple-element.16), channel_id=1, source_target_pairs={{0,2},{2,4},{4,6},{6,8},{8,10},{10,12},{12,14},{14,16},{16,18},{18... | collective-permute-start | bytes 786440 | tf_op jit(solution)/shard_map/ppermute | solution.py:24
  19.6 18.0 %collective-permute-start.2 = (f32[3,128,128]{2,1,0:T(8,128)}, f32[3,128,128]{2,1,0:T(8,128)}, u32[]{:S(2)}, u32[]{:S(2)}) collective-permute-start(f32[3,128,128]{2,1,0:T(8,128)} %slice_bitcast_fusion), channel_id=1, source_target_pairs={{2,0},{4,2},{6,4},{8,6},{10,8},{12,10},{14,12},{16,14},{18,16},{20... | collective-permute-start | bytes 589832 | tf_op jit(solution)/shard_map/ppermute | solution.py:24
  29.6 15.1 %all-to-all-start = ((f32[32,1,128]{2,1,0:T(1,128)}), f32[32,1,128]{2,1,0:T(1,128)S(1)}, u32[]{:S(2)}, u32[]{:S(2)}) async-start(f32[32,1,128]{2,1,0:T(1,128)} %bitcast.3), calls=%async_computation | async-start | bytes 32768 | tf_op jit(solution)/shard_map/all_to_all | solution.py:376
  37.6 0.9 %copy-start.2 = (f32[2,128,128]{2,1,0:T(8,128)S(1)}, f32[2,128,128]{2,1,0:T(8,128)}, u32[]{:S(2)}) copy-start(f32[2,128,128]{2,1,0:T(8,128)} %copy-done.1) | copy-start | bytes 393220
  44.7 1.4 %collective-permute-start.3 = (f32[2,2,64,128]{3,2,1,0:T(8,128)S(1)}, f32[2,2,64,128]{3,2,1,0:T(8,128)S(1)}, u32[]{:S(2)}, u32[]{:S(2)}) collective-permute-start(f32[2,2,64,128]{3,2,1,0:T(8,128)S(1)} %get-tuple-element.28), channel_id=1, source_target_pairs={{0,1},{1,0},{2,3},{3,2},{4,5},{5,4},{6,7},{7,6},{8,9},{9,8},{10,11... | collective-permute-start | bytes 393224 | tf_op jit(solution)/shard_map/ppermute | solution.py:24

commit v3 on v2

v3 whole, which is shorter than its diff:
```python
import functools

import jax
import jax.numpy as jnp
from jax import lax
from jax.experimental import pallas as pl
from jax.experimental.pallas import tpu as pltpu
from jax.sharding import PartitionSpec as P

POISSON = 0.3
SHEAR = 0.5 / (1.0 + POISSON)
RATIO = 2.0 * POISSON / (1.0 - 2.0 * POISSON)
CLASS = [0.0] + [12.0 * SHEAR / 64.0 / 3.0**order for order in (1, 2, 3)]
CORNER = CLASS[1] * (RATIO + 4.0) + CLASS[2] * (2.0 * (RATIO + 3.0) + 2.0) + CLASS[3] * (RATIO + 4.0)
ROWS = 64


def permute(shard, axis, by, wrap=False):
    devices = lax.axis_size(axis)
    if wrap:
        pairs = [(i, (i + by) % devices) for i in range(devices)]
    else:
        pairs = [(i, i + by) for i in range(devices) if 0 <= i + by < devices]
    return lax.ppermute(shard, axis, pairs)


def next_lane(value):
    width = value.shape[-1]
    lane = lax.broadcasted_iota(jnp.int32, value.shape, value.ndim - 1)
    return jnp.where(lane == width - 1, 0.0, pltpu.roll(value, width - 1, value.ndim - 1))


def last_lane(value):
    lane = lax.broadcasted_iota(jnp.int32, value.shape, value.ndim - 1)
    return jnp.where(lane == 0, 0.0, pltpu.roll(value, 1, value.ndim - 1))


def plane_modes(ref, at, start, count):
    out = []
    for comp in range(3):
        here = ref[at + (comp, pl.ds(start, count))]
        below = ref[at + (comp, pl.ds(start + 1, count))]
        level, change = here + below, below - here
        level_next, change_next = next_lane(level), next_lane(change)
        out.append(((level + level_next, change + change_next), (level_next - level, change_next - change)))
    return out


def layer_modes(low, high):
    out = []
    for comp in range(3):
        modes = {}
        for a in range(2):
            for b in range(2):
                if a or b:
                    modes[a, b, 0] = low[comp][a][b] + high[comp][a][b]
                modes[a, b, 1] = high[comp][a][b] - low[comp][a][b]
        out.append(modes)
    return out


PAIRS = (((0, (1, 1, 0)), (2, (0, 1, 1))), ((1, (1, 1, 0)), (2, (1, 0, 1))), ((0, (1, 0, 1)), (1, (0, 1, 1))))


def stiff(modes):
    u, v, w = modes
    out = [{}, {}, {}]
    trace = RATIO * (u[1, 0, 0] + v[0, 1, 0] + w[0, 0, 1])
    out[0][1, 0, 0] = trace + 2.0 * u[1, 0, 0]
    out[1][0, 1, 0] = trace + 2.0 * v[0, 1, 0]
    out[2][0, 0, 1] = trace + 2.0 * w[0, 0, 1]
    for (one, at), (two, by) in PAIRS:
        both = RATIO * (modes[one][at] + modes[two][by])
        out[one][at] = both + 3.0 * modes[one][at]
        out[two][by] = both + 3.0 * modes[two][by]
    out[0][0, 1, 0] = out[1][1, 0, 0] = u[0, 1, 0] + v[1, 0, 0]
    out[1][0, 0, 1] = out[2][0, 1, 0] = v[0, 0, 1] + w[0, 1, 0]
    out[2][1, 0, 0] = out[0][0, 0, 1] = w[1, 0, 0] + u[0, 0, 1]
    first = u[0, 1, 1] + v[1, 0, 1]
    second = v[1, 0, 1] + w[1, 1, 0]
    third = w[1, 1, 0] + u[0, 1, 1]
    out[0][0, 1, 1] = first + third
    out[1][1, 0, 1] = first + second
    out[2][1, 1, 0] = second + third
    for comp in range(3):
        out[comp][1, 1, 1] = (RATIO + 4.0) * modes[comp][1, 1, 1]
    return out


def paired(modes, forces):
    total = None
    for order in (1, 2, 3):
        part = None
        for comp in range(3):
            for key, force in forces[comp].items():
                if sum(key) == order:
                    term = modes[comp][key] * force
                    part = term if part is None else part + term
        part = CLASS[order] * part
        total = part if total is None else total + part
    return total


def layer_forces(low, high, stiffness):
    forces = stiff(layer_modes(low, high))
    weight = [None] + [CLASS[order] * stiffness for order in (1, 2, 3)]
    lower, upper = {}, {}
    for comp in range(3):
        for a in range(2):
            for b in range(2):
                change = weight[a + b + 1] * forces[comp][a, b, 1]
                if a or b:
                    level = weight[a + b] * forces[comp][a, b, 0]
                    lower[comp, a, b] = level - change
                    upper[comp, a, b] = level + change
                else:
                    lower[comp, a, b] = -change
                    upper[comp, a, b] = change
    return lower, upper


def nodal(forces, comp, carry, start, count):
    sides = []
    for b in range(2):
        level, change = forces[comp, 0, b], forces[comp, 1, b]
        sides.append(level - change + last_lane(level + change))
    carry[comp, pl.ds(start + 8, count), :] = sides[0] + sides[1]
    return sides[0] - sides[1] + carry[comp, pl.ds(start + 7, count), :]


def add_up(parts):
    row = lax.broadcasted_iota(jnp.int32, (8, parts[0].shape[-1]), 0)
    out = jnp.zeros(row.shape, jnp.float32)
    for place, part in enumerate(parts):
        out = jnp.where(row == place, jnp.sum(part, axis=0, keepdims=True), out)
    return out


def inverse_diagonal(free, total, edge, start, count):
    total = total + last_lane(total)
    edge[pl.ds(start + 8, count), :] = total
    return free / (CORNER * (total + edge[pl.ds(start + 7, count), :]))


def pack_kernel(
    base_hbm, rhs_hbm, factor_hbm, ids_hbm, mask_hbm,
    up_ref, res_ref, mod_ref, scale_ref, free_ref,
    base_ref, rhs_ref, factor_ref, ids_ref, mask_ref, sems,
):
    layers, height, width = factor_ref.shape
    pairs = (
        (base_hbm, base_ref),
        (ids_hbm, ids_ref),
        (factor_hbm, factor_ref),
        (mask_hbm, mask_ref),
        (rhs_hbm.at[0], rhs_ref),
    )
    copies = [pltpu.make_async_copy(source, target, sems.at[place]) for place, (source, target) in enumerate(pairs)]
    for copy in copies:
        copy.start()
    for copy in copies[:3]:
        copy.wait()
    ids = ids_ref[...]
    scale = jnp.full(ids.shape, base_ref[0])
    for zone in range(1, base_ref.shape[0]):
        scale = jnp.where(ids == zone, base_ref[zone], scale)
    modulus = factor_ref[...] * scale
    scale_ref[...] = scale
    mod_ref[...] = modulus
    copies[3].wait()
    free = 1.0 - mask_ref[...].astype(jnp.float32)
    free_ref[...] = free
    row = lax.broadcasted_iota(jnp.int32, (height, width), 0)

    def inverse(lower, upper, free):
        total = lower + upper
        total = total + last_lane(total)
        total = total + jnp.where(row == 0, 0.0, pltpu.roll(total, 1, 0))
        return free / (CORNER * total)

    top = inverse(modulus[layers - 2], modulus[layers - 1], free[layers - 1])
    up_ref[3] = modulus[layers - 1]
    copies[4].wait()
    res = free[None] * rhs_ref[...]
    res_ref[...] = res
    up_ref[0:3] = res[:, layers - 1] * top


def down_kernel(rhs_hbm, disp_hbm, mod_ref, free_ref, down_ref, low_ref, edge, sems):
    copies = [
        pltpu.make_async_copy(rhs_hbm.at[0, :, 0], down_ref.at[0:3], sems.at[0]),
        pltpu.make_async_copy(rhs_hbm.at[0, :, 1], down_ref.at[3:6], sems.at[1]),
        pltpu.make_async_copy(disp_hbm.at[0, :, 0], low_ref, sems.at[2]),
    ]
    for copy in copies:
        copy.start()
    height = mod_ref.shape[1]
    down_ref[6] = mod_ref[0]
    down_ref[7] = free_ref[0]
    edge[0:8, :] = jnp.zeros((8, edge.shape[1]), jnp.float32)
    inverse = inverse_diagonal(free_ref[1], mod_ref[0] + mod_ref[1], edge, 0, height)
    for copy in copies:
        copy.wait()
    down_ref[3:6] = down_ref[3:6] * inverse


def below_kernel(up_ref, res_ref, mod_ref, free_ref, z_ref, v_ref, part_ref, inv_ref, sums_ref, under, carry, edge):
    layers, height, width = mod_ref.shape
    count = min(ROWS, height)
    edge[:, 0:8, :] = jnp.zeros((layers, 8, width), jnp.float32)
    carry[:, :, 0:8, :] = jnp.zeros((layers, 3, 8, width), jnp.float32)
    under[:, height : height + 8, :] = jnp.zeros((3, 8, width), jnp.float32)
    z_ref[:, :, height : height + 8, :] = jnp.zeros((layers, 3, 8, width), jnp.float32)
    v_ref[:, :, height : height + 8, :] = jnp.zeros((layers - 1, 3, 8, width), jnp.float32)
    zero = jnp.zeros((count, width), jnp.float32)

    def modulus(layer, rows):
        return mod_ref[layer, rows, :] if layer >= 0 else up_ref[3, rows, :]

    def start_block(block, norm):
        start = pl.multiple_of(block * count, count)
        rows = pl.ds(start, count)
        for plane in range(layers):
            total = modulus(plane - 1, rows) + modulus(plane, rows)
            inverse = inverse_diagonal(free_ref[plane, rows, :], total, edge.at[plane], start, count)
            inv_ref[plane, rows, :] = inverse
            for comp in range(3):
                res = res_ref[comp, plane, rows, :]
                z = inverse * res
                z_ref[plane, comp, rows, :] = z
                norm = norm + res * z
        for comp in range(3):
            under[comp, rows, :] = up_ref[comp, rows, :]
        return norm

    norm = lax.fori_loop(0, height // count, start_block, zero)

    def image_block(block, sums):
        along, across = sums
        start = pl.multiple_of(block * count, count)
        rows = pl.ds(start, count)
        low = plane_modes(under, (), start, count)
        held = None
        for layer in range(layers):
            high = plane_modes(z_ref, (layer,), start, count)
            lower, upper = layer_forces(low, high, modulus(layer - 1, rows))
            if layer > 0:
                plane = layer - 1
                lower = {key: lower[key] + held[key] for key in lower}
                for comp in range(3):
                    image = nodal(lower, comp, carry.at[plane], start, count)
                    v = inv_ref[plane, rows, :] * image
                    v_ref[plane, comp, rows, :] = v
                    along = along + image * z_ref[plane, comp, rows, :]
                    across = across + image * v
            held, low = upper, high
        for comp in range(3):
            part_ref[comp, rows, :] = nodal(held, comp, carry.at[layers - 1], start, count)
        return along, across

    along, across = lax.fori_loop(0, height // count, image_block, (zero, zero))
    sums_ref[...] = add_up((norm, along, across))


def above_kernel(
    down_ref, z_ref, low_v_ref, part_ref, inv_ref, mod_ref, low_sums_ref,
    top_ref, v_ref, sums_ref, over, carry, edge, inv,
):
    layers, height, width = mod_ref.shape
    count = min(ROWS, height)
    edge[0:8, :] = jnp.zeros((8, width), jnp.float32)
    carry[:, :, 0:8, :] = jnp.zeros((2, 3, 8, width), jnp.float32)
    over[:, height : height + 8, :] = jnp.zeros((3, 8, width), jnp.float32)
    top_ref[:, height : height + 8, :] = jnp.zeros((3, 8, width), jnp.float32)
    v_ref[:, :, height : height + 8, :] = jnp.zeros((2, 3, 8, width), jnp.float32)
    zero = jnp.zeros((count, width), jnp.float32)

    def start_block(block, _):
        start = pl.multiple_of(block * count, count)
        rows = pl.ds(start, count)
        total = mod_ref[layers - 1, rows, :] + down_ref[6, rows, :]
        inverse = inverse_diagonal(down_ref[7, rows, :], total, edge, start, count)
        inv[rows, :] = inverse
        for comp in range(3):
            top_ref[comp, rows, :] = inverse * down_ref[comp, rows, :]
            over[comp, rows, :] = down_ref[3 + comp, rows, :]
        return 0

    lax.fori_loop(0, height // count, start_block, 0)

    def image_block(block, sums):
        along, across = sums
        start = pl.multiple_of(block * count, count)
        rows = pl.ds(start, count)
        low = plane_modes(z_ref, (layers - 1,), start, count)
        high = plane_modes(top_ref, (), start, count)
        lower, held = layer_forces(low, high, mod_ref[layers - 1, rows, :])
        for comp in range(3):
            image = nodal(lower, comp, carry.at[0], start, count) + part_ref[comp, rows, :]
            v = inv_ref[layers - 1, rows, :] * image
            v_ref[0, comp, rows, :] = v
            along = along + image * z_ref[layers - 1, comp, rows, :]
            across = across + image * v
        lower, _ = layer_forces(high, plane_modes(over, (), start, count), down_ref[6, rows, :])
        lower = {key: lower[key] + held[key] for key in lower}
        for comp in range(3):
            v_ref[1, comp, rows, :] = inv[rows, :] * nodal(lower, comp, carry.at[1], start, count)
        return along, across

    along, across = lax.fori_loop(0, height // count, image_block, (zero, zero))

    def energy_block(block, energy):
        start = pl.multiple_of(block * count, count)
        low = None
        for plane in range(layers + 1):
            if plane < layers - 1:
                high = plane_modes(low_v_ref, (plane,), start, count)
            else:
                high = plane_modes(v_ref, (plane - layers + 1,), start, count)
            if plane > 0:
                modes = layer_modes(low, high)
                energy = energy + mod_ref[plane - 1, pl.ds(start, count), :] * paired(modes, stiff(modes))
            low = high
        return energy

    energy = lax.fori_loop(0, height // count, energy_block, zero)
    sums = low_sums_ref[...] + add_up((zero[:8], along, across, energy))
    sums = jnp.sum(sums, axis=1, keepdims=True)
    lane = lax.broadcasted_iota(jnp.int32, (8, width), 1)
    row = lax.broadcasted_iota(jnp.int32, (8, width), 0)
    sums = jnp.sum(jnp.where(lane == row, sums, 0.0), axis=0, keepdims=True)
    sums_ref[...] = jnp.broadcast_to(sums, sums_ref.shape)


def edge_modes(ref, at, block, count, last):
    out = []
    for comp in range(3):
        here = ref[at(comp) + (pl.ds(block * count, count),)]
        if last:
            row = lax.broadcasted_iota(jnp.int32, here.shape, 0)
            below = jnp.where(row == count - 1, 0.0, pltpu.roll(here, count - 1, 0))
        else:
            below = ref[at(comp) + (pl.ds(block * count + 1, count),)]
        level, change = here + below, below - here
        level_next, change_next = next_lane(level), next_lane(change)
        out.append(((level + level_next, change + change_next), (level_next - level, change_next - change)))
    return out


def term_kernel(load_ref, z_ref, top_ref, low_v_ref, v_ref, disp_ref, above_ref, scale_ref, term_ref):
    layers, height, width = scale_ref.shape
    loads, share = term_ref.shape[0], term_ref.shape[3]
    for block in range(loads):
        start = block * share
        place = lax.rem(block - load_ref[0] + loads, loads)
        low = None
        for plane in range(layers + 1):
            if plane < layers:
                z = plane_modes(z_ref, (plane,), start, share)
                u = edge_modes(disp_ref, lambda comp: (0, comp, plane), block, share, block == loads - 1)
            else:
                z = plane_modes(top_ref, (), start, share)
                u = edge_modes(above_ref, lambda comp: (comp,), block, share, block == loads - 1)
            if plane < layers - 1:
                v = plane_modes(low_v_ref, (plane,), start, share)
            else:
                v = plane_modes(v_ref, (plane - layers + 1,), start, share)
            high = [z, v, u]
            if plane > 0:
                z, v, u = [layer_modes(one, two) for one, two in zip(low, high)]
                forces = stiff(u)
                scale = scale_ref[plane - 1, start : start + share, :]
                term_ref[place, 0, plane - 1] = scale * paired(z, forces)
                term_ref[place, 1, plane - 1] = scale * paired(v, forces)
            low = high


def solve_weights(sums_ref, load, loads):
    device = lax.broadcasted_iota(jnp.int32, sums_ref.shape, 0)
    lane = lax.broadcasted_iota(jnp.int32, (1, sums_ref.shape[1]), 1)
    mine = jnp.where(lax.rem(device, loads) == load, sums_ref[...], 0.0)
    mine = jnp.sum(mine, axis=0, keepdims=True)
    norm, along, across, energy = [
        jnp.sum(jnp.where(lane == place, mine, 0.0), axis=1, keepdims=True) for place in range(4)
    ]
    first = norm / along
    later = first * first * across - norm
    second = later / (first * first * (energy - across * across / along))
    return first + second * (first * across / along), second * first


def disp_kernel(loads, load_ref, sums_ref, z_ref, low_v_ref, v_ref, x_ref):
    layers, height = x_ref.shape[2], x_ref.shape[3]
    from_z, from_v = solve_weights(sums_ref, load_ref[0], loads)
    for comp in range(3):
        for plane in range(layers):
            v = low_v_ref[plane, comp, 0:height] if plane < layers - 1 else v_ref[0, comp, 0:height]
            x_ref[0, comp, plane] = from_z * z_ref[plane, comp, 0:height] - from_v * v


def grad_kernel(load_ref, sums_ref, *refs):
    term_refs, grad_ref = refs[:-1], refs[-1]
    loads = len(term_refs)
    total = None
    for place in range(loads):
        from_z, from_v = solve_weights(sums_ref, lax.rem(load_ref[0] - place + loads, loads), loads)
        part = from_z * term_refs[place][0] - from_v * term_refs[place][1]
        total = part if total is None else total + part
    grad_ref[...] = total


def f32(*shape):
    return jax.ShapeDtypeStruct(shape, jnp.float32)


def shards(forward_disp, adjoint_rhs, modulus_factor, zone_base, zone_ids, fixed_mask):
    layers, height, width = modulus_factor.shape
    loads = lax.axis_size("load")
    devices = lax.axis_size("space") * loads
    load = lax.axis_index("load")
    whole = pl.BlockSpec(memory_space=pltpu.VMEM)
    scalar = pl.BlockSpec(memory_space=pltpu.SMEM)
    params = pltpu.CompilerParams(vmem_limit_bytes=12 * 2**20)
    pad = height + 8
    share = height // loads
    position = load.astype(jnp.int32)[None]

    def hbm(*arrays):
        return [pltpu.with_memory_space_constraint(array, pltpu.HBM) for array in arrays]

    far = pl.BlockSpec(memory_space=pltpu.HBM)
    up, res, modulus, scale, free = pl.pallas_call(
        pack_kernel,
        out_shape=[f32(4, height, width), f32(3, layers, height, width)] + [f32(layers, height, width)] * 3,
        in_specs=[far] * 5,
        out_specs=[whole] * 5,
        scratch_shapes=[
            pltpu.SMEM(zone_base.shape, jnp.float32),
            pltpu.VMEM((3, layers, height, width), jnp.float32),
            pltpu.VMEM((layers, height, width), jnp.float32),
            pltpu.VMEM((layers, height, width), jnp.int32),
            pltpu.VMEM((layers, height, width), jnp.int32),
            pltpu.SemaphoreType.DMA((5,)),
        ],
        compiler_params=params,
        name="pack",
    )(*hbm(zone_base, adjoint_rhs, modulus_factor, zone_ids, fixed_mask))
    from_below = permute(up, "space", 1)
    down, lowest = pl.pallas_call(
        down_kernel,
        out_shape=(f32(8, height, width), f32(3, height, width)),
        in_specs=[far] * 2 + [whole] * 2,
        out_specs=[whole] * 2,
        scratch_shapes=[pltpu.VMEM((pad, width), jnp.float32), pltpu.SemaphoreType.DMA((3,))],
        compiler_params=params,
        name="down",
    )(*hbm(adjoint_rhs, forward_disp), modulus, free)
    from_above = permute(down, "space", -1)

    z, low_v, part, inverse, low_sums = pl.pallas_call(
        below_kernel,
        out_shape=(
            f32(layers, 3, pad, width),
            f32(layers - 1, 3, pad, width),
            f32(3, height, width),
            f32(layers, height, width),
            f32(8, width),
        ),
        in_specs=[whole] * 4,
        out_specs=[whole] * 5,
        scratch_shapes=[
            pltpu.VMEM((3, pad, width), jnp.float32),
            pltpu.VMEM((layers, 3, pad, width), jnp.float32),
            pltpu.VMEM((layers, pad, width), jnp.float32),
        ],
        compiler_params=params,
        cost_estimate=pl.CostEstimate(flops=9 * 10**9, bytes_accessed=2 * 2**20, transcendentals=0),
        name="below",
    )(from_below, res, modulus, free)
    lowest, low_sums = lax.optimization_barrier((lowest, low_sums))
    above_disp = permute(lowest, "space", -1)

    top, v, sums = pl.pallas_call(
        above_kernel,
        out_shape=(f32(3, pad, width), f32(2, 3, pad, width), f32(devices, 128)),
        in_specs=[whole] * 7,
        out_specs=[whole] * 3,
        scratch_shapes=[
            pltpu.VMEM((3, pad, width), jnp.float32),
            pltpu.VMEM((2, 3, pad, width), jnp.float32),
            pltpu.VMEM((pad, width), jnp.float32),
            pltpu.VMEM((height, width), jnp.float32),
        ],
        compiler_params=params,
        name="above",
    )(from_above, z, low_v, part, inverse, modulus, low_sums)
    sums = lax.all_to_all(sums, ("space", "load"), 0, 0, tiled=True)

    terms = pl.pallas_call(
        term_kernel,
        out_shape=f32(loads, 2, layers, share, width),
        in_specs=[scalar] + [whole] * 7,
        out_specs=whole,
        compiler_params=params,
        name="term",
    )(position, z, top, low_v, v, forward_disp, above_disp, scale)
    sums, terms = lax.optimization_barrier((sums, terms))
    terms = [terms[0]] + [permute(terms[by], "load", by, wrap=True) for by in range(1, loads)]

    x = pl.pallas_call(
        functools.partial(disp_kernel, loads),
        out_shape=f32(1, 3, layers, height, width),
        in_specs=[scalar] + [whole] * 4,
        out_specs=whole,
        compiler_params=params,
        name="disp",
    )(position, sums, z, low_v, v)
    grad = pl.pallas_call(
        grad_kernel,
        out_shape=f32(layers, share, width),
        in_specs=[scalar] + [whole] * (1 + loads),
        out_specs=whole,
        compiler_params=params,
        name="grad",
    )(position, sums, *terms)
    return x, grad


def solution(mesh):
    placed = (
        P("load", None, "space", None, None),
        P("load", None, "space", None, None),
        P("space", None, None),
        P(),
        P("space", None, None),
        P("space", None, None),
    )
    return jax.shard_map(
        shards,
        mesh=mesh,
        in_specs=placed,
        out_specs=(P("load", None, "space", None, None), P("space", "load", None)),
        check_vma=False,
    )
```

time: 47.3 us -> 44.1 us (0.932)
  starting transfers between devices: 16.1 us -> 12.4 us
  local copies, waits for them, and re-layouts: 1.61 us -> 0.02 us
  Pallas kernels: 9.17 us -> 10.5 us
  waiting for transfers between devices: 19.4 us -> 20.2 us
    all_to_all x1, starting transfers between devices: 8.02 us -> 4.89 us  [shards(): sums = lax.all_to_all(sums, ('space', 'load'), 0, 0, tiled=True)]
    pallas_call x3 -> x6, Pallas kernels: 6.28 us -> 8.64 us  [the longest x1 3.07 us: shards(): pl.pallas_call(above_kernel, out_shape=(f32(3, pad, width), f32(2, 3, pad...]
    all_to_all x1, waiting for transfers between devices: 3.27 us -> 5.18 us  [shards(): sums = lax.all_to_all(sums, ('space', 'load'), 0, 0, tiled=True)]
    ppermute x4, waiting for transfers between devices: 16.1 us -> 15.1 us  [permute(): return lax.ppermute(shard, axis, pairs)]
    pallas_call x1, Pallas kernels: 2.89 us -> 1.86 us  [shards(): pl.pallas_call(term_kernel, out_shape=f32(loads, 2, layers, share, width)...]
    unnamed x6 -> x2, local copies, waits for them, and re-layouts: 0.91 us -> 0.01 us
    squeeze x1 -> x0, local copies, waits for them, and re-layouts: 0.69 us -> none  [shards(): lowest = forward_disp[0, :, 0]]
    ppermute x4, starting transfers between devices: 8.13 us -> 7.51 us  [permute(): return lax.ppermute(shard, axis, pairs)]
  transfers between devices with their start and end apart: 5 -> 5, of which waited for: 4 -> 4; matrix products, arithmetic and copies ran while one was open for 1% -> 0% of each run, Pallas kernels for 15% -> 19%
where the time goes in v3:
time: 44.1 us; the launch traced here: 43.9 us
  waiting for transfers between devices  20.2 us (46%)
  starting transfers between devices  12.4 us (28%)
  Pallas kernels  10.5 us (24%)
  between operations  0.73 us (2%)
    ppermute x4, waiting for transfers between devices, permute(): return lax.ppermute(shard, axis, pairs)  15.1 us
    ppermute x4, starting transfers between devices, permute(): return lax.ppermute(shard, axis, pairs)  7.51 us
    all_to_all x1, waiting for transfers between devices, shards(): sums = lax.all_to_all(sums, ('space', 'load'), 0, 0, tiled=True)  5.18 us
    all_to_all x1, starting transfers between devices, shards(): sums = lax.all_to_all(sums, ('space', 'load'), 0, 0, tiled=True)  4.89 us
    pallas_call x1, Pallas kernels, shards(): pl.pallas_call(above_kernel, out_shape=(f32(3, pad, width), f32(2, 3, pad...  3.07 us
    pallas_call x1, Pallas kernels, shards(): pl.pallas_call(term_kernel, out_shape=f32(loads, 2, layers, share, width)...  1.86 us
    pallas_call x1, Pallas kernels, shards(): pl.pallas_call(below_kernel, out_shape=(f32(layers, 3, pad, width), f32(l...  1.46 us
    pallas_call x1, Pallas kernels, shards(): pl.pallas_call(pack_kernel, out_shape=[f32(4, height, width), f32(3, laye...  1.28 us
  transfers between devices with their start and end apart: 5, of which 4 were waited for; matrix products, arithmetic and copies ran while one was open for 0% of the time, Pallas kernels for 19%

profile of v3, /device:TPU:0, one launch (start us, length us, event | category | flops | bytes accessed | tf_op | source)
XLA Modules:
  0.0 43.9 jit_solution(3514619128790553321)
XLA Ops:
  0.6 1.3 %pack.1 = (f32[4,128,128]{2,1,0:T(8,128)S(1)}, f32[3,2,128,128]{3,2,1,0:T(8,128)S(1)}, f32[2,128,128]{2,1,0:T(8,128)S(1)}, f32[2,128,128]{2,1,0:T(8,128)S(1)}, f32[2,128,128]{2,1,0:T(8,128)S(1)}) custom-call(f32[8]{0:T(128)} %base_hbm.1, f32[1,3,2,128,128]{4,3,2,1,0:T(8,128)} %rhs_hbm.3, f32[2,128,128]{2,1,0:T(8,128)} %factor_hbm.1, s32[2,128,128]{2,1,0:T(8,128)} %ids_hbm.1, ...), custom_call_target="tpu_custom_call" | custom-call | tf_op jit(solution)/shard_map/pack/pallas_call | solution.py:432
  1.9 4.9 %collective-permute-start.1 = (f32[4,128,128]{2,1,0:T(8,128)S(1)}, f32[4,128,128]{2,1,0:T(8,128)S(1)}, u32[]{:S(2)}, u32[]{:S(2)}) collective-permute-start(f32[4,128,128]{2,1,0:T(8,128)S(1)} %get-tuple-element.24), channel_id=1, source_target_pairs={{0,2},{2,4},{4,6},{6,8},{8,10},{10,12},{12,14},{14,16},{16,18},{18... | collective-permute-start | bytes 786440 | tf_op jit(solution)/shard_map/ppermute | solution.py:24
  6.8 1.2 %down.1 = (f32[8,128,128]{2,1,0:T(8,128)S(1)}, f32[3,128,128]{2,1,0:T(8,128)S(1)}) custom-call(f32[1,3,2,128,128]{4,3,2,1,0:T(8,128)} %rhs_hbm.3, f32[1,3,2,128,128]{4,3,2,1,0:T(8,128)} %disp_ref.1, f32[2,128,128]{2,1,0:T(8,128)S(1)} %get-tuple-element.21.mod_ref, f32[2,128,128]{2,1,0:T(8,128)S(1)} %get-tuple-element.22.free_ref), custom_call_target="tpu_custom_call" | custom-call | tf_op jit(solution)/shard_map/down/pallas_call | solution.py:449
  8.0 1.3 %collective-permute-start = (f32[8,128,128]{2,1,0:T(8,128)S(1)}, f32[8,128,128]{2,1,0:T(8,128)S(1)}, u32[]{:S(2)}, u32[]{:S(2)}) collective-permute-start(f32[8,128,128]{2,1,0:T(8,128)S(1)} %get-tuple-element.23), channel_id=1, source_target_pairs={{2,0},{4,2},{6,4},{8,6},{10,8},{12,10},{14,12},{16,14},{18,16},{20... | collective-permute-start | bytes 1572872 | tf_op jit(solution)/shard_map/ppermute | solution.py:24
  9.3 3.1 %collective-permute-done.1.up_ref = f32[4,128,128]{2,1,0:T(8,128)S(1)} collective-permute-done((f32[4,128,128]{2,1,0:T(8,128)S(1)}, f32[4,128,128]{2,1,0:T(8,128)S(1)}, u32[]{:S(2)}, u32[]{:S(2)}) %collective-permute-start.1) | collective-permute-done | bytes 262176 | tf_op jit(solution)/shard_map/ppermute | solution.py:24
  12.3 1.5 %below.1 = (f32[2,3,136,128]{3,2,1,0:T(8,128)S(1)}, f32[1,3,136,128]{3,2,1,0:T(8,128)S(1)}, f32[3,128,128]{2,1,0:T(8,128)S(1)}, f32[2,128,128]{2,1,0:T(8,128)S(1)}, f32[8,128]{1,0:T(8,128)S(1)}) custom-call(f32[4,128,128]{2,1,0:T(8,128)S(1)} %collective-permute-done.1.up_ref, f32[3,2,128,128]{3,2,1,0:T(8,128)S(1)} %get-tuple-element.25.res_ref, ...), custom_call_target="tpu_custom_call" | custom-call | flops 8999999488 | bytes 2097152 | tf_op jit(solution)/shard_map/below/pallas_call | solution.py:460
  13.8 1.3 %collective-permute-start.2 = (f32[3,128,128]{2,1,0:T(8,128)S(1)}, f32[3,128,128]{2,1,0:T(8,128)S(1)}, u32[]{:S(2)}, u32[]{:S(2)}) collective-permute-start(f32[3,128,128]{2,1,0:T(8,128)S(1)} %get-tuple-element.36), channel_id=1, source_target_pairs={{2,0},{4,2},{6,4},{8,6},{10,8},{12,10},{14,12},{16,14},{18,16},{20... | collective-permute-start | bytes 589832 | tf_op jit(solution)/shard_map/ppermute | solution.py:24
  15.1 11.6 %collective-permute-done.down_ref = f32[8,128,128]{2,1,0:T(8,128)S(1)} collective-permute-done((f32[8,128,128]{2,1,0:T(8,128)S(1)}, f32[8,128,128]{2,1,0:T(8,128)S(1)}, u32[]{:S(2)}, u32[]{:S(2)}) %collective-permute-start) | collective-permute-done | bytes 524320 | tf_op jit(solution)/shard_map/ppermute | solution.py:24
  26.6 0.0 copy-start
  26.6 3.1 %above.1 = (f32[3,136,128]{2,1,0:T(8,128)S(1)}, f32[2,3,136,128]{3,2,1,0:T(8,128)S(1)}, f32[32,128]{1,0:T(8,128)}) custom-call(f32[8,128,128]{2,1,0:T(8,128)S(1)} %collective-permute-done.down_ref, f32[2,3,136,128]{3,2,1,0:T(8,128)S(1)} %get-tuple-element.26.z_ref, f32[1,3,136,128]{3,2,1,0:T(8,128)S(1)} %get-tuple-element.27.low_v_ref, ...), custom_call_target="tpu_custom_call" | custom-call | tf_op jit(solution)/shard_map/above/pallas_call | solution.py:483
  29.7 4.9 %all-to-all-start = ((f32[32,1,128]{2,1,0:T(1,128)}), f32[32,1,128]{2,1,0:T(1,128)S(1)}, u32[]{:S(2)}, u32[]{:S(2)}) async-start(f32[32,1,128]{2,1,0:T(1,128)} %bitcast.2), calls=%async_computation | async-start | bytes 32768 | tf_op jit(solution)/shard_map/all_to_all | solution.py:497
  34.6 0.0 collective-permute-done.2.above_ref
  34.6 0.0 copy-done
  34.6 1.9 %term.1 = f32[2,2,2,64,128]{4,3,2,1,0:T(8,128)S(1)} custom-call(s32[1]{0:T(128)} %bitcast.load_ref, f32[2,3,136,128]{3,2,1,0:T(8,128)S(1)} %get-tuple-element.26.z_ref, f32[3,136,128]{2,1,0:T(8,128)S(1)} %get-tuple-element.34.top_ref, f32[1,3,136,128]{3,2,1,0:T(8,128)S(1)} %get-tuple-element.27.low_v_ref, f32[2,3,136,128]{3,2,1,0:T(8,128)S(1)} %get-tuple-element.35.v_ref, ...), custom_call_target="tpu_custom_call" | custom-call | tf_op jit(solution)/shard_map/term/pallas_call | solution.py:499
  36.5 5.2 %all-to-all-done = f32[32,1,128]{2,1,0:T(1,128)S(1)} async-done(((f32[32,1,128]{2,1,0:T(1,128)}), f32[32,1,128]{2,1,0:T(1,128)S(1)}, u32[]{:S(2)}, u32[]{:S(2)}) %all-to-all-start) | async-done | bytes 16416 | tf_op jit(solution)/shard_map/all_to_all | solution.py:497
  41.7 0.1 collective-permute-start.3
  41.8 0.9 %disp.1 = f32[1,3,2,128,128]{4,3,2,1,0:T(8,128)} custom-call(s32[1]{0:T(128)} %bitcast.load_ref, f32[32,128]{1,0:T(8,128)S(1)} %bitcast.9, f32[2,3,136,128]{3,2,1,0:T(8,128)S(1)} %get-tuple-element.26.z_ref, f32[1,3,136,128]{3,2,1,0:T(8,128)S(1)} %get-tuple-element.27.low_v_ref, f32[2,3,136,128]{3,2,1,0:T(8,128)S(1)} %get-tuple-element.35.v_ref), custom_call_target="tpu_custom_call" | custom-call | tf_op jit(solution)/shard_map/disp/pallas_call | solution.py:510
  42.7 0.4 collective-permute-done.3.refs_1_
  43.1 0.8 %grad.1 = f32[2,64,128]{2,1,0:T(8,128)} custom-call(s32[1]{0:T(128)} %bitcast.load_ref, f32[32,128]{1,0:T(8,128)S(1)} %bitcast.10, f32[2,2,64,128]{3,2,1,0:T(8,128)S(1)} %get-tuple-element.41.refs_0_, f32[2,2,64,128]{3,2,1,0:T(8,128)S(1)} %collective-permute-done.3.refs_1_), custom_call_target="tpu_custom_call" | custom-call | tf_op jit(solution)/shard_map/grad/pallas_call | solution.py:518
  (1 shorter events, 0.0 us)
Async XLA Ops:
  1.9 10.4 %collective-permute-start.1 = (f32[4,128,128]{2,1,0:T(8,128)S(1)}, f32[4,128,128]{2,1,0:T(8,128)S(1)}, u32[]{:S(2)}, u32[]{:S(2)}) collective-permute-start(f32[4,128,128]{2,1,0:T(8,128)S(1)} %get-tuple-element.24), channel_id=1, source_target_pairs={{0,2},{2,4},{4,6},{6,8},{8,10},{10,12},{12,14},{14,16},{16,18},{18... | collective-permute-start | bytes 786440 | tf_op jit(solution)/shard_map/ppermute | solution.py:24
  8.0 18.7 %collective-permute-start = (f32[8,128,128]{2,1,0:T(8,128)S(1)}, f32[8,128,128]{2,1,0:T(8,128)S(1)}, u32[]{:S(2)}, u32[]{:S(2)}) collective-permute-start(f32[8,128,128]{2,1,0:T(8,128)S(1)} %get-tuple-element.23), channel_id=1, source_target_pairs={{2,0},{4,2},{6,4},{8,6},{10,8},{12,10},{14,12},{16,14},{18,16},{20... | collective-permute-start | bytes 1572872 | tf_op jit(solution)/shard_map/ppermute | solution.py:24
  13.8 20.8 %collective-permute-start.2 = (f32[3,128,128]{2,1,0:T(8,128)S(1)}, f32[3,128,128]{2,1,0:T(8,128)S(1)}, u32[]{:S(2)}, u32[]{:S(2)}) collective-permute-start(f32[3,128,128]{2,1,0:T(8,128)S(1)} %get-tuple-element.36), channel_id=1, source_target_pairs={{2,0},{4,2},{6,4},{8,6},{10,8},{12,10},{14,12},{16,14},{18,16},{20... | collective-permute-start | bytes 589832 | tf_op jit(solution)/shard_map/ppermute | solution.py:24
  26.6 8.0 %copy-start = (f32[1,3,2,128,128]{4,3,2,1,0:T(8,128)S(1)}, f32[1,3,2,128,128]{4,3,2,1,0:T(8,128)}, u32[]{:S(2)}) copy-start(f32[1,3,2,128,128]{4,3,2,1,0:T(8,128)} %disp_ref.1) | copy-start | bytes 1179652
  29.7 12.0 %all-to-all-start = ((f32[32,1,128]{2,1,0:T(1,128)}), f32[32,1,128]{2,1,0:T(1,128)S(1)}, u32[]{:S(2)}, u32[]{:S(2)}) async-start(f32[32,1,128]{2,1,0:T(1,128)} %bitcast.2), calls=%async_computation | async-start | bytes 32768 | tf_op jit(solution)/shard_map/all_to_all | solution.py:497
  41.7 1.4 %collective-permute-start.3 = (f32[2,2,64,128]{3,2,1,0:T(8,128)S(1)}, f32[2,2,64,128]{3,2,1,0:T(8,128)S(1)}, u32[]{:S(2)}, u32[]{:S(2)}) collective-permute-start(f32[2,2,64,128]{3,2,1,0:T(8,128)S(1)} %get-tuple-element.40), channel_id=1, source_target_pairs={{0,1},{1,0},{2,3},{3,2},{4,5},{5,4},{6,7},{7,6},{8,9},{9,8},{10,11... | collective-permute-start | bytes 393224 | tf_op jit(solution)/shard_map/ppermute | solution.py:24

commit v4 on v3

--- a/solution.py
+++ b/solution.py
@@ -142,71 +142,69 @@
     return free / (CORNER * (total + edge[pl.ds(start + 7, count), :]))
 
 
+def received(shared, item, load, start, count):
+    loads, share = len(shared), shared[0].shape[0] // 3
+    rows = pl.ds(pl.multiple_of(item * share + lax.rem(start, share), 8), count)
+    distance = lax.rem(load - start // share + loads, loads)
+    out = shared[0][rows, :]
+    for by in range(1, loads):
+        out = jnp.where(distance == by, shared[by][rows, :], out)
+    return out
+
+
 def pack_kernel(
-    base_hbm, rhs_hbm, factor_hbm, ids_hbm, mask_hbm,
-    up_ref, res_ref, mod_ref, scale_ref, free_ref,
-    base_ref, rhs_ref, factor_ref, ids_ref, mask_ref, sems,
+    load_ref, base_hbm, rhs_hbm, factor_hbm, ids_hbm, mask_hbm, disp_hbm,
+    up_ref, part_ref, down_ref, low_ref, res_ref, mod_ref, scale_ref, free_ref,
+    base_ref, rhs_ref, factor_ref, ids_ref, mask_ref, edge, sems,
 ):
     layers, height, width = factor_ref.shape
+    share = part_ref.shape[0] // 2
+    mine = pl.ds(pl.multiple_of(load_ref[0] * share, 8), share)
     pairs = (
         (base_hbm, base_ref),
         (ids_hbm, ids_ref),
         (factor_hbm, factor_ref),
         (mask_hbm, mask_ref),
         (rhs_hbm.at[0], rhs_ref),
+        (disp_hbm.at[0, :, 0], low_ref),
     )
     copies = [pltpu.make_async_copy(source, target, sems.at[place]) for place, (source, target) in enumerate(pairs)]
     for copy in copies:
         copy.start()
+    edge[:, 0:8, :] = jnp.zeros((2, 8, width), jnp.float32)
     for copy in copies[:3]:
         copy.wait()
-    ids = ids_ref[...]
-    scale = jnp.full(ids.shape, base_ref[0])
+    scale = jnp.full(ids_ref.shape, base_ref[0])
     for zone in range(1, base_ref.shape[0]):
-        scale = jnp.where(ids == zone, base_ref[zone], scale)
+        scale = jnp.where(ids_ref[...] == zone, base_ref[zone], scale)
     modulus = factor_ref[...] * scale
     scale_ref[...] = scale
     mod_ref[...] = modulus
     copies[3].wait()
     free = 1.0 - mask_ref[...].astype(jnp.float32)
     free_ref[...] = free
-    row = lax.broadcasted_iota(jnp.int32, (height, width), 0)
-
-    def inverse(lower, upper, free):
-        total = lower + upper
-        total = total + last_lane(total)
-        total = total + jnp.where(row == 0, 0.0, pltpu.roll(total, 1, 0))
-        return free / (CORNER * total)
-
-    top = inverse(modulus[layers - 2], modulus[layers - 1], free[layers - 1])
-    up_ref[3] = modulus[layers - 1]
+    up_ref[3 * height :] = mod_ref[layers - 1, mine, :]
+    part_ref[0:share] = mod_ref[0, mine, :]
+    part_ref[share:] = free_ref[0, mine, :]
+    top = inverse_diagonal(free[layers - 1], modulus[layers - 2] + modulus[layers - 1], edge.at[0], 0, height)
+    second = top
+    if layers > 2:
+        second = inverse_diagonal(free[1], modulus[0] + modulus[1], edge.at[1], 0, height)
     copies[4].wait()
-    res = free[None] * rhs_ref[...]
-    res_ref[...] = res
-    up_ref[0:3] = res[:, layers - 1] * top
-
-
-def down_kernel(rhs_hbm, disp_hbm, mod_ref, free_ref, down_ref, low_ref, edge, sems):
-    copies = [
-        pltpu.make_async_copy(rhs_hbm.at[0, :, 0], down_ref.at[0:3], sems.at[0]),
-        pltpu.make_async_copy(rhs_hbm.at[0, :, 1], down_ref.at[3:6], sems.at[1]),
-        pltpu.make_async_copy(disp_hbm.at[0, :, 0], low_ref, sems.at[2]),
-    ]
-    for copy in copies:
-        copy.start()
-    height = mod_ref.shape[1]
-    down_ref[6] = mod_ref[0]
-    down_ref[7] = free_ref[0]
-    edge[0:8, :] = jnp.zeros((8, edge.shape[1]), jnp.float32)
-    inverse = inverse_diagonal(free_ref[1], mod_ref[0] + mod_ref[1], edge, 0, height)
-    for copy in copies:
-        copy.wait()
-    down_ref[3:6] = down_ref[3:6] * inverse
-
-
-def below_kernel(up_ref, res_ref, mod_ref, free_ref, z_ref, v_ref, part_ref, inv_ref, sums_ref, under, carry, edge):
+    for comp in range(3):
+        res = free * rhs_ref[comp]
+        res_ref[comp] = res
+        up_ref[comp * height : (comp + 1) * height] = res[layers - 1] * top
+        down_ref[comp] = res[0]
+        down_ref[3 + comp] = res[1] * second
+    copies[5].wait()
+
+
+def below_kernel(load_ref, up_ref, res_ref, mod_ref, free_ref, *refs):
+    z_ref, v_ref, part_ref, inv_ref, sums_ref, under, carry, edge = refs[-8:]
+    shared = refs[:-8]
     layers, height, width = mod_ref.shape
-    count = min(ROWS, height)
+    count = min(ROWS, height // len(shared))
     edge[:, 0:8, :] = jnp.zeros((layers, 8, width), jnp.float32)
     carry[:, :, 0:8, :] = jnp.zeros((layers, 3, 8, width), jnp.float32)
     under[:, height : height + 8, :] = jnp.zeros((3, 8, width), jnp.float32)
@@ -214,14 +212,16 @@
     v_ref[:, :, height : height + 8, :] = jnp.zeros((layers - 1, 3, 8, width), jnp.float32)
     zero = jnp.zeros((count, width), jnp.float32)
 
-    def modulus(layer, rows):
-        return mod_ref[layer, rows, :] if layer >= 0 else up_ref[3, rows, :]
+    def modulus(layer, start):
+        if layer < 0:
+            return received(shared, 0, load_ref[0], start, count)
+        return mod_ref[layer, pl.ds(start, count), :]
 
     def start_block(block, norm):
         start = pl.multiple_of(block * count, count)
         rows = pl.ds(start, count)
         for plane in range(layers):
-            total = modulus(plane - 1, rows) + modulus(plane, rows)
+            total = modulus(plane - 1, start) + modulus(plane, start)
             inverse = inverse_diagonal(free_ref[plane, rows, :], total, edge.at[plane], start, count)
             inv_ref[plane, rows, :] = inverse
             for comp in range(3):
@@ -230,7 +230,7 @@
                 z_ref[plane, comp, rows, :] = z
                 norm = norm + res * z
         for comp in range(3):
-            under[comp, rows, :] = up_ref[comp, rows, :]
+            under[comp, rows, :] = up_ref[pl.ds(comp * height + start, count), :]
         return norm
 
     norm = lax.fori_loop(0, height // count, start_block, zero)
@@ -243,7 +243,7 @@
         held = None
         for layer in range(layers):
             high = plane_modes(z_ref, (layer,), start, count)
-            lower, upper = layer_forces(low, high, modulus(layer - 1, rows))
+            lower, upper = layer_forces(low, high, modulus(layer - 1, start))
             if layer > 0:
                 plane = layer - 1
                 lower = {key: lower[key] + held[key] for key in lower}
@@ -262,12 +262,11 @@
     sums_ref[...] = add_up((norm, along, across))
 
 
-def above_kernel(
-    down_ref, z_ref, low_v_ref, part_ref, inv_ref, mod_ref, low_sums_ref,
-    top_ref, v_ref, sums_ref, over, carry, edge, inv,
-):
+def above_kernel(load_ref, down_ref, z_ref, low_v_ref, part_ref, inv_ref, mod_ref, low_sums_ref, *refs):
+    top_ref, v_ref, sums_ref, over, carry, edge, inv = refs[-7:]
+    shared = refs[:-7]
     layers, height, width = mod_ref.shape
-    count = min(ROWS, height)
+    count = min(ROWS, height // len(shared))
     edge[0:8, :] = jnp.zeros((8, width), jnp.float32)
     carry[:, :, 0:8, :] = jnp.zeros((2, 3, 8, width), jnp.float32)
     over[:, height : height + 8, :] = jnp.zeros((3, 8, width), jnp.float32)
@@ -278,8 +277,8 @@
     def start_block(block, _):
         start = pl.multiple_of(block * count, count)
         rows = pl.ds(start, count)
-        total = mod_ref[layers - 1, rows, :] + down_ref[6, rows, :]
-        inverse = inverse_diagonal(down_ref[7, rows, :], total, edge, start, count)
+        total = mod_ref[layers - 1, rows, :] + received(shared, 1, load_ref[0], start, count)
+        inverse = inverse_diagonal(received(shared, 2, load_ref[0], start, count), total, edge, start, count)
         inv[rows, :] = inverse
         for comp in range(3):
             top_ref[comp, rows, :] = inverse * down_ref[comp, rows, :]
@@ -301,7 +300,8 @@
             v_ref[0, comp, rows, :] = v
             along = along + image * z_ref[layers - 1, comp, rows, :]
             across = across + image * v
-        lower, _ = layer_forces(high, plane_modes(over, (), start, count), down_ref[6, rows, :])
+        stiffness = received(shared, 1, load_ref[0], start, count)
+        lower, _ = layer_forces(high, plane_modes(over, (), start, count), stiffness)
         lower = {key: lower[key] + held[key] for key in lower}
         for comp in range(3):
             v_ref[1, comp, rows, :] = inv[rows, :] * nodal(lower, comp, carry.at[1], start, count)
@@ -429,32 +429,28 @@
         return [pltpu.with_memory_space_constraint(array, pltpu.HBM) for array in arrays]
 
     far = pl.BlockSpec(memory_space=pltpu.HBM)
-    up, res, modulus, scale, free = pl.pallas_call(
+    up, part_down, down, lowest, res, modulus, scale, free = pl.pallas_call(
         pack_kernel,
-        out_shape=[f32(4, height, width), f32(3, layers, height, width)] + [f32(layers, height, width)] * 3,
-        in_specs=[far] * 5,
-        out_specs=[whole] * 5,
+        out_shape=[f32(3 * height + share, width), f32(2 * share, width), f32(6, height, width), f32(3, height, width)]
+        + [f32(3, layers, height, width)]
+        + [f32(layers, height, width)] * 3,
+        in_specs=[scalar] + [far] * 6,
+        out_specs=[whole] * 8,
         scratch_shapes=[
             pltpu.SMEM(zone_base.shape, jnp.float32),
             pltpu.VMEM((3, layers, height, width), jnp.float32),
             pltpu.VMEM((layers, height, width), jnp.float32),
             pltpu.VMEM((layers, height, width), jnp.int32),
             pltpu.VMEM((layers, height, width), jnp.int32),
-            pltpu.SemaphoreType.DMA((5,)),
+            pltpu.VMEM((2, pad, width), jnp.float32),
+            pltpu.SemaphoreType.DMA((6,)),
         ],
         compiler_params=params,
         name="pack",
-    )(*hbm(zone_base, adjoint_rhs, modulus_factor, zone_ids, fixed_mask))
+    )(position, *hbm(zone_base, adjoint_rhs, modulus_factor, zone_ids, fixed_mask, forward_disp))
     from_below = permute(up, "space", 1)
-    down, lowest = pl.pallas_call(
-        down_kernel,
-        out_shape=(f32(8, height, width), f32(3, height, width)),
-        in_specs=[far] * 2 + [whole] * 2,
-        out_specs=[whole] * 2,
-        scratch_shapes=[pltpu.VMEM((pad, width), jnp.float32), pltpu.SemaphoreType.DMA((3,))],
-        compiler_params=params,
-        name="down",
-    )(*hbm(adjoint_rhs, forward_disp), modulus, free)
+    shared = jnp.concatenate([from_below[3 * height :], permute(part_down, "space", -1)])
+    shared = [shared] + [permute(shared, "load", by, wrap=True) for by in range(1, loads)]
     from_above = permute(down, "space", -1)
 
     z, low_v, part, inverse, low_sums = pl.pallas_call(
@@ -466,7 +462,7 @@
             f32(layers, height, width),
             f32(8, width),
         ),
-        in_specs=[whole] * 4,
+        in_specs=[scalar] + [whole] * (4 + loads),
         out_specs=[whole] * 5,
         scratch_shapes=[
             pltpu.VMEM((3, pad, width), jnp.float32),
@@ -474,16 +470,16 @@
             pltpu.VMEM((layers, pad, width), jnp.float32),
         ],
         compiler_params=params,
-        cost_estimate=pl.CostEstimate(flops=9 * 10**9, bytes_accessed=2 * 2**20, transcendentals=0),
+        cost_estimate=pl.CostEstimate(flops=10**9, bytes_accessed=2**10, transcendentals=0),
         name="below",
-    )(from_below, res, modulus, free)
+    )(position, from_below, res, modulus, free, *shared)
     lowest, low_sums = lax.optimization_barrier((lowest, low_sums))
     above_disp = permute(lowest, "space", -1)
 
     top, v, sums = pl.pallas_call(
         above_kernel,
         out_shape=(f32(3, pad, width), f32(2, 3, pad, width), f32(devices, 128)),
-        in_specs=[whole] * 7,
+        in_specs=[scalar] + [whole] * (7 + loads),
         out_specs=[whole] * 3,
         scratch_shapes=[
             pltpu.VMEM((3, pad, width), jnp.float32),
@@ -493,7 +489,7 @@
         ],
         compiler_params=params,
         name="above",
-    )(from_above, z, low_v, part, inverse, modulus, low_sums)
+    )(position, from_above, z, low_v, part, inverse, modulus, low_sums, *shared)
     sums = lax.all_to_all(sums, ("space", "load"), 0, 0, tiled=True)
 
     terms = pl.pallas_call(

time: 44.1 us -> 41.6 us (0.943)
  waiting for transfers between devices: 20.2 us -> 16.8 us
  starting transfers between devices: 12.4 us -> 14.5 us
  Pallas kernels: 10.5 us -> 9.39 us
    ppermute x4 -> x6, waiting for transfers between devices: 15.1 us -> 11.6 us  [permute(): return lax.ppermute(shard, axis, pairs)]
    ppermute x4 -> x6, starting transfers between devices: 7.51 us -> 8.87 us  [permute(): return lax.ppermute(shard, axis, pairs)]
    pallas_call x2 -> x1, Pallas kernels: 2.45 us -> 1.32 us  [shards(): pl.pallas_call(pack_kernel, out_shape=[f32(3 * height + share, width), f3...]
    all_to_all x1, starting transfers between devices: 4.89 us -> 5.6 us  [shards(): sums = lax.all_to_all(sums, ('space', 'load'), 0, 0, tiled=True)]
  transfers between devices with their start and end apart: 5 -> 7, of which waited for: 4 -> 6; matrix products, arithmetic and copies ran while one was open for 0% -> 0% of each run, Pallas kernels for 19% -> 18%
where the time goes in v4:
time: 41.6 us; the launch traced here: 41.4 us
  waiting for transfers between devices  16.8 us (40%)
  starting transfers between devices  14.5 us (35%)
  Pallas kernels  9.39 us (23%)
  between operations  0.74 us (2%)
    ppermute x6, waiting for transfers between devices, permute(): return lax.ppermute(shard, axis, pairs)  11.6 us
    ppermute x6, starting transfers between devices, permute(): return lax.ppermute(shard, axis, pairs)  8.87 us
    all_to_all x1, starting transfers between devices, shards(): sums = lax.all_to_all(sums, ('space', 'load'), 0, 0, tiled=True)  5.6 us
    all_to_all x1, waiting for transfers between devices, shards(): sums = lax.all_to_all(sums, ('space', 'load'), 0, 0, tiled=True)  5.19 us
    pallas_call x1, Pallas kernels, shards(): pl.pallas_call(above_kernel, out_shape=(f32(3, pad, width), f32(2, 3, pad...  3.1 us
    pallas_call x1, Pallas kernels, shards(): pl.pallas_call(term_kernel, out_shape=f32(loads, 2, layers, share, width)...  1.86 us
    pallas_call x1, Pallas kernels, shards(): pl.pallas_call(below_kernel, out_shape=(f32(layers, 3, pad, width), f32(l...  1.46 us
    pallas_call x1, Pallas kernels, shards(): pl.pallas_call(pack_kernel, out_shape=[f32(3 * height + share, width), f3...  1.32 us
  transfers between devices with their start and end apart: 7, of which 6 were waited for; matrix products, arithmetic and copies ran while one was open for 0% of the time, Pallas kernels for 18%

profile of v4, /device:TPU:0, one launch (start us, length us, event | category | flops | bytes accessed | tf_op | source)
XLA Modules:
  0.0 41.4 jit_solution(7195867987666960341)
XLA Ops:
  0.6 1.3 %pack.1 = (f32[448,128]{1,0:T(8,128)S(1)}, f32[128,128]{1,0:T(8,128)S(1)}, f32[6,128,128]{2,1,0:T(8,128)S(1)}, f32[3,128,128]{2,1,0:T(8,128)S(1)}, f32[3,2,128,1...) custom-call(s32[1]{0:T(128)} %bitcast.load_ref, ...), custom_call_target="tpu_custom_call" | custom-call | tf_op jit(solution)/shard_map/pack/pallas_call | solution.py:432
  2.0 4.9 %collective-permute-start.1 = (f32[448,128]{1,0:T(8,128)S(1)}, f32[448,128]{1,0:T(8,128)S(1)}, u32[]{:S(2)}, u32[]{:S(2)}) collective-permute-start(f32[448,128]{1,0:T(8,128)S(1)} %get-tuple-element.23), channel_id=1, source_target_pairs={{0,2},{2,4},{4,6},{6,8},{8,10},{10,12},{12,14},{14,16},{16,18},{18... | collective-permute-start | bytes 688136 | tf_op jit(solution)/shard_map/ppermute | solution.py:24
  6.8 1.3 %collective-permute-start.2 = (f32[128,128]{1,0:T(8,128)S(1)}, f32[128,128]{1,0:T(8,128)S(1)}, u32[]{:S(2)}, u32[]{:S(2)}) collective-permute-start(f32[128,128]{1,0:T(8,128)S(1)} %get-tuple-element.27), channel_id=1, source_target_pairs={{2,0},{4,2},{6,4},{8,6},{10,8},{12,10},{14,12},{16,14},{18,16},{20... | collective-permute-start | bytes 196616 | tf_op jit(solution)/shard_map/ppermute | solution.py:24
  8.1 1.3 %collective-permute-start = (f32[6,128,128]{2,1,0:T(8,128)S(1)}, f32[6,128,128]{2,1,0:T(8,128)S(1)}, u32[]{:S(2)}, u32[]{:S(2)}) collective-permute-start(f32[6,128,128]{2,1,0:T(8,128)S(1)} %get-tuple-element.22), channel_id=1, source_target_pairs={{2,0},{4,2},{6,4},{8,6},{10,8},{12,10},{14,12},{16,14},{18,16},{20... | collective-permute-start | bytes 1179656 | tf_op jit(solution)/shard_map/ppermute | solution.py:24
  9.4 2.2 %collective-permute-done.1.up_ref = f32[448,128]{1,0:T(8,128)S(1)} collective-permute-done((f32[448,128]{1,0:T(8,128)S(1)}, f32[448,128]{1,0:T(8,128)S(1)}, u32[]{:S(2)}, u32[]{:S(2)}) %collective-permute-start.1) | collective-permute-done | bytes 229408 | tf_op jit(solution)/shard_map/ppermute | solution.py:24
  11.7 4.5 %collective-permute-done.2 = f32[128,128]{1,0:T(8,128)S(1)} collective-permute-done((f32[128,128]{1,0:T(8,128)S(1)}, f32[128,128]{1,0:T(8,128)S(1)}, u32[]{:S(2)}, u32[]{:S(2)}) %collective-permute-start.2) | collective-permute-done | bytes 65568 | tf_op jit(solution)/shard_map/ppermute | solution.py:24
  16.2 0.1 collective-permute-start.3
  16.2 1.3 %collective-permute-done.3.refs_1_ = f32[192,128]{1,0:T(8,128)S(1)} collective-permute-done((f32[192,128]{1,0:T(8,128)S(1)}, f32[192,128]{1,0:T(8,128)S(1)}, u32[]{:S(2)}, u32[]{:S(2)}) %collective-permute-start.3) | collective-permute-done | bytes 98336 | tf_op jit(solution)/shard_map/ppermute | solution.py:24
  17.5 1.5 %below.1 = (f32[2,3,136,128]{3,2,1,0:T(8,128)S(1)}, f32[1,3,136,128]{3,2,1,0:T(8,128)S(1)}, f32[3,128,128]{2,1,0:T(8,128)S(1)}, f32[2,128,128]{2,1,0:T(8,128)S(1)}, f32[8,128]{1,0:T(8,128)S(1)}) custom-call(s32[1]{0:T(128)} %bitcast.load_ref, f32[448,128]{1,0:T(8,128)S(1)} %collective-permute-done.1.up_ref, ...), custom_call_target="tpu_custom_call" | custom-call | flops 1000000000 | bytes 1024 | tf_op jit(solution)/shard_map/below/pallas_call | solution.py:456
  19.0 1.3 %collective-permute-start.4 = (f32[3,128,128]{2,1,0:T(8,128)S(1)}, f32[3,128,128]{2,1,0:T(8,128)S(1)}, u32[]{:S(2)}, u32[]{:S(2)}) collective-permute-start(f32[3,128,128]{2,1,0:T(8,128)S(1)} %get-tuple-element.38), channel_id=1, source_target_pairs={{2,0},{4,2},{6,4},{8,6},{10,8},{12,10},{14,12},{16,14},{18,16},{20... | collective-permute-start | bytes 589832 | tf_op jit(solution)/shard_map/ppermute | solution.py:24
  20.3 3.1 %collective-permute-done.down_ref = f32[6,128,128]{2,1,0:T(8,128)S(1)} collective-permute-done((f32[6,128,128]{2,1,0:T(8,128)S(1)}, f32[6,128,128]{2,1,0:T(8,128)S(1)}, u32[]{:S(2)}, u32[]{:S(2)}) %collective-permute-start) | collective-permute-done | bytes 393248 | tf_op jit(solution)/shard_map/ppermute | solution.py:24
  23.4 0.0 copy-start
  23.4 3.1 %above.1 = (f32[3,136,128]{2,1,0:T(8,128)S(1)}, f32[2,3,136,128]{3,2,1,0:T(8,128)S(1)}, f32[32,128]{1,0:T(8,128)}) custom-call(s32[1]{0:T(128)} %bitcast.load_ref, f32[6,128,128]{2,1,0:T(8,128)S(1)} %collective-permute-done.down_ref, f32[2,3,136,128]{3,2,1,0:T(8,128)S(1)} %get-tuple-element.28.z_ref, f32[1,3,136,128]{3,2,1,0:T(8,128)S(1)} %get-tuple-element.29.low_v_ref, ...), custom_call_target="tpu_custom_call" | custom-call | tf_op jit(solution)/shard_map/above/pallas_call | solution.py:479
  26.5 5.6 %all-to-all-start = ((f32[32,1,128]{2,1,0:T(1,128)}), f32[32,1,128]{2,1,0:T(1,128)S(1)}, u32[]{:S(2)}, u32[]{:S(2)}) async-start(f32[32,1,128]{2,1,0:T(1,128)} %bitcast.2), calls=%async_computation | async-start | bytes 32768 | tf_op jit(solution)/shard_map/all_to_all | solution.py:493
  32.1 0.0 collective-permute-done.4.above_ref
  32.2 0.0 copy-done
  32.2 1.9 %term.1 = f32[2,2,2,64,128]{4,3,2,1,0:T(8,128)S(1)} custom-call(s32[1]{0:T(128)} %bitcast.load_ref, f32[2,3,136,128]{3,2,1,0:T(8,128)S(1)} %get-tuple-element.28.z_ref, f32[3,136,128]{2,1,0:T(8,128)S(1)} %get-tuple-element.36.top_ref, f32[1,3,136,128]{3,2,1,0:T(8,128)S(1)} %get-tuple-element.29.low_v_ref, f32[2,3,136,128]{3,2,1,0:T(8,128)S(1)} %get-tuple-element.37.v_ref, ...), custom_call_target="tpu_custom_call" | custom-call | tf_op jit(solution)/shard_map/term/pallas_call | solution.py:495
  34.0 5.2 %all-to-all-done = f32[32,1,128]{2,1,0:T(1,128)S(1)} async-done(((f32[32,1,128]{2,1,0:T(1,128)}), f32[32,1,128]{2,1,0:T(1,128)S(1)}, u32[]{:S(2)}, u32[]{:S(2)}) %all-to-all-start) | async-done | bytes 16416 | tf_op jit(solution)/shard_map/all_to_all | solution.py:493
  39.2 0.1 collective-permute-start.5
  39.3 0.9 %disp.1 = f32[1,3,2,128,128]{4,3,2,1,0:T(8,128)} custom-call(s32[1]{0:T(128)} %bitcast.load_ref, f32[32,128]{1,0:T(8,128)S(1)} %bitcast.9, f32[2,3,136,128]{3,2,1,0:T(8,128)S(1)} %get-tuple-element.28.z_ref, f32[1,3,136,128]{3,2,1,0:T(8,128)S(1)} %get-tuple-element.29.low_v_ref, f32[2,3,136,128]{3,2,1,0:T(8,128)S(1)} %get-tuple-element.37.v_ref), custom_call_target="tpu_custom_call" | custom-call | tf_op jit(solution)/shard_map/disp/pallas_call | solution.py:506
  40.2 0.4 %collective-permute-done.5.refs_1_ = f32[2,2,64,128]{3,2,1,0:T(8,128)S(1)} collective-permute-done((f32[2,2,64,128]{3,2,1,0:T(8,128)S(1)}, f32[2,2,64,128]{3,2,1,0:T(8,128)S(1)}, u32[]{:S(2)}, u32[]{:S(2)}) %collective-permute-start.5) | collective-permute-done | bytes 131104 | tf_op jit(solution)/shard_map/ppermute | solution.py:24
  40.7 0.8 %grad.1 = f32[2,64,128]{2,1,0:T(8,128)} custom-call(s32[1]{0:T(128)} %bitcast.load_ref, f32[32,128]{1,0:T(8,128)S(1)} %bitcast.10, f32[2,2,64,128]{3,2,1,0:T(8,128)S(1)} %get-tuple-element.43.refs_0_, f32[2,2,64,128]{3,2,1,0:T(8,128)S(1)} %collective-permute-done.5.refs_1_), custom_call_target="tpu_custom_call" | custom-call | tf_op jit(solution)/shard_map/grad/pallas_call | solution.py:514
  (3 shorter events, 0.0 us)
Async XLA Ops:
  2.0 9.7 %collective-permute-start.1 = (f32[448,128]{1,0:T(8,128)S(1)}, f32[448,128]{1,0:T(8,128)S(1)}, u32[]{:S(2)}, u32[]{:S(2)}) collective-permute-start(f32[448,128]{1,0:T(8,128)S(1)} %get-tuple-element.23), channel_id=1, source_target_pairs={{0,2},{2,4},{4,6},{6,8},{8,10},{10,12},{12,14},{14,16},{16,18},{18... | collective-permute-start | bytes 688136 | tf_op jit(solution)/shard_map/ppermute | solution.py:24
  6.8 9.3 %collective-permute-start.2 = (f32[128,128]{1,0:T(8,128)S(1)}, f32[128,128]{1,0:T(8,128)S(1)}, u32[]{:S(2)}, u32[]{:S(2)}) collective-permute-start(f32[128,128]{1,0:T(8,128)S(1)} %get-tuple-element.27), channel_id=1, source_target_pairs={{2,0},{4,2},{6,4},{8,6},{10,8},{12,10},{14,12},{16,14},{18,16},{20... | collective-permute-start | bytes 196616 | tf_op jit(solution)/shard_map/ppermute | solution.py:24
  8.1 15.3 %collective-permute-start = (f32[6,128,128]{2,1,0:T(8,128)S(1)}, f32[6,128,128]{2,1,0:T(8,128)S(1)}, u32[]{:S(2)}, u32[]{:S(2)}) collective-permute-start(f32[6,128,128]{2,1,0:T(8,128)S(1)} %get-tuple-element.22), channel_id=1, source_target_pairs={{2,0},{4,2},{6,4},{8,6},{10,8},{12,10},{14,12},{16,14},{18,16},{20... | collective-permute-start | bytes 1179656 | tf_op jit(solution)/shard_map/ppermute | solution.py:24
  16.2 1.4 %collective-permute-start.3 = (f32[192,128]{1,0:T(8,128)S(1)}, f32[192,128]{1,0:T(8,128)S(1)}, u32[]{:S(2)}, u32[]{:S(2)}) collective-permute-start(f32[192,128]{1,0:T(8,128)S(1)} %pad_maximum_fusion.refs_0_), channel_id=1, source_target_pairs={{0,1},{1,0},{2,3},{3,2},{4,5},{5,4},{6,7},{7,6},{8,9},{9,8},{10,11... | collective-permute-start | bytes 294920 | tf_op jit(solution)/shard_map/ppermute | solution.py:24
  19.0 13.1 %collective-permute-start.4 = (f32[3,128,128]{2,1,0:T(8,128)S(1)}, f32[3,128,128]{2,1,0:T(8,128)S(1)}, u32[]{:S(2)}, u32[]{:S(2)}) collective-permute-start(f32[3,128,128]{2,1,0:T(8,128)S(1)} %get-tuple-element.38), channel_id=1, source_target_pairs={{2,0},{4,2},{6,4},{8,6},{10,8},{12,10},{14,12},{16,14},{18,16},{20... | collective-permute-start | bytes 589832 | tf_op jit(solution)/shard_map/ppermute | solution.py:24
  23.4 8.7 %copy-start = (f32[1,3,2,128,128]{4,3,2,1,0:T(8,128)S(1)}, f32[1,3,2,128,128]{4,3,2,1,0:T(8,128)}, u32[]{:S(2)}) copy-start(f32[1,3,2,128,128]{4,3,2,1,0:T(8,128)} %disp_ref.1) | copy-start | bytes 1179652
  26.5 12.7 %all-to-all-start = ((f32[32,1,128]{2,1,0:T(1,128)}), f32[32,1,128]{2,1,0:T(1,128)S(1)}, u32[]{:S(2)}, u32[]{:S(2)}) async-start(f32[32,1,128]{2,1,0:T(1,128)} %bitcast.2), calls=%async_computation | async-start | bytes 32768 | tf_op jit(solution)/shard_map/all_to_all | solution.py:493
  39.2 1.4 %collective-permute-start.5 = (f32[2,2,64,128]{3,2,1,0:T(8,128)S(1)}, f32[2,2,64,128]{3,2,1,0:T(8,128)S(1)}, u32[]{:S(2)}, u32[]{:S(2)}) collective-permute-start(f32[2,2,64,128]{3,2,1,0:T(8,128)S(1)} %get-tuple-element.42), channel_id=1, source_target_pairs={{0,1},{1,0},{2,3},{3,2},{4,5},{5,4},{6,7},{7,6},{8,9},{9,8},{10,11... | collective-permute-start | bytes 393224 | tf_op jit(solution)/shard_map/ppermute | solution.py:24

commit v5 on v4

--- a/solution.py
+++ b/solution.py
@@ -347,7 +347,26 @@
     return out
 
 
-def term_kernel(load_ref, z_ref, top_ref, low_v_ref, v_ref, disp_ref, above_ref, scale_ref, term_ref):
+def early_kernel(z_ref, disp_ref, scale_ref, early_ref):
+    layers, height, width = early_ref.shape
+    count = min(ROWS, height)
+    for block in range(height // count):
+        start = block * count
+        low = None
+        for plane in range(layers + 1):
+            last = block == height // count - 1
+            u = edge_modes(disp_ref, lambda comp: (0, comp, plane), block, count, last)
+            high = (plane_modes(z_ref, (plane,), start, count), u)
+            if plane > 0:
+                z, u = [layer_modes(one, two) for one, two in zip(low, high)]
+                rows = slice(start, start + count)
+                early_ref[plane - 1, rows, :] = scale_ref[plane - 1, rows, :] * paired(z, stiff(u))
+            low = high
+
+
+def term_kernel(
+    load_ref, early_ref, z_ref, top_ref, low_v_ref, v_ref, disp_ref, above_ref, scale_ref, term_ref
+):
     layers, height, width = scale_ref.shape
     loads, share = term_ref.shape[0], term_ref.shape[3]
     for block in range(loads):
@@ -355,23 +374,30 @@
         place = lax.rem(block - load_ref[0] + loads, loads)
         low = None
         for plane in range(layers + 1):
+            z = None
+            if plane == layers - 1:
+                z = plane_modes(z_ref, (plane,), start, share)
+            if plane == layers:
+                z = plane_modes(top_ref, (), start, share)
             if plane < layers:
-                z = plane_modes(z_ref, (plane,), start, share)
                 u = edge_modes(disp_ref, lambda comp: (0, comp, plane), block, share, block == loads - 1)
             else:
-                z = plane_modes(top_ref, (), start, share)
                 u = edge_modes(above_ref, lambda comp: (comp,), block, share, block == loads - 1)
             if plane < layers - 1:
                 v = plane_modes(low_v_ref, (plane,), start, share)
             else:
                 v = plane_modes(v_ref, (plane - layers + 1,), start, share)
-            high = [z, v, u]
+            high = [v, u, z]
             if plane > 0:
-                z, v, u = [layer_modes(one, two) for one, two in zip(low, high)]
+                layer = plane - 1
+                scale = scale_ref[layer, start : start + share, :]
+                v, u = [layer_modes(one, two) for one, two in zip(low[:2], high[:2])]
                 forces = stiff(u)
-                scale = scale_ref[plane - 1, start : start + share, :]
-                term_ref[place, 0, plane - 1] = scale * paired(z, forces)
-                term_ref[place, 1, plane - 1] = scale * paired(v, forces)
+                if plane < layers:
+                    term_ref[place, 0, layer] = early_ref[layer, start : start + share, :]
+                else:
+                    term_ref[place, 0, layer] = scale * paired(layer_modes(low[2], z), forces)
+                term_ref[place, 1, layer] = scale * paired(v, forces)
             low = high
 
 
@@ -389,22 +415,24 @@
     return first + second * (first * across / along), second * first
 
 
-def disp_kernel(loads, load_ref, sums_ref, z_ref, low_v_ref, v_ref, x_ref):
+def disp_kernel(loads, load_ref, sums_ref, z_ref, low_v_ref, v_ref, x_ref, weight_ref):
     layers, height = x_ref.shape[2], x_ref.shape[3]
-    from_z, from_v = solve_weights(sums_ref, load_ref[0], loads)
+    for place in range(loads):
+        weights = solve_weights(sums_ref, lax.rem(load_ref[0] - place + loads, loads), loads)
+        for which, weight in enumerate(weights):
+            weight_ref[2 * place + which] = jnp.broadcast_to(weight, weight_ref.shape[1:])
+    from_z, from_v = weight_ref[0, 0:1, :], weight_ref[1, 0:1, :]
     for comp in range(3):
         for plane in range(layers):
             v = low_v_ref[plane, comp, 0:height] if plane < layers - 1 else v_ref[0, comp, 0:height]
             x_ref[0, comp, plane] = from_z * z_ref[plane, comp, 0:height] - from_v * v
 
 
-def grad_kernel(load_ref, sums_ref, *refs):
+def grad_kernel(weight_ref, *refs):
     term_refs, grad_ref = refs[:-1], refs[-1]
-    loads = len(term_refs)
     total = None
-    for place in range(loads):
-        from_z, from_v = solve_weights(sums_ref, lax.rem(load_ref[0] - place + loads, loads), loads)
-        part = from_z * term_refs[place][0] - from_v * term_refs[place][1]
+    for place, term_ref in enumerate(term_refs):
+        part = weight_ref[2 * place, 0:1, :] * term_ref[0] - weight_ref[2 * place + 1, 0:1, :] * term_ref[1]
         total = part if total is None else total + part
     grad_ref[...] = total
 
@@ -473,7 +501,15 @@
         cost_estimate=pl.CostEstimate(flops=10**9, bytes_accessed=2**10, transcendentals=0),
         name="below",
     )(position, from_below, res, modulus, free, *shared)
-    lowest, low_sums = lax.optimization_barrier((lowest, low_sums))
+    early = pl.pallas_call(
+        early_kernel,
+        out_shape=f32(layers - 1, height, width),
+        in_specs=[whole] * 3,
+        out_specs=whole,
+        compiler_params=params,
+        name="early",
+    )(z, forward_disp, scale)
+    lowest, early = lax.optimization_barrier((lowest, early))
     above_disp = permute(lowest, "space", -1)
 
     top, v, sums = pl.pallas_call(
@@ -495,30 +531,30 @@
     terms = pl.pallas_call(
         term_kernel,
         out_shape=f32(loads, 2, layers, share, width),
-        in_specs=[scalar] + [whole] * 7,
+        in_specs=[scalar] + [whole] * 8,
         out_specs=whole,
         compiler_params=params,
         name="term",
-    )(position, z, top, low_v, v, forward_disp, above_disp, scale)
+    )(position, early, z, top, low_v, v, forward_disp, above_disp, scale)
     sums, terms = lax.optimization_barrier((sums, terms))
     terms = [terms[0]] + [permute(terms[by], "load", by, wrap=True) for by in range(1, loads)]
 
-    x = pl.pallas_call(
+    x, weights = pl.pallas_call(
         functools.partial(disp_kernel, loads),
-        out_shape=f32(1, 3, layers, height, width),
+        out_shape=(f32(1, 3, layers, height, width), f32(2 * loads, 8, width)),
         in_specs=[scalar] + [whole] * 4,
-        out_specs=whole,
+        out_specs=[whole] * 2,
         compiler_params=params,
         name="disp",
     )(position, sums, z, low_v, v)
     grad = pl.pallas_call(
         grad_kernel,
         out_shape=f32(layers, share, width),
-        in_specs=[scalar] + [whole] * (1 + loads),
+        in_specs=[whole] * (1 + loads),
         out_specs=whole,
         compiler_params=params,
         name="grad",
-    )(position, sums, *terms)
+    )(weights, *terms)
     return x, grad
 
 

time: 41.6 us -> 40.8 us (0.981)
  starting transfers between devices: 14.5 us -> 13.8 us
  waiting for transfers between devices: 16.8 us -> 16.3 us
    ppermute x6, waiting for transfers between devices: 11.6 us -> 10.8 us  [permute(): return lax.ppermute(shard, axis, pairs)]
    pallas_call x1 -> x2, Pallas kernels: 0.9 us -> 1.63 us  [the longest x1 0.91 us: shards(): pl.pallas_call(functools.partial(disp_kernel, loads), out_shape=(f32(1, 3...]
    all_to_all x1, starting transfers between devices: 5.6 us -> 4.89 us  [shards(): sums = lax.all_to_all(sums, ('space', 'load'), 0, 0, tiled=True)]
  transfers between devices with their start and end apart: 7 -> 7, of which waited for: 6 -> 6; matrix products, arithmetic and copies ran while one was open for 0% -> 0% of each run, Pallas kernels for 18% -> 19%
where the time goes in v5:
time: 40.8 us; the launch traced here: 40.6 us
  waiting for transfers between devices  16.3 us (40%)
  starting transfers between devices  13.8 us (34%)
  Pallas kernels  9.78 us (24%)
  between operations  0.74 us (2%)
    ppermute x6, waiting for transfers between devices, permute(): return lax.ppermute(shard, axis, pairs)  10.8 us
    ppermute x6, starting transfers between devices, permute(): return lax.ppermute(shard, axis, pairs)  8.87 us
    all_to_all x1, waiting for transfers between devices, shards(): sums = lax.all_to_all(sums, ('space', 'load'), 0, 0, tiled=True)  5.44 us
    all_to_all x1, starting transfers between devices, shards(): sums = lax.all_to_all(sums, ('space', 'load'), 0, 0, tiled=True)  4.89 us
    pallas_call x1, Pallas kernels, shards(): pl.pallas_call(above_kernel, out_shape=(f32(3, pad, width), f32(2, 3, pad...  3.1 us
    pallas_call x1, Pallas kernels, shards(): pl.pallas_call(term_kernel, out_shape=f32(loads, 2, layers, share, width)...  1.62 us
    pallas_call x1, Pallas kernels, shards(): pl.pallas_call(below_kernel, out_shape=(f32(layers, 3, pad, width), f32(l...  1.46 us
    pallas_call x1, Pallas kernels, shards(): pl.pallas_call(pack_kernel, out_shape=[f32(3 * height + share, width), f3...  1.32 us
  transfers between devices with their start and end apart: 7, of which 6 were waited for; matrix products, arithmetic and copies ran while one was open for 0% of the time, Pallas kernels for 19%

profile of v5, /device:TPU:0, one launch (start us, length us, event | category | flops | bytes accessed | tf_op | source)
XLA Modules:
  0.0 40.6 jit_solution(9334778126432313837)
XLA Ops:
  0.6 1.3 %pack.1 = (f32[448,128]{1,0:T(8,128)S(1)}, f32[128,128]{1,0:T(8,128)S(1)}, f32[6,128,128]{2,1,0:T(8,128)S(1)}, f32[3,128,128]{2,1,0:T(8,128)S(1)}, f32[3,2,128,1...) custom-call(s32[1]{0:T(128)} %bitcast.load_ref, ...), custom_call_target="tpu_custom_call" | custom-call | tf_op jit(solution)/shard_map/pack/pallas_call | solution.py:460
  2.0 4.9 %collective-permute-start.1 = (f32[448,128]{1,0:T(8,128)S(1)}, f32[448,128]{1,0:T(8,128)S(1)}, u32[]{:S(2)}, u32[]{:S(2)}) collective-permute-start(f32[448,128]{1,0:T(8,128)S(1)} %get-tuple-element.25), channel_id=1, source_target_pairs={{0,2},{2,4},{4,6},{6,8},{8,10},{10,12},{12,14},{14,16},{16,18},{18... | collective-permute-start | bytes 688136 | tf_op jit(solution)/shard_map/ppermute | solution.py:24
  6.8 1.3 %collective-permute-start.2 = (f32[128,128]{1,0:T(8,128)S(1)}, f32[128,128]{1,0:T(8,128)S(1)}, u32[]{:S(2)}, u32[]{:S(2)}) collective-permute-start(f32[128,128]{1,0:T(8,128)S(1)} %get-tuple-element.29), channel_id=1, source_target_pairs={{2,0},{4,2},{6,4},{8,6},{10,8},{12,10},{14,12},{16,14},{18,16},{20... | collective-permute-start | bytes 196616 | tf_op jit(solution)/shard_map/ppermute | solution.py:24
  8.1 1.3 %collective-permute-start = (f32[6,128,128]{2,1,0:T(8,128)S(1)}, f32[6,128,128]{2,1,0:T(8,128)S(1)}, u32[]{:S(2)}, u32[]{:S(2)}) collective-permute-start(f32[6,128,128]{2,1,0:T(8,128)S(1)} %get-tuple-element.24), channel_id=1, source_target_pairs={{2,0},{4,2},{6,4},{8,6},{10,8},{12,10},{14,12},{16,14},{18,16},{20... | collective-permute-start | bytes 1179656 | tf_op jit(solution)/shard_map/ppermute | solution.py:24
  9.4 2.2 %collective-permute-done.1.up_ref = f32[448,128]{1,0:T(8,128)S(1)} collective-permute-done((f32[448,128]{1,0:T(8,128)S(1)}, f32[448,128]{1,0:T(8,128)S(1)}, u32[]{:S(2)}, u32[]{:S(2)}) %collective-permute-start.1) | collective-permute-done | bytes 229408 | tf_op jit(solution)/shard_map/ppermute | solution.py:24
  11.7 4.5 %collective-permute-done.2 = f32[128,128]{1,0:T(8,128)S(1)} collective-permute-done((f32[128,128]{1,0:T(8,128)S(1)}, f32[128,128]{1,0:T(8,128)S(1)}, u32[]{:S(2)}, u32[]{:S(2)}) %collective-permute-start.2) | collective-permute-done | bytes 65568 | tf_op jit(solution)/shard_map/ppermute | solution.py:24
  16.2 0.1 collective-permute-start.3
  16.2 1.3 %collective-permute-done.3.refs_1_ = f32[192,128]{1,0:T(8,128)S(1)} collective-permute-done((f32[192,128]{1,0:T(8,128)S(1)}, f32[192,128]{1,0:T(8,128)S(1)}, u32[]{:S(2)}, u32[]{:S(2)}) %collective-permute-start.3) | collective-permute-done | bytes 98336 | tf_op jit(solution)/shard_map/ppermute | solution.py:24
  17.5 0.0 copy-start
  17.5 1.5 %below.1 = (f32[2,3,136,128]{3,2,1,0:T(8,128)S(1)}, f32[1,3,136,128]{3,2,1,0:T(8,128)S(1)}, f32[3,128,128]{2,1,0:T(8,128)S(1)}, f32[2,128,128]{2,1,0:T(8,128)S(1)}, f32[8,128]{1,0:T(8,128)S(1)}) custom-call(s32[1]{0:T(128)} %bitcast.load_ref, f32[448,128]{1,0:T(8,128)S(1)} %collective-permute-done.1.up_ref, ...), custom_call_target="tpu_custom_call" | custom-call | flops 1000000000 | bytes 1024 | tf_op jit(solution)/shard_map/below/pallas_call | solution.py:484
  19.0 0.0 copy-done
  19.0 0.7 %early.1.early_ref = f32[1,128,128]{2,1,0:T(8,128)S(1)} custom-call(f32[2,3,136,128]{3,2,1,0:T(8,128)S(1)} %get-tuple-element.30.z_ref, f32[1,3,2,128,128]{4,3,2,1,0:T(8,128)S(1)} %copy-done, f32[2,128,128]{2,1,0:T(8,128)S(1)} %get-tuple-element.37.scale_ref), custom_call_target="tpu_custom_call" | custom-call | tf_op jit(solution)/shard_map/early/pallas_call | solution.py:504
  19.7 1.3 %collective-permute-start.4 = (f32[3,128,128]{2,1,0:T(8,128)S(1)}, f32[3,128,128]{2,1,0:T(8,128)S(1)}, u32[]{:S(2)}, u32[]{:S(2)}) collective-permute-start(f32[3,128,128]{2,1,0:T(8,128)S(1)} %get-tuple-element.41), channel_id=1, source_target_pairs={{2,0},{4,2},{6,4},{8,6},{10,8},{12,10},{14,12},{16,14},{18,16},{20... | collective-permute-start | bytes 589832 | tf_op jit(solution)/shard_map/ppermute | solution.py:24
  21.0 2.4 %collective-permute-done.down_ref = f32[6,128,128]{2,1,0:T(8,128)S(1)} collective-permute-done((f32[6,128,128]{2,1,0:T(8,128)S(1)}, f32[6,128,128]{2,1,0:T(8,128)S(1)}, u32[]{:S(2)}, u32[]{:S(2)}) %collective-permute-start) | collective-permute-done | bytes 393248 | tf_op jit(solution)/shard_map/ppermute | solution.py:24
  23.4 3.1 %above.1 = (f32[3,136,128]{2,1,0:T(8,128)S(1)}, f32[2,3,136,128]{3,2,1,0:T(8,128)S(1)}, f32[32,128]{1,0:T(8,128)}) custom-call(s32[1]{0:T(128)} %bitcast.load_ref, f32[6,128,128]{2,1,0:T(8,128)S(1)} %collective-permute-done.down_ref, f32[2,3,136,128]{3,2,1,0:T(8,128)S(1)} %get-tuple-element.30.z_ref, f32[1,3,136,128]{3,2,1,0:T(8,128)S(1)} %get-tuple-element.31.low_v_ref, ...), custom_call_target="tpu_custom_call" | custom-call | tf_op jit(solution)/shard_map/above/pallas_call | solution.py:515
  26.5 4.9 %all-to-all-start = ((f32[32,1,128]{2,1,0:T(1,128)}), f32[32,1,128]{2,1,0:T(1,128)S(1)}, u32[]{:S(2)}, u32[]{:S(2)}) async-start(f32[32,1,128]{2,1,0:T(1,128)} %bitcast.2), calls=%async_computation | async-start | bytes 32768 | tf_op jit(solution)/shard_map/all_to_all | solution.py:529
  31.4 0.0 collective-permute-done.4.above_ref
  31.4 1.6 %term.1 = f32[2,2,2,64,128]{4,3,2,1,0:T(8,128)S(1)} custom-call(s32[1]{0:T(128)} %bitcast.load_ref, f32[1,128,128]{2,1,0:T(8,128)S(1)} %early.1.early_ref, f32[2,3,136,128]{3,2,1,0:T(8,128)S(1)} %get-tuple-element.30.z_ref, f32[3,136,128]{2,1,0:T(8,128)S(1)} %get-tuple-element.39.top_ref, f32[1,3,136,128]{3,2,1,0:T(8,128)S(1)} %get-tuple-element.31.low_v_ref, ...), custom_call_target="tpu_custom_call" | custom-call | tf_op jit(solution)/shard_map/term/pallas_call | solution.py:531
  33.1 5.4 %all-to-all-done = f32[32,1,128]{2,1,0:T(1,128)S(1)} async-done(((f32[32,1,128]{2,1,0:T(1,128)}), f32[32,1,128]{2,1,0:T(1,128)S(1)}, u32[]{:S(2)}, u32[]{:S(2)}) %all-to-all-start) | async-done | bytes 16416 | tf_op jit(solution)/shard_map/all_to_all | solution.py:529
  38.5 0.1 collective-permute-start.5
  38.6 0.9 %disp.1 = (f32[1,3,2,128,128]{4,3,2,1,0:T(8,128)}, f32[4,8,128]{2,1,0:T(8,128)S(1)}) custom-call(s32[1]{0:T(128)} %bitcast.load_ref, f32[32,128]{1,0:T(8,128)S(1)} %bitcast.9, f32[2,3,136,128]{3,2,1,0:T(8,128)S(1)} %get-tuple-element.30.z_ref, f32[1,3,136,128]{3,2,1,0:T(8,128)S(1)} %get-tuple-element.31.low_v_ref, f32[2,3,136,128]{3,2,1,0:T(8,128)S(1)} %get-tuple-element.40.v_ref), custom_call_target="tpu_custom_call" | custom-call | tf_op jit(solution)/shard_map/disp/pallas_call | solution.py:542
  39.5 0.4 %collective-permute-done.5.refs_1_ = f32[2,2,64,128]{3,2,1,0:T(8,128)S(1)} collective-permute-done((f32[2,2,64,128]{3,2,1,0:T(8,128)S(1)}, f32[2,2,64,128]{3,2,1,0:T(8,128)S(1)}, u32[]{:S(2)}, u32[]{:S(2)}) %collective-permute-start.5) | collective-permute-done | bytes 131104 | tf_op jit(solution)/shard_map/ppermute | solution.py:24
  39.9 0.7 %grad.1 = f32[2,64,128]{2,1,0:T(8,128)} custom-call(f32[4,8,128]{2,1,0:T(8,128)S(1)} %get-tuple-element.44.weight_ref, f32[2,2,64,128]{3,2,1,0:T(8,128)S(1)} %get-tuple-element.47.refs_0_, f32[2,2,64,128]{3,2,1,0:T(8,128)S(1)} %collective-permute-done.5.refs_1_), custom_call_target="tpu_custom_call" | custom-call | tf_op jit(solution)/shard_map/grad/pallas_call | solution.py:550
  (3 shorter events, 0.0 us)
Async XLA Ops:
  2.0 9.7 %collective-permute-start.1 = (f32[448,128]{1,0:T(8,128)S(1)}, f32[448,128]{1,0:T(8,128)S(1)}, u32[]{:S(2)}, u32[]{:S(2)}) collective-permute-start(f32[448,128]{1,0:T(8,128)S(1)} %get-tuple-element.25), channel_id=1, source_target_pairs={{0,2},{2,4},{4,6},{6,8},{8,10},{10,12},{12,14},{14,16},{16,18},{18... | collective-permute-start | bytes 688136 | tf_op jit(solution)/shard_map/ppermute | solution.py:24
  6.8 9.3 %collective-permute-start.2 = (f32[128,128]{1,0:T(8,128)S(1)}, f32[128,128]{1,0:T(8,128)S(1)}, u32[]{:S(2)}, u32[]{:S(2)}) collective-permute-start(f32[128,128]{1,0:T(8,128)S(1)} %get-tuple-element.29), channel_id=1, source_target_pairs={{2,0},{4,2},{6,4},{8,6},{10,8},{12,10},{14,12},{16,14},{18,16},{20... | collective-permute-start | bytes 196616 | tf_op jit(solution)/shard_map/ppermute | solution.py:24
  8.1 15.3 %collective-permute-start = (f32[6,128,128]{2,1,0:T(8,128)S(1)}, f32[6,128,128]{2,1,0:T(8,128)S(1)}, u32[]{:S(2)}, u32[]{:S(2)}) collective-permute-start(f32[6,128,128]{2,1,0:T(8,128)S(1)} %get-tuple-element.24), channel_id=1, source_target_pairs={{2,0},{4,2},{6,4},{8,6},{10,8},{12,10},{14,12},{16,14},{18,16},{20... | collective-permute-start | bytes 1179656 | tf_op jit(solution)/shard_map/ppermute | solution.py:24
  16.2 1.4 %collective-permute-start.3 = (f32[192,128]{1,0:T(8,128)S(1)}, f32[192,128]{1,0:T(8,128)S(1)}, u32[]{:S(2)}, u32[]{:S(2)}) collective-permute-start(f32[192,128]{1,0:T(8,128)S(1)} %pad_maximum_fusion.refs_0_), channel_id=1, source_target_pairs={{0,1},{1,0},{2,3},{3,2},{4,5},{5,4},{6,7},{7,6},{8,9},{9,8},{10,11... | collective-permute-start | bytes 294920 | tf_op jit(solution)/shard_map/ppermute | solution.py:24
  17.5 1.5 %copy-start = (f32[1,3,2,128,128]{4,3,2,1,0:T(8,128)S(1)}, f32[1,3,2,128,128]{4,3,2,1,0:T(8,128)}, u32[]{:S(2)}) copy-start(f32[1,3,2,128,128]{4,3,2,1,0:T(8,128)} %disp_ref.3) | copy-start | bytes 1179652
  19.7 11.7 %collective-permute-start.4 = (f32[3,128,128]{2,1,0:T(8,128)S(1)}, f32[3,128,128]{2,1,0:T(8,128)S(1)}, u32[]{:S(2)}, u32[]{:S(2)}) collective-permute-start(f32[3,128,128]{2,1,0:T(8,128)S(1)} %get-tuple-element.41), channel_id=1, source_target_pairs={{2,0},{4,2},{6,4},{8,6},{10,8},{12,10},{14,12},{16,14},{18,16},{20... | collective-permute-start | bytes 589832 | tf_op jit(solution)/shard_map/ppermute | solution.py:24
  26.5 12.0 %all-to-all-start = ((f32[32,1,128]{2,1,0:T(1,128)}), f32[32,1,128]{2,1,0:T(1,128)S(1)}, u32[]{:S(2)}, u32[]{:S(2)}) async-start(f32[32,1,128]{2,1,0:T(1,128)} %bitcast.2), calls=%async_computation | async-start | bytes 32768 | tf_op jit(solution)/shard_map/all_to_all | solution.py:529
  38.5 1.4 %collective-permute-start.5 = (f32[2,2,64,128]{3,2,1,0:T(8,128)S(1)}, f32[2,2,64,128]{3,2,1,0:T(8,128)S(1)}, u32[]{:S(2)}, u32[]{:S(2)}) collective-permute-start(f32[2,2,64,128]{3,2,1,0:T(8,128)S(1)} %get-tuple-element.46), channel_id=1, source_target_pairs={{0,1},{1,0},{2,3},{3,2},{4,5},{5,4},{6,7},{7,6},{8,9},{9,8},{10,11... | collective-permute-start | bytes 393224 | tf_op jit(solution)/shard_map/ppermute | solution.py:24

commit v6 on v5

--- a/solution.py
+++ b/solution.py
@@ -262,30 +262,21 @@
     sums_ref[...] = add_up((norm, along, across))
 
 
-def above_kernel(load_ref, down_ref, z_ref, low_v_ref, part_ref, inv_ref, mod_ref, low_sums_ref, *refs):
-    top_ref, v_ref, sums_ref, over, carry, edge, inv = refs[-7:]
-    shared = refs[:-7]
+def above_kernel(
+    down_ref, z_ref, low_v_ref, part_ref, inv_ref, mod_ref, low_sums_ref, inv_top_ref, mod_top_ref,
+    top_ref, v_ref, sums_ref, over, carry,
+):
     layers, height, width = mod_ref.shape
-    count = min(ROWS, height // len(shared))
-    edge[0:8, :] = jnp.zeros((8, width), jnp.float32)
+    count = min(ROWS, height)
     carry[:, :, 0:8, :] = jnp.zeros((2, 3, 8, width), jnp.float32)
     over[:, height : height + 8, :] = jnp.zeros((3, 8, width), jnp.float32)
     top_ref[:, height : height + 8, :] = jnp.zeros((3, 8, width), jnp.float32)
     v_ref[:, :, height : height + 8, :] = jnp.zeros((2, 3, 8, width), jnp.float32)
     zero = jnp.zeros((count, width), jnp.float32)
 
-    def start_block(block, _):
-        start = pl.multiple_of(block * count, count)
-        rows = pl.ds(start, count)
-        total = mod_ref[layers - 1, rows, :] + received(shared, 1, load_ref[0], start, count)
-        inverse = inverse_diagonal(received(shared, 2, load_ref[0], start, count), total, edge, start, count)
-        inv[rows, :] = inverse
-        for comp in range(3):
-            top_ref[comp, rows, :] = inverse * down_ref[comp, rows, :]
-            over[comp, rows, :] = down_ref[3 + comp, rows, :]
-        return 0
-
-    lax.fori_loop(0, height // count, start_block, 0)
+    for comp in range(3):
+        top_ref[comp, 0:height, :] = inv_top_ref[...] * down_ref[comp]
+        over[comp, 0:height, :] = down_ref[3 + comp]
 
     def image_block(block, sums):
         along, across = sums
@@ -300,11 +291,10 @@
             v_ref[0, comp, rows, :] = v
             along = along + image * z_ref[layers - 1, comp, rows, :]
             across = across + image * v
-        stiffness = received(shared, 1, load_ref[0], start, count)
-        lower, _ = layer_forces(high, plane_modes(over, (), start, count), stiffness)
+        lower, _ = layer_forces(high, plane_modes(over, (), start, count), mod_top_ref[rows, :])
         lower = {key: lower[key] + held[key] for key in lower}
         for comp in range(3):
-            v_ref[1, comp, rows, :] = inv[rows, :] * nodal(lower, comp, carry.at[1], start, count)
+            v_ref[1, comp, rows, :] = inv_top_ref[rows, :] * nodal(lower, comp, carry.at[1], start, count)
         return along, across
 
     along, across = lax.fori_loop(0, height // count, image_block, (zero, zero))
@@ -347,58 +337,79 @@
     return out
 
 
-def early_kernel(z_ref, disp_ref, scale_ref, early_ref):
-    layers, height, width = early_ref.shape
+def dot(modes, forces):
+    total = None
+    for comp in range(3):
+        for a in range(2):
+            for b in range(2):
+                term = modes[comp][a][b] * forces[comp, a, b]
+                total = term if total is None else total + term
+    return total
+
+
+def early_kernel(load_ref, z_ref, low_v_ref, disp_ref, scale_ref, mod_ref, *refs):
+    early_ref, upper_ref, inv_top_ref, mod_top_ref, edge = refs[-5:]
+    shared = refs[:-5]
+    layers, height, width = scale_ref.shape
+    share = height // len(shared)
+    edge[0:8, :] = jnp.zeros((8, width), jnp.float32)
+    for start in range(0, height, share):
+        rows = slice(start, start + share)
+        stiffness = received(shared, 1, load_ref[0], start, share)
+        free = received(shared, 2, load_ref[0], start, share)
+        mod_top_ref[rows, :] = stiffness
+        total = mod_ref[layers - 1, rows, :] + stiffness
+        inv_top_ref[rows, :] = inverse_diagonal(free, total, edge, start, share)
     count = min(ROWS, height)
     for block in range(height // count):
         start = block * count
+        rows = slice(start, start + count)
         low = None
-        for plane in range(layers + 1):
+        for plane in range(layers):
             last = block == height // count - 1
             u = edge_modes(disp_ref, lambda comp: (0, comp, plane), block, count, last)
-            high = (plane_modes(z_ref, (plane,), start, count), u)
+            z = plane_modes(z_ref, (plane,), start, count)
+            v = plane_modes(low_v_ref, (plane,), start, count) if plane < layers - 1 else None
             if plane > 0:
-                z, u = [layer_modes(one, two) for one, two in zip(low, high)]
-                rows = slice(start, start + count)
-                early_ref[plane - 1, rows, :] = scale_ref[plane - 1, rows, :] * paired(z, stiff(u))
-            low = high
+                layer = plane - 1
+                lower, upper = layer_forces(low[0], u, scale_ref[layer, rows, :])
+                early_ref[0, layer, rows, :] = dot(low[1], lower) + dot(z, upper)
+                part = dot(low[2], lower)
+                if plane < layers - 1:
+                    part = part + dot(v, upper)
+                else:
+                    for place, key in enumerate(sorted(upper)):
+                        upper_ref[place, rows, :] = upper[key]
+                early_ref[1, layer, rows, :] = part
+            low = (u, z, v)
 
 
 def term_kernel(
-    load_ref, early_ref, z_ref, top_ref, low_v_ref, v_ref, disp_ref, above_ref, scale_ref, term_ref
+    load_ref, early_ref, upper_ref, z_ref, top_ref, v_ref, disp_ref, above_ref, scale_ref, term_ref
 ):
     layers, height, width = scale_ref.shape
     loads, share = term_ref.shape[0], term_ref.shape[3]
+    keys = [(comp, a, b) for comp in range(3) for a in range(2) for b in range(2)]
     for block in range(loads):
         start = block * share
+        rows = slice(start, start + share)
         place = lax.rem(block - load_ref[0] + loads, loads)
-        low = None
-        for plane in range(layers + 1):
-            z = None
-            if plane == layers - 1:
-                z = plane_modes(z_ref, (plane,), start, share)
-            if plane == layers:
-                z = plane_modes(top_ref, (), start, share)
-            if plane < layers:
-                u = edge_modes(disp_ref, lambda comp: (0, comp, plane), block, share, block == loads - 1)
-            else:
-                u = edge_modes(above_ref, lambda comp: (comp,), block, share, block == loads - 1)
-            if plane < layers - 1:
-                v = plane_modes(low_v_ref, (plane,), start, share)
-            else:
-                v = plane_modes(v_ref, (plane - layers + 1,), start, share)
-            high = [v, u, z]
-            if plane > 0:
-                layer = plane - 1
-                scale = scale_ref[layer, start : start + share, :]
-                v, u = [layer_modes(one, two) for one, two in zip(low[:2], high[:2])]
-                forces = stiff(u)
-                if plane < layers:
-                    term_ref[place, 0, layer] = early_ref[layer, start : start + share, :]
-                else:
-                    term_ref[place, 0, layer] = scale * paired(layer_modes(low[2], z), forces)
-                term_ref[place, 1, layer] = scale * paired(v, forces)
-            low = high
+        z_low = plane_modes(z_ref, (layers - 1,), start, share)
+        v_low = plane_modes(v_ref, (0,), start, share)
+        for layer in range(layers - 1):
+            term_ref[place, 0, layer] = early_ref[0, layer, rows, :]
+            part = early_ref[1, layer, rows, :]
+            if layer == layers - 2:
+                part = part + dot(v_low, {key: upper_ref[at, rows, :] for at, key in enumerate(keys)})
+            term_ref[place, 1, layer] = part
+        last = block == loads - 1
+        u_low = edge_modes(disp_ref, lambda comp: (0, comp, layers - 1), block, share, last)
+        u_high = edge_modes(above_ref, lambda comp: (comp,), block, share, last)
+        lower, upper = layer_forces(u_low, u_high, scale_ref[layers - 1, rows, :])
+        z_high = plane_modes(top_ref, (), start, share)
+        term_ref[place, 0, layers - 1] = dot(z_low, lower) + dot(z_high, upper)
+        v_high = plane_modes(v_ref, (1,), start, share)
+        term_ref[place, 1, layers - 1] = dot(v_low, lower) + dot(v_high, upper)
 
 
 def solve_weights(sums_ref, load, loads):
@@ -415,21 +426,22 @@
     return first + second * (first * across / along), second * first
 
 
-def disp_kernel(loads, load_ref, sums_ref, z_ref, low_v_ref, v_ref, x_ref, weight_ref):
-    layers, height = x_ref.shape[2], x_ref.shape[3]
+def weight_kernel(loads, load_ref, sums_ref, weight_ref):
     for place in range(loads):
         weights = solve_weights(sums_ref, lax.rem(load_ref[0] - place + loads, loads), loads)
         for which, weight in enumerate(weights):
             weight_ref[2 * place + which] = jnp.broadcast_to(weight, weight_ref.shape[1:])
+
+
+def finish_kernel(weight_ref, z_ref, low_v_ref, v_ref, *refs):
+    term_refs = refs[:-2]
+    x_ref, grad_ref = refs[-2:]
+    layers, height = x_ref.shape[2], x_ref.shape[3]
     from_z, from_v = weight_ref[0, 0:1, :], weight_ref[1, 0:1, :]
     for comp in range(3):
         for plane in range(layers):
             v = low_v_ref[plane, comp, 0:height] if plane < layers - 1 else v_ref[0, comp, 0:height]
             x_ref[0, comp, plane] = from_z * z_ref[plane, comp, 0:height] - from_v * v
-
-
-def grad_kernel(weight_ref, *refs):
-    term_refs, grad_ref = refs[:-1], refs[-1]
     total = None
     for place, term_ref in enumerate(term_refs):
         part = weight_ref[2 * place, 0:1, :] * term_ref[0] - weight_ref[2 * place + 1, 0:1, :] * term_ref[1]
@@ -501,31 +513,30 @@
         cost_estimate=pl.CostEstimate(flops=10**9, bytes_accessed=2**10, transcendentals=0),
         name="below",
     )(position, from_below, res, modulus, free, *shared)
-    early = pl.pallas_call(
+    early, upper, inverse_top, modulus_top = pl.pallas_call(
         early_kernel,
-        out_shape=f32(layers - 1, height, width),
-        in_specs=[whole] * 3,
-        out_specs=whole,
+        out_shape=(f32(2, layers - 1, height, width), f32(12, height, width), f32(height, width), f32(height, width)),
+        in_specs=[scalar] + [whole] * (5 + loads),
+        out_specs=[whole] * 4,
+        scratch_shapes=[pltpu.VMEM((pad, width), jnp.float32)],
         compiler_params=params,
         name="early",
-    )(z, forward_disp, scale)
+    )(position, z, low_v, forward_disp, scale, modulus, *shared)
     lowest, early = lax.optimization_barrier((lowest, early))
     above_disp = permute(lowest, "space", -1)
 
     top, v, sums = pl.pallas_call(
         above_kernel,
         out_shape=(f32(3, pad, width), f32(2, 3, pad, width), f32(devices, 128)),
-        in_specs=[scalar] + [whole] * (7 + loads),
+        in_specs=[whole] * 9,
         out_specs=[whole] * 3,
         scratch_shapes=[
             pltpu.VMEM((3, pad, width), jnp.float32),
             pltpu.VMEM((2, 3, pad, width), jnp.float32),
-            pltpu.VMEM((pad, width), jnp.float32),
-            pltpu.VMEM((height, width), jnp.float32),
         ],
         compiler_params=params,
         name="above",
-    )(position, from_above, z, low_v, part, inverse, modulus, low_sums, *shared)
+    )(from_above, z, low_v, part, inverse, modulus, low_sums, inverse_top, modulus_top)
     sums = lax.all_to_all(sums, ("space", "load"), 0, 0, tiled=True)
 
     terms = pl.pallas_call(
@@ -535,27 +546,26 @@
         out_specs=whole,
         compiler_params=params,
         name="term",
-    )(position, early, z, top, low_v, v, forward_disp, above_disp, scale)
-    sums, terms = lax.optimization_barrier((sums, terms))
+    )(position, early, upper, z, top, v, forward_disp, above_disp, scale)
     terms = [terms[0]] + [permute(terms[by], "load", by, wrap=True) for by in range(1, loads)]
 
-    x, weights = pl.pallas_call(
-        functools.partial(disp_kernel, loads),
-        out_shape=(f32(1, 3, layers, height, width), f32(2 * loads, 8, width)),
-        in_specs=[scalar] + [whole] * 4,
+    weights = pl.pallas_call(
+        functools.partial(weight_kernel, loads),
+        out_shape=f32(2 * loads, 8, width),
+        in_specs=[scalar, whole],
+        out_specs=whole,
+        compiler_params=params,
+        cost_estimate=pl.CostEstimate(flops=4 * 10**9, bytes_accessed=2**20, transcendentals=0),
+        name="weight",
+    )(position, sums)
+    return pl.pallas_call(
+        finish_kernel,
+        out_shape=(f32(1, 3, layers, height, width), f32(layers, share, width)),
+        in_specs=[whole] * (4 + loads),
         out_specs=[whole] * 2,
         compiler_params=params,
-        name="disp",
-    )(position, sums, z, low_v, v)
-    grad = pl.pallas_call(
-        grad_kernel,
-        out_shape=f32(layers, share, width),
-        in_specs=[whole] * (1 + loads),
-        out_specs=whole,
-        compiler_params=params,
-        name="grad",
-    )(weights, *terms)
-    return x, grad
+        name="finish",
+    )(weights, z, low_v, v, *terms)
 
 
 def solution(mesh):

time: 40.8 us -> 39.5 us (0.968)
  Pallas kernels: 9.78 us -> 8.75 us
  waiting for transfers between devices: 16.3 us -> 15.7 us
    ppermute x6, waiting for transfers between devices: 10.8 us -> 10.1 us  [permute(): return lax.ppermute(shard, axis, pairs)]
    pallas_call x1, Pallas kernels: 1.62 us -> 1.11 us  [shards(): pl.pallas_call(term_kernel, out_shape=f32(loads, 2, layers, share, width)...]
  transfers between devices with their start and end apart: 7 -> 7, of which waited for: 6 -> 5; matrix products, arithmetic and copies ran while one was open for 0% -> 0% of each run, Pallas kernels for 19% -> 17%
where the time goes in v6:
time: 39.5 us; the launch traced here: 39.2 us
  waiting for transfers between devices  15.7 us (40%)
  starting transfers between devices  14 us (35%)
  Pallas kernels  8.75 us (22%)
  between operations  0.75 us (2%)
    ppermute x6, waiting for transfers between devices, permute(): return lax.ppermute(shard, axis, pairs)  10.1 us
    ppermute x6, starting transfers between devices, permute(): return lax.ppermute(shard, axis, pairs)  9.12 us
    all_to_all x1, waiting for transfers between devices, shards(): sums = lax.all_to_all(sums, ('space', 'load'), 0, 0, tiled=True)  5.6 us
    all_to_all x1, starting transfers between devices, shards(): sums = lax.all_to_all(sums, ('space', 'load'), 0, 0, tiled=True)  4.89 us
    pallas_call x1, Pallas kernels, shards(): pl.pallas_call(above_kernel, out_shape=(f32(3, pad, width), f32(2, 3, pad...  2.89 us
    pallas_call x1, Pallas kernels, shards(): pl.pallas_call(below_kernel, out_shape=(f32(layers, 3, pad, width), f32(l...  1.47 us
    pallas_call x1, Pallas kernels, shards(): pl.pallas_call(pack_kernel, out_shape=[f32(3 * height + share, width), f3...  1.32 us
    pallas_call x1, Pallas kernels, shards(): pl.pallas_call(term_kernel, out_shape=f32(loads, 2, layers, share, width)...  1.11 us
  transfers between devices with their start and end apart: 7, of which 5 were waited for; matrix products, arithmetic and copies ran while one was open for 0% of the time, Pallas kernels for 17%

profile of v6, /device:TPU:0, one launch (start us, length us, event | category | flops | bytes accessed | tf_op | source)
XLA Modules:
  0.0 39.2 jit_solution(7964438669363463841)
XLA Ops:
  0.6 1.3 %pack.1 = (f32[448,128]{1,0:T(8,128)S(1)}, f32[128,128]{1,0:T(8,128)S(1)}, f32[6,128,128]{2,1,0:T(8,128)S(1)}, f32[3,128,128]{2,1,0:T(8,128)S(1)}, f32[3,2,128,1...) custom-call(s32[1]{0:T(128)} %bitcast.load_ref, ...), custom_call_target="tpu_custom_call" | custom-call | tf_op jit(solution)/shard_map/pack/pallas_call | solution.py:472
  2.0 4.9 %collective-permute-start.1 = (f32[448,128]{1,0:T(8,128)S(1)}, f32[448,128]{1,0:T(8,128)S(1)}, u32[]{:S(2)}, u32[]{:S(2)}) collective-permute-start(f32[448,128]{1,0:T(8,128)S(1)} %get-tuple-element.25), channel_id=1, source_target_pairs={{0,2},{2,4},{4,6},{6,8},{8,10},{10,12},{12,14},{14,16},{16,18},{18... | collective-permute-start | bytes 688136 | tf_op jit(solution)/shard_map/ppermute | solution.py:24
  6.8 1.3 %collective-permute-start.2 = (f32[128,128]{1,0:T(8,128)S(1)}, f32[128,128]{1,0:T(8,128)S(1)}, u32[]{:S(2)}, u32[]{:S(2)}) collective-permute-start(f32[128,128]{1,0:T(8,128)S(1)} %get-tuple-element.29), channel_id=1, source_target_pairs={{2,0},{4,2},{6,4},{8,6},{10,8},{12,10},{14,12},{16,14},{18,16},{20... | collective-permute-start | bytes 196616 | tf_op jit(solution)/shard_map/ppermute | solution.py:24
  8.1 1.3 %collective-permute-start = (f32[6,128,128]{2,1,0:T(8,128)S(1)}, f32[6,128,128]{2,1,0:T(8,128)S(1)}, u32[]{:S(2)}, u32[]{:S(2)}) collective-permute-start(f32[6,128,128]{2,1,0:T(8,128)S(1)} %get-tuple-element.24), channel_id=1, source_target_pairs={{2,0},{4,2},{6,4},{8,6},{10,8},{12,10},{14,12},{16,14},{18,16},{20... | collective-permute-start | bytes 1179656 | tf_op jit(solution)/shard_map/ppermute | solution.py:24
  9.4 2.2 %collective-permute-done.1.up_ref = f32[448,128]{1,0:T(8,128)S(1)} collective-permute-done((f32[448,128]{1,0:T(8,128)S(1)}, f32[448,128]{1,0:T(8,128)S(1)}, u32[]{:S(2)}, u32[]{:S(2)}) %collective-permute-start.1) | collective-permute-done | bytes 229408 | tf_op jit(solution)/shard_map/ppermute | solution.py:24
  11.7 4.5 %collective-permute-done.2 = f32[128,128]{1,0:T(8,128)S(1)} collective-permute-done((f32[128,128]{1,0:T(8,128)S(1)}, f32[128,128]{1,0:T(8,128)S(1)}, u32[]{:S(2)}, u32[]{:S(2)}) %collective-permute-start.2) | collective-permute-done | bytes 65568 | tf_op jit(solution)/shard_map/ppermute | solution.py:24
  16.2 0.1 collective-permute-start.3
  16.2 1.3 %collective-permute-done.3.refs_1_ = f32[192,128]{1,0:T(8,128)S(1)} collective-permute-done((f32[192,128]{1,0:T(8,128)S(1)}, f32[192,128]{1,0:T(8,128)S(1)}, u32[]{:S(2)}, u32[]{:S(2)}) %collective-permute-start.3) | collective-permute-done | bytes 98336 | tf_op jit(solution)/shard_map/ppermute | solution.py:24
  17.5 0.0 copy-start
  17.5 1.5 %below.1 = (f32[2,3,136,128]{3,2,1,0:T(8,128)S(1)}, f32[1,3,136,128]{3,2,1,0:T(8,128)S(1)}, f32[3,128,128]{2,1,0:T(8,128)S(1)}, f32[2,128,128]{2,1,0:T(8,128)S(1)}, f32[8,128]{1,0:T(8,128)S(1)}) custom-call(s32[1]{0:T(128)} %bitcast.load_ref, f32[448,128]{1,0:T(8,128)S(1)} %collective-permute-done.1.up_ref, ...), custom_call_target="tpu_custom_call" | custom-call | flops 1000000000 | bytes 1024 | tf_op jit(solution)/shard_map/below/pallas_call | solution.py:496
  19.0 0.0 copy-done
  19.0 1.0 %early.1 = (f32[2,1,128,128]{3,2,1,0:T(8,128)S(1)}, f32[12,128,128]{2,1,0:T(8,128)S(1)}, f32[128,128]{1,0:T(8,128)S(1)}, f32[128,128]{1,0:T(8,128)S(1)}) custom-call(s32[1]{0:T(128)} %bitcast.load_ref, f32[2,3,136,128]{3,2,1,0:T(8,128)S(1)} %get-tuple-element.30.z_ref, f32[1,3,136,128]{3,2,1,0:T(8,128)S(1)} %get-tuple-element.31.low_v_ref, ...), custom_call_target="tpu_custom_call" | custom-call | tf_op jit(solution)/shard_map/early/pallas_call | solution.py:516
  20.1 1.3 %collective-permute-start.4 = (f32[3,128,128]{2,1,0:T(8,128)S(1)}, f32[3,128,128]{2,1,0:T(8,128)S(1)}, u32[]{:S(2)}, u32[]{:S(2)}) collective-permute-start(f32[3,128,128]{2,1,0:T(8,128)S(1)} %get-tuple-element.45), channel_id=1, source_target_pairs={{2,0},{4,2},{6,4},{8,6},{10,8},{12,10},{14,12},{16,14},{18,16},{20... | collective-permute-start | bytes 589832 | tf_op jit(solution)/shard_map/ppermute | solution.py:24
  21.4 2.1 %collective-permute-done.down_ref = f32[6,128,128]{2,1,0:T(8,128)S(1)} collective-permute-done((f32[6,128,128]{2,1,0:T(8,128)S(1)}, f32[6,128,128]{2,1,0:T(8,128)S(1)}, u32[]{:S(2)}, u32[]{:S(2)}) %collective-permute-start) | collective-permute-done | bytes 393248 | tf_op jit(solution)/shard_map/ppermute | solution.py:24
  23.4 2.9 %above.1 = (f32[3,136,128]{2,1,0:T(8,128)S(1)}, f32[2,3,136,128]{3,2,1,0:T(8,128)S(1)}, f32[32,128]{1,0:T(8,128)}) custom-call(f32[6,128,128]{2,1,0:T(8,128)S(1)} %collective-permute-done.down_ref, f32[2,3,136,128]{3,2,1,0:T(8,128)S(1)} %get-tuple-element.30.z_ref, f32[1,3,136,128]{3,2,1,0:T(8,128)S(1)} %get-tuple-element.31.low_v_ref, ...), custom_call_target="tpu_custom_call" | custom-call | tf_op jit(solution)/shard_map/above/pallas_call | solution.py:528
  26.3 4.9 %all-to-all-start = ((f32[32,1,128]{2,1,0:T(1,128)}), f32[32,1,128]{2,1,0:T(1,128)S(1)}, u32[]{:S(2)}, u32[]{:S(2)}) async-start(f32[32,1,128]{2,1,0:T(1,128)} %bitcast.2), calls=%async_computation | async-start | bytes 32768 | tf_op jit(solution)/shard_map/all_to_all | solution.py:540
  31.2 0.0 collective-permute-done.4.above_ref
  31.2 1.1 %term.1 = f32[2,2,2,64,128]{4,3,2,1,0:T(8,128)S(1)} custom-call(s32[1]{0:T(128)} %bitcast.load_ref, f32[2,1,128,128]{3,2,1,0:T(8,128)S(1)} %get-tuple-element.42.early_ref, f32[12,128,128]{2,1,0:T(8,128)S(1)} %get-tuple-element.43.upper_ref, f32[2,3,136,128]{3,2,1,0:T(8,128)S(1)} %get-tuple-element.30.z_ref, f32[3,136,128]{2,1,0:T(8,128)S(1)} %get-tuple-element.44.top_ref, ...), custom_call_target="tpu_custom_call" | custom-call | tf_op jit(solution)/shard_map/term/pallas_call | solution.py:542
  32.4 0.3 collective-permute-start.5
  32.7 5.6 %all-to-all-done = f32[32,1,128]{2,1,0:T(1,128)S(1)} async-done(((f32[32,1,128]{2,1,0:T(1,128)}), f32[32,1,128]{2,1,0:T(1,128)S(1)}, u32[]{:S(2)}, u32[]{:S(2)}) %all-to-all-start) | async-done | bytes 16416 | tf_op jit(solution)/shard_map/all_to_all | solution.py:540
  38.3 0.1 weight.1.weight_ref
  38.4 0.0 collective-permute-done.5.refs_1_
  38.4 0.8 %finish.1 = (f32[1,3,2,128,128]{4,3,2,1,0:T(8,128)}, f32[2,64,128]{2,1,0:T(8,128)}) custom-call(f32[4,8,128]{2,1,0:T(8,128)S(1)} %weight.1.weight_ref, f32[2,3,136,128]{3,2,1,0:T(8,128)S(1)} %get-tuple-element.30.z_ref, f32[1,3,136,128]{3,2,1,0:T(8,128)S(1)} %get-tuple-element.31.low_v_ref, f32[2,3,136,128]{3,2,1,0:T(8,128)S(1)} %get-tuple-element.39.v_ref, ...), custom_call_target="tpu_custom_call" | custom-call | tf_op jit(solution)/shard_map/finish/pallas_call | solution.py:561
  (3 shorter events, 0.0 us)
Async XLA Ops:
  2.0 9.7 %collective-permute-start.1 = (f32[448,128]{1,0:T(8,128)S(1)}, f32[448,128]{1,0:T(8,128)S(1)}, u32[]{:S(2)}, u32[]{:S(2)}) collective-permute-start(f32[448,128]{1,0:T(8,128)S(1)} %get-tuple-element.25), channel_id=1, source_target_pairs={{0,2},{2,4},{4,6},{6,8},{8,10},{10,12},{12,14},{14,16},{16,18},{18... | collective-permute-start | bytes 688136 | tf_op jit(solution)/shard_map/ppermute | solution.py:24
  6.8 9.3 %collective-permute-start.2 = (f32[128,128]{1,0:T(8,128)S(1)}, f32[128,128]{1,0:T(8,128)S(1)}, u32[]{:S(2)}, u32[]{:S(2)}) collective-permute-start(f32[128,128]{1,0:T(8,128)S(1)} %get-tuple-element.29), channel_id=1, source_target_pairs={{2,0},{4,2},{6,4},{8,6},{10,8},{12,10},{14,12},{16,14},{18,16},{20... | collective-permute-start | bytes 196616 | tf_op jit(solution)/shard_map/ppermute | solution.py:24
  8.1 15.3 %collective-permute-start = (f32[6,128,128]{2,1,0:T(8,128)S(1)}, f32[6,128,128]{2,1,0:T(8,128)S(1)}, u32[]{:S(2)}, u32[]{:S(2)}) collective-permute-start(f32[6,128,128]{2,1,0:T(8,128)S(1)} %get-tuple-element.24), channel_id=1, source_target_pairs={{2,0},{4,2},{6,4},{8,6},{10,8},{12,10},{14,12},{16,14},{18,16},{20... | collective-permute-start | bytes 1179656 | tf_op jit(solution)/shard_map/ppermute | solution.py:24
  16.2 1.4 %collective-permute-start.3 = (f32[192,128]{1,0:T(8,128)S(1)}, f32[192,128]{1,0:T(8,128)S(1)}, u32[]{:S(2)}, u32[]{:S(2)}) collective-permute-start(f32[192,128]{1,0:T(8,128)S(1)} %pad_maximum_fusion.refs_0_), channel_id=1, source_target_pairs={{0,1},{1,0},{2,3},{3,2},{4,5},{5,4},{6,7},{7,6},{8,9},{9,8},{10,11... | collective-permute-start | bytes 294920 | tf_op jit(solution)/shard_map/ppermute | solution.py:24
  17.5 1.5 %copy-start = (f32[1,3,2,128,128]{4,3,2,1,0:T(8,128)S(1)}, f32[1,3,2,128,128]{4,3,2,1,0:T(8,128)}, u32[]{:S(2)}) copy-start(f32[1,3,2,128,128]{4,3,2,1,0:T(8,128)} %disp_ref.3) | copy-start | bytes 1179652
  20.1 11.2 %collective-permute-start.4 = (f32[3,128,128]{2,1,0:T(8,128)S(1)}, f32[3,128,128]{2,1,0:T(8,128)S(1)}, u32[]{:S(2)}, u32[]{:S(2)}) collective-permute-start(f32[3,128,128]{2,1,0:T(8,128)S(1)} %get-tuple-element.45), channel_id=1, source_target_pairs={{2,0},{4,2},{6,4},{8,6},{10,8},{12,10},{14,12},{16,14},{18,16},{20... | collective-permute-start | bytes 589832 | tf_op jit(solution)/shard_map/ppermute | solution.py:24
  26.3 12.0 %all-to-all-start = ((f32[32,1,128]{2,1,0:T(1,128)}), f32[32,1,128]{2,1,0:T(1,128)S(1)}, u32[]{:S(2)}, u32[]{:S(2)}) async-start(f32[32,1,128]{2,1,0:T(1,128)} %bitcast.2), calls=%async_computation | async-start | bytes 32768 | tf_op jit(solution)/shard_map/all_to_all | solution.py:540
  32.4 6.0 %collective-permute-start.5 = (f32[2,2,64,128]{3,2,1,0:T(8,128)S(1)}, f32[2,2,64,128]{3,2,1,0:T(8,128)S(1)}, u32[]{:S(2)}, u32[]{:S(2)}) collective-permute-start(f32[2,2,64,128]{3,2,1,0:T(8,128)S(1)} %get-tuple-element.46), channel_id=1, source_target_pairs={{0,1},{1,0},{2,3},{3,2},{4,5},{5,4},{6,7},{7,6},{8,9},{9,8},{10,11... | collective-permute-start | bytes 393224 | tf_op jit(solution)/shard_map/ppermute | solution.py:24

commit v7 on v6

--- a/solution.py
+++ b/solution.py
@@ -13,6 +13,12 @@
 CLASS = [0.0] + [12.0 * SHEAR / 64.0 / 3.0**order for order in (1, 2, 3)]
 CORNER = CLASS[1] * (RATIO + 4.0) + CLASS[2] * (2.0 * (RATIO + 3.0) + 2.0) + CLASS[3] * (RATIO + 4.0)
 ROWS = 64
+
+
+def unrolled(low, high, body, carry):
+    for step in range(low, high):
+        carry = body(step, carry)
+    return carry
 
 
 def permute(shard, axis, by, wrap=False):
@@ -144,7 +150,7 @@
 
 def received(shared, item, load, start, count):
     loads, share = len(shared), shared[0].shape[0] // 3
-    rows = pl.ds(pl.multiple_of(item * share + lax.rem(start, share), 8), count)
+    rows = pl.ds(item * share + start % share, count)
     distance = lax.rem(load - start // share + loads, loads)
     out = shared[0][rows, :]
     for by in range(1, loads):
@@ -218,7 +224,7 @@
         return mod_ref[layer, pl.ds(start, count), :]
 
     def start_block(block, norm):
-        start = pl.multiple_of(block * count, count)
+        start = block * count
         rows = pl.ds(start, count)
         for plane in range(layers):
             total = modulus(plane - 1, start) + modulus(plane, start)
@@ -233,11 +239,11 @@
             under[comp, rows, :] = up_ref[pl.ds(comp * height + start, count), :]
         return norm
 
-    norm = lax.fori_loop(0, height // count, start_block, zero)
+    norm = unrolled(0, height // count, start_block, zero)
 
     def image_block(block, sums):
         along, across = sums
-        start = pl.multiple_of(block * count, count)
+        start = block * count
         rows = pl.ds(start, count)
         low = plane_modes(under, (), start, count)
         held = None
@@ -258,7 +264,7 @@
             part_ref[comp, rows, :] = nodal(held, comp, carry.at[layers - 1], start, count)
         return along, across
 
-    along, across = lax.fori_loop(0, height // count, image_block, (zero, zero))
+    along, across = unrolled(0, height // count, image_block, (zero, zero))
     sums_ref[...] = add_up((norm, along, across))
 
 
@@ -267,7 +273,7 @@
     top_ref, v_ref, sums_ref, over, carry,
 ):
     layers, height, width = mod_ref.shape
-    count = min(ROWS, height)
+    count = height
     carry[:, :, 0:8, :] = jnp.zeros((2, 3, 8, width), jnp.float32)
     over[:, height : height + 8, :] = jnp.zeros((3, 8, width), jnp.float32)
     top_ref[:, height : height + 8, :] = jnp.zeros((3, 8, width), jnp.float32)
@@ -280,7 +286,7 @@
 
     def image_block(block, sums):
         along, across = sums
-        start = pl.multiple_of(block * count, count)
+        start = block * count
         rows = pl.ds(start, count)
         low = plane_modes(z_ref, (layers - 1,), start, count)
         high = plane_modes(top_ref, (), start, count)
@@ -297,10 +303,10 @@
             v_ref[1, comp, rows, :] = inv_top_ref[rows, :] * nodal(lower, comp, carry.at[1], start, count)
         return along, across
 
-    along, across = lax.fori_loop(0, height // count, image_block, (zero, zero))
+    along, across = unrolled(0, height // count, image_block, (zero, zero))
 
     def energy_block(block, energy):
-        start = pl.multiple_of(block * count, count)
+        start = block * count
         low = None
         for plane in range(layers + 1):
             if plane < layers - 1:
@@ -313,7 +319,7 @@
             low = high
         return energy
 
-    energy = lax.fori_loop(0, height // count, energy_block, zero)
+    energy = unrolled(0, height // count, energy_block, zero)
     sums = low_sums_ref[...] + add_up((zero[:8], along, across, energy))
     sums = jnp.sum(sums, axis=1, keepdims=True)
     lane = lax.broadcasted_iota(jnp.int32, (8, width), 1)

time: 39.5 us -> 39.2 us (level)
  Pallas kernels: 8.75 us -> 8.25 us
  transfers between devices with their start and end apart: 7 -> 7, of which waited for: 5 -> 5; matrix products, arithmetic and copies ran while one was open for 0% -> 0% of each run, Pallas kernels for 17% -> 16%
where the time goes in v7:
time: 39.2 us; the launch traced here: 39 us
  waiting for transfers between devices  15.9 us (41%)
  starting transfers between devices  14 us (36%)
  Pallas kernels  8.25 us (21%)
  between operations  0.75 us (2%)
    ppermute x6, waiting for transfers between devices, permute(): return lax.ppermute(shard, axis, pairs)  10.3 us
    ppermute x6, starting transfers between devices, permute(): return lax.ppermute(shard, axis, pairs)  9.12 us
    all_to_all x1, waiting for transfers between devices, shards(): sums = lax.all_to_all(sums, ('space', 'load'), 0, 0, tiled=True)  5.6 us
    all_to_all x1, starting transfers between devices, shards(): sums = lax.all_to_all(sums, ('space', 'load'), 0, 0, tiled=True)  4.89 us
    pallas_call x1, Pallas kernels, shards(): pl.pallas_call(above_kernel, out_shape=(f32(3, pad, width), f32(2, 3, pad...  2.63 us
    pallas_call x1, Pallas kernels, shards(): pl.pallas_call(pack_kernel, out_shape=[f32(3 * height + share, width), f3...  1.32 us
    pallas_call x1, Pallas kernels, shards(): pl.pallas_call(below_kernel, out_shape=(f32(layers, 3, pad, width), f32(l...  1.23 us
    pallas_call x1, Pallas kernels, shards(): pl.pallas_call(term_kernel, out_shape=f32(loads, 2, layers, share, width)...  1.11 us
  transfers between devices with their start and end apart: 7, of which 5 were waited for; matrix products, arithmetic and copies ran while one was open for 0% of the time, Pallas kernels for 16%

profile of v7, /device:TPU:0, one launch (start us, length us, event | category | flops | bytes accessed | tf_op | source)
XLA Modules:
  0.0 39.0 jit_solution(13774686438514004452)
XLA Ops:
  0.6 1.3 %pack.1 = (f32[448,128]{1,0:T(8,128)S(1)}, f32[128,128]{1,0:T(8,128)S(1)}, f32[6,128,128]{2,1,0:T(8,128)S(1)}, f32[3,128,128]{2,1,0:T(8,128)S(1)}, f32[3,2,128,1...) custom-call(s32[1]{0:T(128)} %bitcast.load_ref, ...), custom_call_target="tpu_custom_call" | custom-call | tf_op jit(solution)/shard_map/pack/pallas_call | solution.py:478
  2.0 4.9 %collective-permute-start.1 = (f32[448,128]{1,0:T(8,128)S(1)}, f32[448,128]{1,0:T(8,128)S(1)}, u32[]{:S(2)}, u32[]{:S(2)}) collective-permute-start(f32[448,128]{1,0:T(8,128)S(1)} %get-tuple-element.25), channel_id=1, source_target_pairs={{0,2},{2,4},{4,6},{6,8},{8,10},{10,12},{12,14},{14,16},{16,18},{18... | collective-permute-start | bytes 688136 | tf_op jit(solution)/shard_map/ppermute | solution.py:30
  6.8 1.3 %collective-permute-start.2 = (f32[128,128]{1,0:T(8,128)S(1)}, f32[128,128]{1,0:T(8,128)S(1)}, u32[]{:S(2)}, u32[]{:S(2)}) collective-permute-start(f32[128,128]{1,0:T(8,128)S(1)} %get-tuple-element.29), channel_id=1, source_target_pairs={{2,0},{4,2},{6,4},{8,6},{10,8},{12,10},{14,12},{16,14},{18,16},{20... | collective-permute-start | bytes 196616 | tf_op jit(solution)/shard_map/ppermute | solution.py:30
  8.1 1.3 %collective-permute-start = (f32[6,128,128]{2,1,0:T(8,128)S(1)}, f32[6,128,128]{2,1,0:T(8,128)S(1)}, u32[]{:S(2)}, u32[]{:S(2)}) collective-permute-start(f32[6,128,128]{2,1,0:T(8,128)S(1)} %get-tuple-element.24), channel_id=1, source_target_pairs={{2,0},{4,2},{6,4},{8,6},{10,8},{12,10},{14,12},{16,14},{18,16},{20... | collective-permute-start | bytes 1179656 | tf_op jit(solution)/shard_map/ppermute | solution.py:30
  9.4 2.2 %collective-permute-done.1.up_ref = f32[448,128]{1,0:T(8,128)S(1)} collective-permute-done((f32[448,128]{1,0:T(8,128)S(1)}, f32[448,128]{1,0:T(8,128)S(1)}, u32[]{:S(2)}, u32[]{:S(2)}) %collective-permute-start.1) | collective-permute-done | bytes 229408 | tf_op jit(solution)/shard_map/ppermute | solution.py:30
  11.7 4.5 %collective-permute-done.2 = f32[128,128]{1,0:T(8,128)S(1)} collective-permute-done((f32[128,128]{1,0:T(8,128)S(1)}, f32[128,128]{1,0:T(8,128)S(1)}, u32[]{:S(2)}, u32[]{:S(2)}) %collective-permute-start.2) | collective-permute-done | bytes 65568 | tf_op jit(solution)/shard_map/ppermute | solution.py:30
  16.2 0.1 collective-permute-start.3
  16.2 1.3 %collective-permute-done.3.refs_1_ = f32[192,128]{1,0:T(8,128)S(1)} collective-permute-done((f32[192,128]{1,0:T(8,128)S(1)}, f32[192,128]{1,0:T(8,128)S(1)}, u32[]{:S(2)}, u32[]{:S(2)}) %collective-permute-start.3) | collective-permute-done | bytes 98336 | tf_op jit(solution)/shard_map/ppermute | solution.py:30
  17.5 0.0 copy-start
  17.5 1.2 %below.1 = (f32[2,3,136,128]{3,2,1,0:T(8,128)S(1)}, f32[1,3,136,128]{3,2,1,0:T(8,128)S(1)}, f32[3,128,128]{2,1,0:T(8,128)S(1)}, f32[2,128,128]{2,1,0:T(8,128)S(1)}, f32[8,128]{1,0:T(8,128)S(1)}) custom-call(s32[1]{0:T(128)} %bitcast.load_ref, f32[448,128]{1,0:T(8,128)S(1)} %collective-permute-done.1.up_ref, ...), custom_call_target="tpu_custom_call" | custom-call | flops 1000000000 | bytes 1024 | tf_op jit(solution)/shard_map/below/pallas_call | solution.py:502
  18.8 0.0 copy-done
  18.8 1.0 %early.1 = (f32[2,1,128,128]{3,2,1,0:T(8,128)S(1)}, f32[12,128,128]{2,1,0:T(8,128)S(1)}, f32[128,128]{1,0:T(8,128)S(1)}, f32[128,128]{1,0:T(8,128)S(1)}) custom-call(s32[1]{0:T(128)} %bitcast.load_ref, f32[2,3,136,128]{3,2,1,0:T(8,128)S(1)} %get-tuple-element.30.z_ref, f32[1,3,136,128]{3,2,1,0:T(8,128)S(1)} %get-tuple-element.31.low_v_ref, ...), custom_call_target="tpu_custom_call" | custom-call | tf_op jit(solution)/shard_map/early/pallas_call | solution.py:522
  19.8 1.3 %collective-permute-start.4 = (f32[3,128,128]{2,1,0:T(8,128)S(1)}, f32[3,128,128]{2,1,0:T(8,128)S(1)}, u32[]{:S(2)}, u32[]{:S(2)}) collective-permute-start(f32[3,128,128]{2,1,0:T(8,128)S(1)} %get-tuple-element.45), channel_id=1, source_target_pairs={{2,0},{4,2},{6,4},{8,6},{10,8},{12,10},{14,12},{16,14},{18,16},{20... | collective-permute-start | bytes 589832 | tf_op jit(solution)/shard_map/ppermute | solution.py:30
  21.1 2.3 %collective-permute-done.down_ref = f32[6,128,128]{2,1,0:T(8,128)S(1)} collective-permute-done((f32[6,128,128]{2,1,0:T(8,128)S(1)}, f32[6,128,128]{2,1,0:T(8,128)S(1)}, u32[]{:S(2)}, u32[]{:S(2)}) %collective-permute-start) | collective-permute-done | bytes 393248 | tf_op jit(solution)/shard_map/ppermute | solution.py:30
  23.4 2.6 %above.1 = (f32[3,136,128]{2,1,0:T(8,128)S(1)}, f32[2,3,136,128]{3,2,1,0:T(8,128)S(1)}, f32[32,128]{1,0:T(8,128)}) custom-call(f32[6,128,128]{2,1,0:T(8,128)S(1)} %collective-permute-done.down_ref, f32[2,3,136,128]{3,2,1,0:T(8,128)S(1)} %get-tuple-element.30.z_ref, f32[1,3,136,128]{3,2,1,0:T(8,128)S(1)} %get-tuple-element.31.low_v_ref, ...), custom_call_target="tpu_custom_call" | custom-call | tf_op jit(solution)/shard_map/above/pallas_call | solution.py:534
  26.1 4.9 %all-to-all-start = ((f32[32,1,128]{2,1,0:T(1,128)}), f32[32,1,128]{2,1,0:T(1,128)S(1)}, u32[]{:S(2)}, u32[]{:S(2)}) async-start(f32[32,1,128]{2,1,0:T(1,128)} %bitcast.2), calls=%async_computation | async-start | bytes 32768 | tf_op jit(solution)/shard_map/all_to_all | solution.py:546
  31.0 0.0 collective-permute-done.4.above_ref
  31.0 1.1 %term.1 = f32[2,2,2,64,128]{4,3,2,1,0:T(8,128)S(1)} custom-call(s32[1]{0:T(128)} %bitcast.load_ref, f32[2,1,128,128]{3,2,1,0:T(8,128)S(1)} %get-tuple-element.42.early_ref, f32[12,128,128]{2,1,0:T(8,128)S(1)} %get-tuple-element.43.upper_ref, f32[2,3,136,128]{3,2,1,0:T(8,128)S(1)} %get-tuple-element.30.z_ref, f32[3,136,128]{2,1,0:T(8,128)S(1)} %get-tuple-element.44.top_ref, ...), custom_call_target="tpu_custom_call" | custom-call | tf_op jit(solution)/shard_map/term/pallas_call | solution.py:548
  32.1 0.3 collective-permute-start.5
  32.4 5.6 %all-to-all-done = f32[32,1,128]{2,1,0:T(1,128)S(1)} async-done(((f32[32,1,128]{2,1,0:T(1,128)}), f32[32,1,128]{2,1,0:T(1,128)S(1)}, u32[]{:S(2)}, u32[]{:S(2)}) %all-to-all-start) | async-done | bytes 16416 | tf_op jit(solution)/shard_map/all_to_all | solution.py:546
  38.0 0.1 weight.1.weight_ref
  38.1 0.0 collective-permute-done.5.refs_1_
  38.2 0.8 %finish.1 = (f32[1,3,2,128,128]{4,3,2,1,0:T(8,128)}, f32[2,64,128]{2,1,0:T(8,128)}) custom-call(f32[4,8,128]{2,1,0:T(8,128)S(1)} %weight.1.weight_ref, f32[2,3,136,128]{3,2,1,0:T(8,128)S(1)} %get-tuple-element.30.z_ref, f32[1,3,136,128]{3,2,1,0:T(8,128)S(1)} %get-tuple-element.31.low_v_ref, f32[2,3,136,128]{3,2,1,0:T(8,128)S(1)} %get-tuple-element.39.v_ref, ...), custom_call_target="tpu_custom_call" | custom-call | tf_op jit(solution)/shard_map/finish/pallas_call | solution.py:567
  (3 shorter events, 0.0 us)
Async XLA Ops:
  2.0 9.7 %collective-permute-start.1 = (f32[448,128]{1,0:T(8,128)S(1)}, f32[448,128]{1,0:T(8,128)S(1)}, u32[]{:S(2)}, u32[]{:S(2)}) collective-permute-start(f32[448,128]{1,0:T(8,128)S(1)} %get-tuple-element.25), channel_id=1, source_target_pairs={{0,2},{2,4},{4,6},{6,8},{8,10},{10,12},{12,14},{14,16},{16,18},{18... | collective-permute-start | bytes 688136 | tf_op jit(solution)/shard_map/ppermute | solution.py:30
  6.8 9.3 %collective-permute-start.2 = (f32[128,128]{1,0:T(8,128)S(1)}, f32[128,128]{1,0:T(8,128)S(1)}, u32[]{:S(2)}, u32[]{:S(2)}) collective-permute-start(f32[128,128]{1,0:T(8,128)S(1)} %get-tuple-element.29), channel_id=1, source_target_pairs={{2,0},{4,2},{6,4},{8,6},{10,8},{12,10},{14,12},{16,14},{18,16},{20... | collective-permute-start | bytes 196616 | tf_op jit(solution)/shard_map/ppermute | solution.py:30
  8.1 15.3 %collective-permute-start = (f32[6,128,128]{2,1,0:T(8,128)S(1)}, f32[6,128,128]{2,1,0:T(8,128)S(1)}, u32[]{:S(2)}, u32[]{:S(2)}) collective-permute-start(f32[6,128,128]{2,1,0:T(8,128)S(1)} %get-tuple-element.24), channel_id=1, source_target_pairs={{2,0},{4,2},{6,4},{8,6},{10,8},{12,10},{14,12},{16,14},{18,16},{20... | collective-permute-start | bytes 1179656 | tf_op jit(solution)/shard_map/ppermute | solution.py:30
  16.2 1.4 %collective-permute-start.3 = (f32[192,128]{1,0:T(8,128)S(1)}, f32[192,128]{1,0:T(8,128)S(1)}, u32[]{:S(2)}, u32[]{:S(2)}) collective-permute-start(f32[192,128]{1,0:T(8,128)S(1)} %pad_maximum_fusion.refs_0_), channel_id=1, source_target_pairs={{0,1},{1,0},{2,3},{3,2},{4,5},{5,4},{6,7},{7,6},{8,9},{9,8},{10,11... | collective-permute-start | bytes 294920 | tf_op jit(solution)/shard_map/ppermute | solution.py:30
  17.5 1.2 %copy-start = (f32[1,3,2,128,128]{4,3,2,1,0:T(8,128)S(1)}, f32[1,3,2,128,128]{4,3,2,1,0:T(8,128)}, u32[]{:S(2)}) copy-start(f32[1,3,2,128,128]{4,3,2,1,0:T(8,128)} %disp_ref.3) | copy-start | bytes 1179652
  19.8 11.1 %collective-permute-start.4 = (f32[3,128,128]{2,1,0:T(8,128)S(1)}, f32[3,128,128]{2,1,0:T(8,128)S(1)}, u32[]{:S(2)}, u32[]{:S(2)}) collective-permute-start(f32[3,128,128]{2,1,0:T(8,128)S(1)} %get-tuple-element.45), channel_id=1, source_target_pairs={{2,0},{4,2},{6,4},{8,6},{10,8},{12,10},{14,12},{16,14},{18,16},{20... | collective-permute-start | bytes 589832 | tf_op jit(solution)/shard_map/ppermute | solution.py:30
  26.1 12.0 %all-to-all-start = ((f32[32,1,128]{2,1,0:T(1,128)}), f32[32,1,128]{2,1,0:T(1,128)S(1)}, u32[]{:S(2)}, u32[]{:S(2)}) async-start(f32[32,1,128]{2,1,0:T(1,128)} %bitcast.2), calls=%async_computation | async-start | bytes 32768 | tf_op jit(solution)/shard_map/all_to_all | solution.py:546
  32.1 6.0 %collective-permute-start.5 = (f32[2,2,64,128]{3,2,1,0:T(8,128)S(1)}, f32[2,2,64,128]{3,2,1,0:T(8,128)S(1)}, u32[]{:S(2)}, u32[]{:S(2)}) collective-permute-start(f32[2,2,64,128]{3,2,1,0:T(8,128)S(1)} %get-tuple-element.46), channel_id=1, source_target_pairs={{0,1},{1,0},{2,3},{3,2},{4,5},{5,4},{6,7},{7,6},{8,9},{9,8},{10,11... | collective-permute-start | bytes 393224 | tf_op jit(solution)/shard_map/ppermute | solution.py:30
